TPU v7x, 32 devices: a whole 2x2x4 slice. The times are simulated.
32 devices in a mesh: group: 4 (over x, core), frame: 2 (over y), tensor: 4 (over z).
Axes of the slice: x: 2, y: 2, z: 4, core: 2. Of those that a mesh axis runs over, the one named last changes fastest.
Arguments:
- latent: bfloat16 [4, 4, 256, 1152], P('group', 'frame', 'tensor'), may hold values from -6 to 6
- captions: bfloat16 [4, 2, 120, 4096], P('group'), may hold values from -6 to 6
- bucket: int32 [4], P('group'), may hold values from 0 to 7
- clip_ids: int32 [4, 4], P('group'), may hold values from 0 to 1, as said below
- window_mask: int32 [4, 4, 4], P('group', 'frame'), may hold values 0 or 1
- text_counts: int32 [4, 2], P('group'), may hold values from 1 to 120, as said below
- time_table: bfloat16 [8, 1152], P(None, 'tensor'), may hold values from -6 to 6
- ada_weight: bfloat16 [1152, 9, 1152], P('tensor'), may hold values from -0.1875 to 0.1875
- spatial_inproj: bfloat16 [1152, 3, 1152], P(None, None, 'tensor'), may hold values from -0.1875 to 0.1875
- spatial_outproj: bfloat16 [1152, 1152], P('tensor'), may hold values from -1.5 to 1.5
- temporal_inproj: bfloat16 [1152, 3, 1152], P(None, None, 'tensor'), may hold values from -0.1875 to 0.1875
- temporal_outproj: bfloat16 [1152, 1152], P('tensor'), may hold values from -0.25 to 0.25
- caption_proj: bfloat16 [4096, 1152], P(None, 'tensor'), may hold values from -0.09375 to 0.09375
- cross_gain: bfloat16 [1152], replicated, may hold values from 0.5 to 1.5
- cross_query: bfloat16 [1152, 1152], P(None, 'tensor'), may hold values from -0.1875 to 0.1875
- cross_keyval: bfloat16 [1152, 2, 1152], P(None, None, 'tensor'), may hold values from -0.1875 to 0.1875
- cross_outproj: bfloat16 [1152, 1152], P('tensor'), may hold values from -1 to 1
- mlp_up: bfloat16 [1152, 4608], P(None, 'tensor'), may hold values from -0.1875 to 0.1875
- mlp_down: bfloat16 [4608, 1152], P('tensor'), may hold values from -0.09375 to 0.09375
- cotangent: bfloat16 [4, 4, 256, 1152], P('group', 'frame', 'tensor'), may hold values from -6 to 6
Outputs:
- output: bfloat16 [4, 4, 256, 1152], P('group', 'frame', 'tensor')
- grad_latent: bfloat16 [4, 4, 256, 1152], P('group', 'frame', 'tensor')
- grad_time_table: float32 [8, 1152], P(None, 'tensor')
- grad_ada_weight: float32 [1152, 9, 1152], P('tensor', None, ('group', 'frame'))
- grad_spatial_inproj: float32 [1152, 3, 1152], P(('group', 'frame'), None, 'tensor')
- grad_spatial_outproj: float32 [1152, 1152], P('tensor', ('group', 'frame'))
- grad_temporal_inproj: float32 [1152, 3, 1152], P(('group', 'frame'), None, 'tensor')
- grad_temporal_outproj: float32 [1152, 1152], P('tensor', ('group', 'frame'))
- grad_caption_proj: float32 [4096, 1152], P(('group', 'frame'), 'tensor')
- grad_cross_gain: float32 [1152], replicated
- grad_cross_query: float32 [1152, 1152], P(('group', 'frame'), 'tensor')
- grad_cross_keyval: float32 [1152, 2, 1152], P(('group', 'frame'), None, 'tensor')
- grad_cross_outproj: float32 [1152, 1152], P('tensor', ('group', 'frame'))
- grad_mlp_up: float32 [1152, 4608], P(('group', 'frame'), 'tensor')
- grad_mlp_down: float32 [4608, 1152], P('tensor', ('group', 'frame'))
Inputs may be any that keep to these rules, and one draw needn't show every extreme that they name: `clip_ids`: along each group's frames the clip numbers start at 0 and rise by one at each clip boundary; clips hold 8 consecutive frames except the first and the last, which may be shorter; in one group all frames form a single clip. `text_counts`: the first caption of every group has all 120 tokens valid.
All inputs are finite; a program needn't handle non-finite values. No bound on the sum of `window_mask` on one device may be relied on, other than what follows from the above.
Results may differ from a plain program's by a relative error of at most 0.03.
Values may be sent and summed in bfloat16 or wider, within the bound.
A program may use at most 256 MiB of HBM per device.

v0:
```python
import functools

import jax
import jax.numpy as jnp
from jax import lax
from jax.experimental import pallas as pl
from jax.experimental.pallas import tpu as pltpu
from jax.sharding import PartitionSpec as P

HD = 72
WIN = 4
EPSILON = 1e-06
HIGHEST = lax.Precision.HIGHEST
NEGATIVE = -1e30
WIDE = jnp.float32
NARROW = jnp.bfloat16
GROUP, FRAME, LINE = "group", "frame", "tensor"
BOTH = (GROUP, FRAME)
MESH = pl.DeviceIdType.MESH
CHUNKS = 16
LAG = 2
VMEM_LIMIT = 48 * 2**20


def swish_act(values):
    return values / (1.0 + jnp.exp(-values))


def gelu_tanh(values):
    return (
        0.5
        * values
        * (1.0 + jnp.tanh(0.7978845608028654 * (values + 0.044715 * values * values * values)))
    )


def dot(first, second, contract_first, contract_second):
    return lax.dot_general(
        first, second, (((contract_first,), (contract_second,)), ((), ())), preferred_element_type=WIDE
    )


def split_heads(values):
    return values.reshape(values.shape[:-1] + (values.shape[-1] // HD, HD))


def split_pair(values):
    high_part = values.astype(NARROW)
    rest_part = (values - high_part.astype(WIDE)).astype(NARROW)
    return (high_part, rest_part)


def norm_parts(values):
    centred = values - jnp.mean(values, axis=-1, keepdims=True)
    spread = lax.rsqrt(jnp.mean(centred * centred, axis=-1, keepdims=True) + EPSILON)
    return centred * spread, spread


def remote(source, target, send_sem, recv_sem, where):
    return pltpu.make_async_remote_copy(
        src_ref=source,
        dst_ref=target,
        send_sem=send_sem,
        recv_sem=recv_sem,
        device_id=where,
        device_id_type=MESH,
    )


def greet_line(place, count):
    barrier = pltpu.get_barrier_semaphore()

    @pl.when(place > 0)
    def _():
        pl.semaphore_signal(barrier, inc=1, device_id={LINE: place - 1}, device_id_type=MESH)

    @pl.when(place < count - 1)
    def _():
        pl.semaphore_signal(barrier, inc=1, device_id={LINE: place + 1}, device_id_type=MESH)

    pl.semaphore_wait(
        barrier, (place > 0).astype(jnp.int32) + (place < count - 1).astype(jnp.int32)
    )


def line_sum(count, place, part_ref, land, cross, stage, total, sems, consume):
    in_send, land_recv, cross_recv, out_send, out_recv = sems
    depth = part_ref.shape[0] // CHUNKS
    half = count // 2
    left = place < half
    level = jnp.where(left, place, count - 1 - place)
    inner = jnp.where(left, place + 1, place - 1)
    outer = jnp.where(left, place - 1, place + 1)
    is_end, is_middle = level == 0, level == half - 1

    def rows_of(chunk):
        return pl.ds(pl.multiple_of(chunk * depth, depth), depth)

    def inward(chunk):
        rows = rows_of(chunk)
        return remote(stage.at[rows], land.at[rows], in_send.at[chunk], land_recv.at[chunk], {LINE: inner})

    def across(chunk):
        rows = rows_of(chunk)
        return remote(stage.at[rows], cross.at[rows], in_send.at[chunk], cross_recv.at[chunk], {LINE: inner})

    def outward(chunk):
        rows = rows_of(chunk)
        return remote(total.at[rows], total.at[rows], out_send.at[chunk], out_recv.at[chunk], {LINE: outer})

    def send_in(chunk):
        @pl.when(is_middle)
        def _():
            across(chunk).start()

        @pl.when(jnp.logical_not(is_middle))
        def _():
            inward(chunk).start()

    def gather_in(chunk):
        rows = rows_of(chunk)
        inward(chunk).wait_recv()
        stage[rows] = (part_ref[rows].astype(WIDE) + land[rows].astype(WIDE)).astype(NARROW)
        send_in(chunk)

    def finish(chunk):
        rows = rows_of(chunk)

        @pl.when(is_middle)
        def _():
            across(chunk).wait_recv()
            total[rows] = (stage[rows].astype(WIDE) + cross[rows].astype(WIDE)).astype(NARROW)

        @pl.when(jnp.logical_not(is_middle))
        def _():
            outward(chunk).wait_recv()

        @pl.when(jnp.logical_not(is_end))
        def _():
            outward(chunk).start()

        consume(rows)

    def begin(chunk, carry):
        rows = rows_of(chunk)
        stage[rows] = part_ref[rows]
        send_in(chunk)
        return carry

    def step(number, carry):
        @pl.when(jnp.logical_not(is_end) & (number < CHUNKS))
        def _():
            gather_in(number)

        @pl.when(number >= LAG)
        def _():
            finish(number - LAG)

        return carry

    @pl.when(is_end)
    def _():
        lax.fori_loop(0, CHUNKS, begin, 0)

    lax.fori_loop(0, CHUNKS + LAG, step, 0)

    def settle(chunk, carry):
        @pl.when(is_middle)
        def _():
            across(chunk).wait_send()

        @pl.when(jnp.logical_not(is_middle))
        def _():
            inward(chunk).wait_send()

        @pl.when(jnp.logical_not(is_end))
        def _():
            outward(chunk).wait_send()

        return carry

    lax.fori_loop(0, CHUNKS, settle, 0)


def forward_kernel(
    count, part_ref, base_ref, rows_ref, out_ref, next_ref, normed_ref, land, cross, stage, *sems
):
    place = lax.axis_index(LINE)
    greet_line(place, count)
    gate, gain, shift = (rows_ref[i : i + 1] for i in range(3))

    def consume(rows):
        moved = base_ref[rows] + gate * out_ref[rows].astype(WIDE)
        next_ref[rows] = moved
        normed_ref[rows] = (norm_parts(moved)[0] * gain + shift).astype(NARROW)

    line_sum(count, place, part_ref, land, cross, stage, out_ref, sems, consume)


def backward_kernel(
    count, part_ref, base_ref, grad_ref, below_ref, rows_ref,
    moved_ref, low_ref, sums_ref, total, land, cross, stage, tally, *sems
):
    place = lax.axis_index(LINE)
    greet_line(place, count)
    gain, gate = (rows_ref[i : i + 1] for i in range(2))
    tally[...] = jnp.zeros_like(tally)

    def consume(rows):
        grads = total[rows].astype(WIDE)
        normal, spread = norm_parts(base_ref[rows])
        scaled = grads * gain
        moved = grad_ref[rows] + spread * (
            scaled
            - jnp.mean(scaled, axis=-1, keepdims=True)
            - normal * jnp.mean(scaled * normal, axis=-1, keepdims=True)
        )
        moved_ref[rows] = moved
        low_ref[rows] = (gate * moved).astype(NARROW)
        for i, terms in enumerate((grads, grads * normal, moved * below_ref[rows].astype(WIDE))):
            tally[i] += jnp.sum(terms.reshape(-1, 8, terms.shape[-1]), axis=0)

    line_sum(count, place, part_ref, land, cross, stage, total, sems, consume)
    sums_ref[...] = jnp.zeros_like(sums_ref)
    for i in range(3):
        sums_ref[i : i + 1] = jnp.sum(tally[i], axis=0, keepdims=True)


def vmem(count):
    return [pl.BlockSpec(memory_space=pltpu.VMEM)] * count


def line_sems():
    return [pltpu.SemaphoreType.DMA((CHUNKS,))] * 5


def call_forward(count, part, base, rows):
    shape = part.shape
    return pl.pallas_call(
        functools.partial(forward_kernel, count),
        out_shape=(
            jax.ShapeDtypeStruct(shape, NARROW),
            jax.ShapeDtypeStruct(shape, WIDE),
            jax.ShapeDtypeStruct(shape, NARROW),
        ),
        in_specs=vmem(3),
        out_specs=tuple(vmem(3)),
        scratch_shapes=[pltpu.VMEM(shape, NARROW)] * 3 + line_sems(),
        compiler_params=pltpu.CompilerParams(
            collective_id=1, has_side_effects=True, vmem_limit_bytes=VMEM_LIMIT
        ),
        name="forward_sum",
    )(part, base, rows)


def call_backward(count, part, base, grad, below, rows):
    shape = part.shape
    return pl.pallas_call(
        functools.partial(backward_kernel, count),
        out_shape=(
            jax.ShapeDtypeStruct(shape, WIDE),
            jax.ShapeDtypeStruct(shape, NARROW),
            jax.ShapeDtypeStruct((8, shape[1]), WIDE),
        ),
        in_specs=vmem(5),
        out_specs=tuple(vmem(3)),
        scratch_shapes=[pltpu.VMEM(shape, NARROW)] * 4
        + [pltpu.VMEM((3, 8, shape[1]), WIDE)]
        + line_sems(),
        compiler_params=pltpu.CompilerParams(
            collective_id=2, has_side_effects=True, vmem_limit_bytes=VMEM_LIMIT
        ),
        name="backward_sum",
    )(part, base, grad, below, rows)


def opening_kernel(
    count, groups, frames_axis, latent_ref, act_ref, ada_ref, captions_ref,
    base_ref, normed_ref, mods_ref, spread_ref,
    land, ada, mine, others,
    up_send, down_send, land_recv, ada_sem, mods_send, mods_recv, cap_send, cap_recv, cap_local,
):
    place = lax.axis_index(LINE)
    group = lax.axis_index(GROUP)
    here = lax.axis_index(FRAME)
    last = count - 1
    width = spread_ref.shape[2]
    parts = ada_ref.shape[0]
    share = latent_ref.shape[1]

    loads = [pltpu.make_async_copy(ada_ref.at[k], ada.at[k], ada_sem.at[k]) for k in range(parts)]
    for load in loads:
        load.start()

    barrier = pltpu.get_barrier_semaphore()
    for ahead in range(1, count):
        pl.semaphore_signal(
            barrier, inc=1, device_id={LINE: lax.rem(place + ahead, count)}, device_id_type=MESH
        )
    for ahead in range(1, groups):
        pl.semaphore_signal(
            barrier, inc=1, device_id={GROUP: lax.rem(group + ahead, groups)}, device_id_type=MESH
        )
    pl.semaphore_wait(barrier, count - 1 + groups - 1)

    def shift(owner, up):
        to = place + 1 if up else place - 1
        return remote(
            land.at[owner], land.at[owner], (up_send if up else down_send).at[owner], land_recv.at[owner], {LINE: to}
        )

    land[place] = latent_ref[...]

    @pl.when(place < last)
    def _():
        shift(place, True).start()

    @pl.when(place > 0)
    def _():
        shift(place, False).start()

    def caption_block(to):
        if len(captions_ref.shape) == 3:
            return captions_ref.at[to]
        first = pl.multiple_of((to * frames_axis + here) * width, width)
        return captions_ref.at[:, pl.ds(first, width)]

    def caption_copy(ahead):
        to = lax.rem(group + ahead, groups)
        return remote(
            caption_block(to),
            spread_ref.at[group],
            cap_send.at[ahead],
            cap_recv.at[ahead],
            {GROUP: to},
        )

    own_caption = pltpu.make_async_copy(caption_block(group), spread_ref.at[group], cap_local)
    own_caption.start()
    for ahead in range(1, groups):
        caption_copy(ahead).start()

    def arrive(distance):
        @pl.when(place >= distance)
        def _():
            shift(place - distance, True).wait_recv()

            @pl.when(place < last)
            def _():
                shift(place - distance, True).start()

        @pl.when(place + distance <= last)
        def _():
            shift(place + distance, False).wait_recv()

            @pl.when(place > 0)
            def _():
                shift(place + distance, False).start()

    def weigh(k):
        loads[k].wait()
        product = dot(act_ref[...], ada[k], 1, 0)
        mine[k : k + 1] = product[0:1]

    def mods_copy(ahead):
        return remote(
            mine, others.at[place], mods_send.at[ahead], mods_recv.at[ahead], {LINE: lax.rem(place + ahead, count)}
        )

    mine[...] = jnp.zeros_like(mine)
    cut = parts // 2 + 1
    for k in range(cut):
        weigh(k)
    arrive(1)
    for k in range(cut, parts):
        weigh(k)
    for ahead in range(1, count):
        mods_copy(ahead).start()
    others[place] = mine[...]
    for distance in range(2, count - 1):
        arrive(distance)
    for ahead in range(1, count):
        mods_copy(ahead).wait_recv()
    mods = others[0]
    for i in range(1, count):
        mods = mods + others[i]
    mods_ref[...] = mods
    gain = 1.0 + mods[1:2]
    shift_row = mods[0:1]

    def norm_owner(owner):
        for f in range(latent_ref.shape[0]):
            values = land[owner, f].astype(WIDE)
            rows = pl.ds(pl.multiple_of(owner * share, share), share)
            base_ref[f, rows] = values
            normed_ref[f, rows] = (norm_parts(values)[0] * gain + shift_row).astype(NARROW)

    def near(distance):
        @pl.when(place >= distance)
        def _():
            norm_owner(place - distance)

        @pl.when(place + distance <= last)
        def _():
            norm_owner(place + distance)

    norm_owner(place)
    for distance in range(1, count - 1):
        near(distance)
    if count > 2:
        arrive(count - 1)
    near(count - 1)

    for owner in range(count):

        @pl.when((place < last) & (owner <= place))
        def _():
            shift(owner, True).wait_send()

        @pl.when((place > 0) & (owner >= place))
        def _():
            shift(owner, False).wait_send()

    for ahead in range(1, count):
        mods_copy(ahead).wait_send()
    for ahead in range(1, groups):
        caption_copy(ahead).wait_send()
        caption_copy(ahead).wait_recv()
    own_caption.wait()


def call_opening(count, groups, frames_axis, latent, act, ada, captions):
    frames, share, features = latent.shape
    parts = ada.shape[0]
    length, text_width = captions.shape
    width = text_width // (groups * frames_axis)
    if width % 128:
        blocks = captions.reshape(length, groups, frames_axis, width)
        captions = jnp.transpose(
            lax.dynamic_index_in_dim(blocks, lax.axis_index(FRAME), 2, keepdims=False), (1, 0, 2)
        )
    full = (frames, share * count, features)
    dma = pltpu.SemaphoreType.DMA
    anywhere = pl.BlockSpec(memory_space=pl.ANY)
    return pl.pallas_call(
        functools.partial(opening_kernel, count, groups, frames_axis),
        out_shape=(
            jax.ShapeDtypeStruct(full, WIDE),
            jax.ShapeDtypeStruct(full, NARROW),
            jax.ShapeDtypeStruct((16, features), WIDE),
            jax.ShapeDtypeStruct((groups, length, width), NARROW),
        ),
        in_specs=vmem(2) + [anywhere] * 2,
        out_specs=tuple(vmem(3) + [anywhere]),
        scratch_shapes=[
            pltpu.VMEM((count, frames, share, features), NARROW),
            pltpu.VMEM(ada.shape, NARROW),
            pltpu.VMEM((16, features), WIDE),
            pltpu.VMEM((count, 16, features), WIDE),
            dma((count,)),
            dma((count,)),
            dma((count,)),
            dma((parts,)),
            dma((count,)),
            dma((count,)),
            dma((groups,)),
            dma((groups,)),
            dma,
        ],
        compiler_params=pltpu.CompilerParams(
            collective_id=3, has_side_effects=True, vmem_limit_bytes=VMEM_LIMIT
        ),
        name="opening",
    )(latent, act, ada, captions)


def attend_scores(query, keys, key_valid):
    raw_scores = HD ** (-0.5) * jnp.einsum("fphe,fqhe->fhpq", query, keys, preferred_element_type=WIDE)
    if key_valid is None:
        return raw_scores
    return jnp.where(key_valid[:, None, None, :], raw_scores, NEGATIVE)


def attend_forward(query, keys, values, key_valid):
    scores = attend_scores(query, keys, key_valid)
    row_max = jnp.max(scores, axis=-1, keepdims=True)
    shifted = jnp.exp(scores - row_max)
    row_total = jnp.sum(shifted, axis=-1, keepdims=True)
    probs_low = (shifted / row_total).astype(NARROW)
    heads_out = jnp.einsum("fhpq,fqhe->fphe", probs_low, values, preferred_element_type=WIDE)
    return (heads_out.astype(NARROW), row_max + jnp.log(row_total))


def attend_backward(query, keys, values, key_valid, log_total, grad_out):
    probs = jnp.exp(attend_scores(query, keys, key_valid) - log_total)
    grad_probs = jnp.einsum("fphe,fqhe->fhpq", grad_out, values, preferred_element_type=WIDE)
    grad_values = jnp.einsum("fhpq,fphe->fqhe", probs.astype(NARROW), grad_out, preferred_element_type=WIDE)
    grad_scores = probs * (grad_probs - jnp.sum(grad_probs * probs, axis=-1, keepdims=True))
    grad_scores = grad_scores.astype(NARROW)
    grad_query = HD ** (-0.5) * jnp.einsum("fhpq,fqhe->fphe", grad_scores, keys, preferred_element_type=WIDE)
    grad_keys = HD ** (-0.5) * jnp.einsum("fhpq,fphe->fqhe", grad_scores, query, preferred_element_type=WIDE)
    return (grad_query, grad_keys, grad_values)


def over_heads(first, second):
    return jnp.einsum("fphe,fphe->fhp", first, second, precision=HIGHEST, preferred_element_type=WIDE)


def by_heads(weights, values):
    return jnp.einsum("fhp,fphe->fphe", weights, values, precision=HIGHEST)


def temporal_weights(query, keys, allowed, frames):
    score_list = []
    for offset in range(WIN):
        raw_scores = HD ** (-0.5) * jnp.einsum(
            "fphe,fphe->fhp", query, keys[offset : offset + frames], preferred_element_type=WIDE
        )
        score_list.append(jnp.where(allowed[offset][:, None, None], raw_scores, NEGATIVE))
    scores = jnp.stack(score_list)
    shifted = jnp.exp(scores - jnp.max(scores, axis=0, keepdims=True))
    return shifted / jnp.sum(shifted, axis=0, keepdims=True)


def temporal_mix(probs, values, frames):
    values_wide = values.astype(WIDE)
    mixed = by_heads(probs[0], values_wide[0:frames])
    for offset in range(1, WIN):
        mixed = mixed + by_heads(probs[offset], values_wide[offset : offset + frames])
    return mixed


def temporal_backward(query, keys, values, probs, grad_out, frames):
    query_wide, keys_wide = query.astype(WIDE), keys.astype(WIDE)
    values_wide, grad_wide = values.astype(WIDE), grad_out.astype(WIDE)
    grad_probs = jnp.stack(
        [over_heads(grad_wide, values_wide[offset : offset + frames]) for offset in range(WIN)]
    )
    grad_scores = probs * (grad_probs - jnp.sum(grad_probs * probs, axis=0, keepdims=True))
    grad_query = jnp.zeros(query.shape, WIDE)
    for offset in range(WIN):
        grad_query = grad_query + HD ** (-0.5) * by_heads(
            grad_scores[offset], keys_wide[offset : offset + frames]
        )

    def near_sums(weights, sources):
        found = []
        for cell in range(frames + WIN - 1):
            terms = [
                by_heads(weights[offset][cell - offset : cell - offset + 1], sources[cell - offset : cell - offset + 1])
                for offset in range(WIN)
                if 0 <= cell - offset < frames
            ]
            found.append(sum(terms[1:], terms[0]))
        return found

    grad_keys = near_sums(HD ** (-0.5) * grad_scores, query_wide)
    return (grad_query, grad_keys, near_sums(probs, grad_wide))


def to_next(cells):
    ends = lax.axis_size(FRAME) - 1
    return lax.ppermute(cells, FRAME, [(i, i + 1) for i in range(ends)])


def to_previous(cells):
    ends = lax.axis_size(FRAME) - 1
    return lax.ppermute(cells, FRAME, [(i + 1, i) for i in range(ends)])


def sum_matrix_grads(pieces):
    packed = jnp.concatenate([piece.astype(NARROW) for piece in pieces], axis=1)
    summed = lax.psum_scatter(packed, BOTH, scatter_dimension=0, tiled=True).astype(WIDE)
    found, start = [], 0
    for piece in pieces:
        found.append(summed[:, start : start + piece.shape[1]])
        start += piece.shape[1]
    return found


def per_device(
    latent, captions, bucket, clip_ids, window_mask, text_counts, time_table, ada_weight,
    spatial_inproj, spatial_outproj, temporal_inproj, temporal_outproj, caption_proj, cross_gain,
    cross_query, cross_keyval, cross_outproj, mlp_up, mlp_down, cotangent,
):
    count, groups, frames_axis = (lax.axis_size(axis) for axis in (LINE, GROUP, FRAME))
    place = lax.axis_index(LINE)
    frames, share, features = latent.shape[1:]
    patches = share * count
    tokens = frames * patches
    local = spatial_outproj.shape[0]
    clip_count, text_length, text_width = captions.shape[1:]
    slots = clip_count * text_length

    def flat(values):
        return values.reshape(tokens, -1)

    def grid(values):
        return values.reshape(frames, patches, -1)

    def heads(values):
        return split_heads(grid(values))

    def own(values):
        return lax.dynamic_slice_in_dim(grid(values), place * share, share, axis=1)

    spatial_in, temporal_in, keyval_in = (
        jnp.transpose(w, (1, 2, 0)).reshape(-1, features)
        for w in (spatial_inproj, temporal_inproj, cross_keyval)
    )
    query_in = cross_query.T

    chosen = (jnp.arange(time_table.shape[0]) == bucket[0]).astype(WIDE)
    cond_row = jnp.sum(chosen[:, None] * time_table.astype(WIDE), axis=0)
    act_low = swish_act(cond_row).astype(NARROW)
    caption_here = captions[0].reshape(slots, text_width)
    base_grid, normed_grid, mods, caption_share = call_opening(
        count, groups, frames_axis, latent[0], jnp.broadcast_to(act_low[None], (16, local)),
        jnp.transpose(ada_weight, (1, 0, 2)), caption_here,
    )
    base_zero, spatial_hidden = flat(base_grid), flat(normed_grid)
    cotangent_full = flat(lax.all_gather(cotangent[0], LINE, axis=1, tiled=True))

    text_part = dot(caption_here, caption_proj, 1, 0).astype(NARROW)
    text_rows = lax.all_gather(text_part, LINE, axis=1, tiled=True)

    def rows_of(*rows):
        filled = [jnp.zeros((features,), WIDE)] * (8 - len(rows))
        return jnp.stack(list(rows) + filled)

    spatial_packed = dot(spatial_hidden, spatial_in, 1, 1).astype(NARROW)
    spatial_query, spatial_keys, spatial_values = (
        heads(spatial_packed[:, i * local : (i + 1) * local]) for i in range(3)
    )
    spatial_heads, spatial_logs = attend_forward(spatial_query, spatial_keys, spatial_values, None)
    spatial_flat = flat(spatial_heads)
    spatial_out, base_one, temporal_hidden = call_forward(
        count,
        dot(spatial_flat, spatial_outproj, 1, 0).astype(NARROW),
        base_zero,
        rows_of(mods[2], 1.0 + mods[4], mods[3]),
    )

    temporal_packed = dot(temporal_hidden, temporal_in, 1, 1).astype(NARROW)
    temporal_query = heads(temporal_packed[:, 0:local])
    own_pair = grid(temporal_packed[:, local:])
    near = jnp.concatenate(
        [to_next(own_pair[frames - 2 :]), own_pair, to_previous(own_pair[0:1])], axis=0
    )
    temporal_keys = split_heads(near[:, :, 0:local])
    temporal_values = split_heads(near[:, :, local:])
    first_frame = lax.axis_index(FRAME) * frames
    clip_near = lax.dynamic_slice_in_dim(
        jnp.pad(clip_ids[0], (2, 2), constant_values=-1), first_frame, frames + 4
    )
    own_clip = clip_near[2 : 2 + frames]
    allowed = jnp.stack(
        [
            (clip_near[offset : offset + frames] == own_clip)
            & ((window_mask[0][:, offset] == 1) | (offset == 2))
            for offset in range(WIN)
        ]
    )
    temporal_probs = temporal_weights(temporal_query, temporal_keys, allowed, frames)
    temporal_flat = flat(temporal_mix(temporal_probs, temporal_values, frames).astype(NARROW))
    temporal_out, base_two, cross_hidden = call_forward(
        count,
        dot(temporal_flat, temporal_outproj, 1, 0).astype(NARROW),
        base_one,
        rows_of(mods[5], cross_gain.astype(WIDE), jnp.zeros((features,), WIDE)),
    )

    cross_packed = dot(cross_hidden, query_in, 1, 1).astype(NARROW)
    text_packed = dot(text_rows, keyval_in, 1, 1).astype(NARROW)

    def each_frame(values):
        return jnp.broadcast_to(split_heads(values)[None], (frames, slots, local // HD, HD))

    text_keys, text_values = (each_frame(text_packed[:, i * local : (i + 1) * local]) for i in range(2))
    slot_index = jnp.arange(slots)
    key_valid = (own_clip[:, None] == (slot_index // text_length)[None, :]) & (
        slot_index % text_length < jnp.repeat(text_counts[0], text_length)
    )[None, :]
    cross_queries = heads(cross_packed)
    cross_heads, cross_logs = attend_forward(cross_queries, text_keys, text_values, key_valid)
    cross_flat = flat(cross_heads)
    cross_out, base_three, mlp_hidden = call_forward(
        count,
        dot(cross_flat, cross_outproj, 1, 0).astype(NARROW),
        base_two,
        rows_of(jnp.ones((features,), WIDE), 1.0 + mods[7], mods[6]),
    )

    mlp_inner = dot(mlp_hidden, mlp_up, 1, 0)
    mlp_active, gelu_pull = jax.vjp(gelu_tanh, mlp_inner)
    mlp_low = mlp_active.astype(NARROW)
    grad_four = cotangent_full.astype(WIDE)
    grad_mlp_low = (mods[8] * grad_four).astype(NARROW)
    grad_active = dot(grad_mlp_low, mlp_down, 1, 1)
    grad_inner = gelu_pull(grad_active)[0].astype(NARROW)
    grad_three, grad_cross_low, sums_mlp = call_backward(
        count,
        dot(grad_inner, mlp_up, 1, 1).astype(NARROW),
        base_three,
        grad_four,
        cross_out,
        rows_of(1.0 + mods[7], jnp.ones((features,), WIDE)),
    )
    mlp_out = lax.psum_scatter(
        grid(dot(mlp_low, mlp_down, 1, 0).astype(NARROW)), LINE, scatter_dimension=1, tiled=True
    ).astype(WIDE)
    output = (own(base_three) + mods[8] * mlp_out).astype(NARROW)[None]
    gate_mlp_part = jnp.sum(cotangent[0].astype(WIDE) * mlp_out, axis=(0, 1))
    grad_up, grad_down = sum_matrix_grads(
        [dot(mlp_hidden, grad_inner, 0, 0), dot(grad_mlp_low, mlp_low, 0, 0)]
    )

    grad_cross_heads = dot(grad_cross_low, cross_outproj, 1, 1).astype(NARROW)
    cross_grad_query, text_grad_keys, text_grad_values = attend_backward(
        cross_queries, text_keys, text_values, key_valid, cross_logs, heads(grad_cross_heads)
    )
    grad_cross_packed = flat(cross_grad_query).astype(NARROW)
    grad_two, grad_temporal_low, sums_cross = call_backward(
        count,
        dot(grad_cross_packed, query_in, 1, 0).astype(NARROW),
        base_two,
        grad_three,
        temporal_out,
        rows_of(cross_gain.astype(WIDE), mods[5]),
    )
    grad_text_packed = jnp.concatenate(
        [jnp.sum(part, axis=0).reshape(slots, local) for part in (text_grad_keys, text_grad_values)],
        axis=1,
    )
    text_high, text_rest = split_pair(grad_text_packed)
    grad_keyval_part = dot(text_rows, text_high, 0, 0) + dot(text_rows, text_rest, 0, 0)
    text_grad_part = dot(text_high, keyval_in, 1, 0) + dot(text_rest, keyval_in, 1, 0)
    text_grad = lax.psum_scatter(text_grad_part.astype(NARROW), LINE, scatter_dimension=1, tiled=True)
    text_grad_all = lax.all_gather(text_grad, BOTH).reshape(groups, frames_axis, slots, local)
    text_grad_wide = jnp.sum(text_grad_all.astype(WIDE), axis=1).reshape(groups * slots, local)
    text_all_high, text_all_rest = split_pair(text_grad_wide)
    caption_rows = caption_share.reshape(groups * slots, -1)
    grad_caption = dot(caption_rows, text_all_high, 0, 0) + dot(caption_rows, text_all_rest, 0, 0)
    grad_query_cross, grad_outproj_cross, grad_keyval_cross = sum_matrix_grads(
        [
            dot(cross_hidden, grad_cross_packed, 0, 0),
            dot(grad_cross_low, cross_flat, 0, 0),
            grad_keyval_part,
        ]
    )

    grad_temporal_heads = dot(grad_temporal_low, temporal_outproj, 1, 1).astype(NARROW)
    temporal_grad_query, near_grad_keys, near_grad_values = temporal_backward(
        temporal_query, temporal_keys, temporal_values, temporal_probs, heads(grad_temporal_heads), frames
    )

    def joined(first, last):
        return jnp.concatenate(
            [
                jnp.concatenate([part[cell].reshape(1, patches, local) for cell in range(first, last)], axis=0)
                for part in (near_grad_keys, near_grad_values)
            ],
            axis=2,
        )

    from_next = to_previous(joined(0, 2).astype(NARROW)).astype(WIDE)
    from_previous = to_next(joined(frames + 2, frames + 3).astype(NARROW)).astype(WIDE)
    own_grads = joined(2, 2 + frames)
    own_grads = (
        own_grads
        + jnp.pad(from_next, ((frames - 2, 0), (0, 0), (0, 0)))
        + jnp.pad(from_previous, ((0, frames - 1), (0, 0), (0, 0)))
    )
    grad_temporal_packed = jnp.concatenate(
        [flat(temporal_grad_query).astype(NARROW), flat(own_grads).astype(NARROW)], axis=1
    )
    grad_one, grad_spatial_low, sums_temporal = call_backward(
        count,
        dot(grad_temporal_packed, temporal_in, 1, 0).astype(NARROW),
        base_one,
        grad_two,
        spatial_out,
        rows_of(1.0 + mods[4], mods[2]),
    )
    grad_inproj_temporal, grad_outproj_temporal = sum_matrix_grads(
        [dot(temporal_hidden, grad_temporal_packed, 0, 0), dot(grad_temporal_low, temporal_flat, 0, 0)]
    )

    grad_spatial_heads = dot(grad_spatial_low, spatial_outproj, 1, 1).astype(NARROW)
    spatial_grads = attend_backward(
        spatial_query, spatial_keys, spatial_values, None, spatial_logs, heads(grad_spatial_heads)
    )
    grad_spatial_packed = jnp.concatenate([flat(part) for part in spatial_grads], axis=1).astype(NARROW)
    grad_spatial_part = dot(grad_spatial_packed, spatial_in, 1, 0).astype(NARROW)
    grad_spatial_normed = lax.psum_scatter(
        grid(grad_spatial_part), LINE, scatter_dimension=1, tiled=True
    ).astype(WIDE)
    normal, spread = norm_parts(own(base_zero))
    scaled = grad_spatial_normed * (1.0 + mods[1])
    grad_latent = own(grad_one) + spread * (
        scaled
        - jnp.mean(scaled, axis=-1, keepdims=True)
        - normal * jnp.mean(scaled * normal, axis=-1, keepdims=True)
    )
    shift_part = jnp.sum(grad_spatial_normed, axis=(0, 1))
    scale_part = jnp.sum(grad_spatial_normed * normal, axis=(0, 1))
    grad_inproj_spatial, grad_outproj_spatial = sum_matrix_grads(
        [dot(spatial_hidden, grad_spatial_packed, 0, 0), dot(grad_spatial_low, spatial_flat, 0, 0)]
    )

    shift_spatial, scale_spatial, gate_mlp = lax.psum(
        jnp.stack([shift_part, scale_part, gate_mlp_part]), LINE
    )
    side_row = jnp.pad(jnp.concatenate([cond_row, chosen]), (0, features - local - chosen.shape[0]))
    small = jnp.stack(
        [
            shift_spatial, scale_spatial, sums_temporal[2], sums_temporal[0], sums_temporal[1],
            sums_cross[2], sums_mlp[0], sums_mlp[1], gate_mlp, sums_cross[1], side_row,
        ]
    )
    small_all = lax.all_gather(small, BOTH).reshape(groups, frames_axis, 11, features)
    modulation_grad = jnp.sum(small_all[:, :, 0:9], axis=1)
    grad_gain = jnp.sum(small_all[:, :, 9], axis=(0, 1))
    cond_all = small_all[:, 0, 10, 0:local]
    chosen_all = small_all[:, 0, 10, local : local + chosen.shape[0]]
    act_all, swish_pull = jax.vjp(swish_act, cond_all)
    act_all = act_all.astype(NARROW).astype(WIDE)
    column = features // (groups * frames_axis)
    rank = lax.axis_index(BOTH)
    column_grads = lax.dynamic_slice_in_dim(modulation_grad, rank * column, column, axis=2)
    grad_ada = jnp.einsum("gc,gkd->ckd", act_all, column_grads, precision=HIGHEST)
    grad_act = jnp.einsum("ckd,gkd->gc", ada_weight.astype(WIDE), modulation_grad, precision=HIGHEST)
    grad_cond = swish_pull(grad_act)[0]
    grad_table = jnp.einsum("gn,gc->nc", chosen_all, grad_cond, precision=HIGHEST)

    def unpack(values, parts):
        return values.reshape(values.shape[0], parts, -1)

    return (
        output,
        grad_latent.astype(NARROW)[None],
        grad_table,
        grad_ada,
        unpack(grad_inproj_spatial, 3),
        grad_outproj_spatial.T,
        unpack(grad_inproj_temporal, 3),
        grad_outproj_temporal.T,
        grad_caption,
        grad_gain,
        grad_query_cross,
        unpack(grad_keyval_cross, 2),
        grad_outproj_cross.T,
        grad_up,
        grad_down.T,
    )


def solution(mesh):
    tokens = P(GROUP, FRAME, LINE, None)
    packed_in, rows_in, columns_in = P(None, None, LINE), P(LINE, None), P(None, LINE)
    in_specs = (
        tokens, P(GROUP, None, None, None), P(GROUP), P(GROUP, None), P(GROUP, FRAME, None),
        P(GROUP, None), columns_in, P(LINE, None, None), packed_in, rows_in, packed_in, rows_in,
        columns_in, P(), columns_in, packed_in, rows_in, columns_in, rows_in, tokens,
    )
    packed_out, rows_out, columns_out = P(BOTH, None, LINE), P(LINE, BOTH), P(BOTH, LINE)
    out_specs = (
        tokens, tokens, columns_in, P(LINE, None, BOTH), packed_out, rows_out, packed_out, rows_out,
        columns_out, P(), columns_out, packed_out, rows_out, columns_out, rows_out,
    )
    return jax.shard_map(
        per_device, mesh=mesh, in_specs=in_specs, out_specs=out_specs, check_vma=False
    )
```

profile of v0, /device:TPU:0, one launch (start us, length us, event | category | flops | bytes accessed | tf_op | source)
XLA Modules:
  0.0 705.6 jit_solution(14202542420580161344)
XLA Ops:
  12.6 51.0 %opening.1 = (f32[2,256,1152]{2,1,0:T(8,128)}, bf16[2,256,1152]{2,1,0:T(8,128)(2,1)S(1)}, f32[16,1152]{1,0:T(8,128)S(1)}, bf16[4,240,512]{2,1,0:T(8,128)(2,1)S(1)}) custom-call(bf16[2,64,1152]{2,1,0:T(8,128)(2,1)S(1)} %bitcast.408, bf16[16,288]{1,0:T(8,128)(2,1)S(1)} %broadcast_in_dim.98.act_ref, bf16[9,288,1152]{2,1,0:T(8,128)(2,1)} %bitcast.412, ...), custom_call_target="tpu_custom_call" | custom-call | tf_op jit(solution)/shard_map/opening/pallas_call | solution.py:445
  70.9 1.9 convolution_convert_fusion.11.part_ref
  74.1 36.9 %forward_sum.3 = (bf16[512,1152]{1,0:T(8,128)(2,1)S(1)}, f32[512,1152]{1,0:T(8,128)S(1)}, bf16[512,1152]{1,0:T(8,128)(2,1)S(1)}) custom-call(bf16[512,1152]{1,0:T(8,128)(2,1)S(1)} %copy-done.24, f32[512,1152]{1,0:T(8,128)} %bitcast.413, f32[8,1152]{1,0:T(8,128)S(1)} %stack.78.rows_ref), custom_call_target="tpu_custom_call" | custom-call | tf_op jit(solution)/shard_map/forward_sum/pallas_call | solution.py:239
  116.3 6.1 collective-permute-start
  122.4 1.7 fusion.126
  124.5 3.1 convolution_convert_fusion.26
  127.6 16.5 %all_gather.18 = bf16[240,1152]{0,1:T(8,128)(2,1)S(1)} all-gather(bf16[240,288]{0,1:T(8,128)(2,1)S(1)} %convolution_convert_fusion.26), channel_id=1, replica_groups=mesh['group'=4,'frame'=2,'tensor'=4] {'tensor'}, dimensions={1}, use_global_device_ids=true | all-gather | bytes 691200 | tf_op jit(solution)/shard_map/all_gather | solution.py:625
  144.3 2.6 convolution_convert_fusion.18
  150.3 1.7 fusion.129
  153.4 6.4 pad_maximum_fusion.8
  163.4 34.0 %forward_sum.4 = (bf16[512,1152]{1,0:T(8,128)(2,1)S(1)}, f32[512,1152]{1,0:T(8,128)S(1)}, bf16[512,1152]{1,0:T(8,128)(2,1)S(1)}) custom-call(bf16[512,1152]{1,0:T(8,128)(2,1)S(1)} %convolution_convert_fusion.10.part_ref, f32[512,1152]{1,0:T(8,128)} %copy-done.2, f32[8,1152]{1,0:T(8,128)S(1)} %get-tuple-element.222.rows_ref), custom_call_target="tpu_custom_call" | custom-call | tf_op jit(solution)/shard_map/forward_sum/pallas_call | solution.py:239
  206.5 30.9 %forward_sum.5 = (bf16[512,1152]{1,0:T(8,128)(2,1)S(1)}, f32[512,1152]{1,0:T(8,128)S(1)}, bf16[512,1152]{1,0:T(8,128)(2,1)S(1)}) custom-call(bf16[512,1152]{1,0:T(8,128)(2,1)S(1)} %convolution_convert_fusion.9.part_ref, f32[512,1152]{1,0:T(8,128)} %copy-done.3, f32[8,1152]{1,0:T(8,128)S(1)} %stack.87.rows_ref), custom_call_target="tpu_custom_call" | custom-call | tf_op jit(solution)/shard_map/forward_sum/pallas_call | solution.py:239
  243.6 4.1 fusion.132
  247.7 4.3 fusion.5
  252.1 1.9 convolution_convert_fusion.7.part_ref
  254.0 1.7 bitcast_convert_fusion.grad_ref
  255.7 34.9 %backward_sum.3 = (f32[512,1152]{1,0:T(8,128)S(1)}, bf16[512,1152]{1,0:T(8,128)(2,1)S(1)}, f32[8,1152]{1,0:T(8,128)S(1)}) custom-call(bf16[512,1152]{1,0:T(8,128)(2,1)S(1)} %convolution_convert_fusion.7.part_ref, f32[512,1152]{1,0:T(8,128)} %copy-done.6, f32[512,1152]{1,0:T(8,128)} %bitcast_convert_fusion.grad_ref, bf16[512,1152]{1,0:T(8,128)(2,1)S(1)} %copy-done.23, ...), custom_call_target="tpu_custom_call" | custom-call | tf_op jit(solution)/shard_map/backward_sum/pallas_call | solution.py:258
  293.9 2.2 multiply_reduce_fusion.1
  299.6 32.3 %backward_sum.4 = (f32[512,1152]{1,0:T(8,128)S(1)}, bf16[512,1152]{1,0:T(8,128)(2,1)S(1)}, f32[8,1152]{1,0:T(8,128)S(1)}) custom-call(bf16[512,1152]{1,0:T(8,128)(2,1)S(1)} %convolution_convert_fusion.6.part_ref, f32[512,1152]{1,0:T(8,128)} %copy-done.3, f32[512,1152]{1,0:T(8,128)} %copy-done.8, bf16[512,1152]{1,0:T(8,128)(2,1)S(1)} %copy-done.21, ...), custom_call_target="tpu_custom_call" | custom-call | tf_op jit(solution)/shard_map/backward_sum/pallas_call | solution.py:258
  345.1 5.7 convolution_convert_fusion.8
  351.7 6.2 collective-permute-start.3
  359.0 2.7 collective-permute-done.3
  365.2 47.3 %backward_sum.5 = (f32[512,1152]{1,0:T(8,128)S(1)}, bf16[512,1152]{1,0:T(8,128)(2,1)S(1)}, f32[8,1152]{1,0:T(8,128)S(1)}) custom-call(bf16[512,1152]{1,0:T(8,128)(2,1)S(1)} %convolution_convert_fusion.5.part_ref, f32[512,1152]{1,0:T(8,128)} %copy-done.2, f32[512,1152]{1,0:T(8,128)} %copy-done.7, bf16[512,1152]{1,0:T(8,128)(2,1)S(1)} %copy-done.19, ...), custom_call_target="tpu_custom_call" | custom-call | tf_op jit(solution)/shard_map/backward_sum/pallas_call | solution.py:258
  414.8 1.7 reshape_reshape.31
  416.6 2.3 fusion.21
  423.7 2.6 convolution_convert_fusion.4
  431.3 1.7 pad_maximum_fusion.3
  433.0 5.3 copy.327
  442.2 1.7 pad_maximum_fusion.2
  443.9 5.2 copy.325
  453.0 1.7 pad_maximum_fusion.1
  454.7 5.2 copy.323
  461.3 3.2 convolution_convert_fusion.1
  464.5 2.0 convolution_convert_fusion
  466.4 2.8 pad_maximum_fusion
  469.2 8.6 %copy.329 = bf16[1152,2304]{1,0:T(8,128)(2,1)} copy(bf16[1152,2304]{0,1:T(8,128)(2,1)} %pad_maximum_fusion) | data formatting | bytes 10616832
  480.0 2.0 fusion.35
  483.3 17.5 %psum.7 = f32[3,1152]{1,0:T(4,128)S(1)} all-reduce(f32[3,1152]{1,0:T(4,128)S(1)} %pad_maximum_fusion.15), channel_id=1, replica_groups=mesh['group'=4,'frame'=2,'tensor'=4] {'tensor'}, use_global_device_ids=true, to_apply=%region_18.19 | all-reduce | flops 3456 | bytes 27648 | tf_op jit(solution)/shard_map/psum | solution.py:811
  500.9 20.4 %all-gather.3 = f32[8,11,1152]{2,1,0:T(8,128)S(1)} all-gather(f32[1,11,1152]{2,1,0:T(8,128)S(1)} %bitcast.489), channel_id=3, replica_groups=mesh['group'=4,'frame'=2,'tensor'=4] {'group','frame'}, dimensions={0}, use_global_device_ids=true | all-gather | bytes 456192 | tf_op jit(solution)/shard_map/all_gather | solution.py:821
  522.1 7.6 %convolution_bitcast_fusion.2 = f32[4,288]{1,0:T(4,128)S(1)} fusion(f32[4,9,1152]{2,0,1:T(4,128)S(1)} %copy.336, bf16[288,9,1152]{2,0,1:T(8,128)(2,1)} %param.27), kind=kOutput, calls=%fused_computation.87 | convolution fusion | flops 143327232 | bytes 6142464 | tf_op jit(solution)/shard_map/ckd,gkd->gc/dot_general | solution.py:832
  530.5 2.5 fusion.91
  533.0 2.3 fusion.70
  542.9 36.1 %reduce-scatter.24.cloned.1.call-done = bf16[144,1152]{1,0:T(8,128)(2,1)} async-done(((bf16[1152,1152]{1,0:T(8,128)(2,1)}), bf16[144,1152]{1,0:T(8,128)(2,1)}) %reduce-scatter.24.cloned.1.call-update) | async-done | bytes 331792
  581.4 44.9 %reduce-scatter.22.cloned.1.call-done = bf16[144,1152]{1,0:T(8,128)(2,1)} async-done(((bf16[1152,1152]{1,0:T(8,128)(2,1)}), bf16[144,1152]{1,0:T(8,128)(2,1)}) %reduce-scatter.22.cloned.1.call-update) | async-done | bytes 331792
  634.8 52.3 %reduce-scatter.28.cloned.1.call-done = bf16[144,2304]{1,0:T(8,128)(2,1)} async-done(((bf16[1152,2304]{1,0:T(8,128)(2,1)}), bf16[144,2304]{1,0:T(8,128)(2,1)}) %reduce-scatter.28.cloned.1.call-update) | async-done | bytes 663568
  691.2 2.6 copy.250
  693.8 2.4 slice_bitcast_fusion
  696.1 2.4 copy.251
  (459 shorter events, 115.4 us)
Async XLA Ops:
  7.2 240.5 %copy-start = (bf16[1152,1152]{1,0:T(8,128)(2,1)S(1)}, bf16[1152,1152]{1,0:T(8,128)(2,1)}, u32[]{:S(2)}) copy-start(bf16[1152,1152]{1,0:T(8,128)(2,1)} %param.37) | copy-start | bytes 7962628
  7.2 234.9 %all-gather.8.cloned.1.call-start = ((), (), s32[]{:S(2)}) async-start(), calls=%async_computation.10 | async-start | bytes 1474560 | tf_op jit(solution)/shard_map/all_gather | solution.py:622
  7.9 418.5 %reduce-scatter.20.cloned.1.call-start = ((), (), s32[]{:S(2)}) async-start(), calls=%async_computation.9 | async-start | bytes 737280 | tf_op jit(solution)/shard_map/reduce_scatter | solution.py:738
  12.6 51.8 %copy-start.114 = (bf16[1152,3,288]{0,2,1:T(8,128)(2,1)S(1)}, bf16[1152,3,288]{0,2,1:T(8,128)(2,1)}, u32[]{:S(2)}) copy-start(bf16[1152,3,288]{0,2,1:T(8,128)(2,1)} %param.28) | copy-start | bytes 5971972
  74.1 37.0 %copy-start.112 = (bf16[1152,3,288]{0,2,1:T(8,128)(2,1)S(1)}, bf16[1152,3,288]{0,2,1:T(8,128)(2,1)}, u32[]{:S(2)}) copy-start(bf16[1152,3,288]{0,2,1:T(8,128)(2,1)} %param.30) | copy-start | bytes 5971972
  113.3 10.8 %copy-start.124 = (s32[1,2]{1,0:T(1,128)S(1)}, s32[1,2]{1,0:T(1,128)}, u32[]{:S(2)}) copy-start(s32[1,2]{1,0:T(1,128)} %param.25) | copy-start | bytes 28
  113.3 11.0 %copy-start.106 = (s32[1,2,4]{2,1,0:T(2,128)S(1)}, s32[1,2,4]{2,1,0:T(2,128)}, u32[]{:S(2)}) copy-start(s32[1,2,4]{2,1,0:T(2,128)} %param.24) | copy-start | bytes 100
  113.3 11.2 %copy-start.108 = (bf16[1152]{0:T(1024)(128)(2,1)S(1)}, bf16[1152]{0:T(1024)(128)(2,1)}, u32[]{:S(2)}) copy-start(bf16[1152]{0:T(1024)(128)(2,1)} %param.33) | copy-start | bytes 6916
  114.0 37.9 %collective-permute-start.1 = (bf16[1,256,576]{1,2,0:T(8,128)(2,1)}, bf16[1,256,576]{1,2,0:T(8,128)(2,1)}, u32[]{:S(2)}, u32[]{:S(2)}) collective-permute-start(bf16[1,256,576]{1,2,0:T(8,128)(2,1)} %slice_bitcast_fusion.4), channel_id=1, source_target_pairs={{4,0},{5,1},{6,2},{7,3},{12,8},{13,9},{14,10},{15,11},{20,16},{21,... | collective-permute-start | bytes 884744 | tf_op jit(solution)/shard_map/ppermute | solution.py:568
  116.3 37.0 %collective-permute-start = (bf16[2,256,576]{1,0,2:T(2,128)(2,1)}, bf16[2,256,576]{1,0,2:T(2,128)(2,1)}, u32[]{:S(2)}, u32[]{:S(2)}) collective-permute-start(bf16[2,256,576]{1,0,2:T(2,128)(2,1)} %reshape.510), channel_id=1, source_target_pairs={{0,4},{1,5},{2,6},{3,7},{8,12},{9,13},{10,14},{11,15},{16,20},{17,... | collective-permute-start | bytes 1769480 | tf_op jit(solution)/shard_map/ppermute | solution.py:563
  124.5 19.6 %copy-start.125 = (s32[1,4]{1,0:T(1,128)S(1)}, s32[1,4]{1,0:T(1,128)}, u32[]{:S(2)}) copy-start(s32[1,4]{1,0:T(1,128)} %param.23) | copy-start | bytes 52
  144.1 3.5 copy-start.40
  153.3 6.6 copy-start.79
  153.3 7.9 %copy-start.109 = (pred[2]{0:T(512)(128)(4,1)S(1)}, pred[2]{0:T(512)(128)(4,1)}, u32[]{:S(2)}) copy-start(pred[2]{0:T(512)(128)(4,1)} %get-tuple-element.231) | copy-start | bytes 10
  162.5 34.9 %copy-start.75 = (bf16[36,8,2,256]{3,1,2,0:T(8,128)(2,1)}, bf16[36,8,2,256]{3,1,2,0:T(8,128)(2,1)S(1)}, u32[]{:S(2)}) copy-start(bf16[36,8,2,256]{3,1,2,0:T(8,128)(2,1)S(1)} %copy.340) | copy-start | bytes 884740
  163.4 37.5 %copy-start.118 = (bf16[1152,288]{0,1:T(8,128)(2,1)S(1)}, bf16[1152,288]{0,1:T(8,128)(2,1)}, u32[]{:S(2)}) copy-start(bf16[1152,288]{0,1:T(8,128)(2,1)} %param.34) | copy-start | bytes 1990660
  206.5 35.6 %copy-start.93 = (f32[1152]{0:T(1024)S(1)}, f32[1152]{0:T(1024)}, u32[]{:S(2)}) copy-start(f32[1152]{0:T(1024)} %get-tuple-element.147) | copy-start | bytes 13828
  243.6 4.1 copy-start.69
  243.6 4.1 copy-start.32
  255.7 37.5 %copy-start.117 = (bf16[288,1152]{1,0:T(8,128)(2,1)S(1)}, bf16[288,1152]{1,0:T(8,128)(2,1)}, u32[]{:S(2)}) copy-start(bf16[288,1152]{1,0:T(8,128)(2,1)} %param.36) | copy-start | bytes 1990660
  299.6 34.9 %copy-start.121 = (bf16[288,1152]{1,0:T(8,128)(2,1)S(1)}, bf16[288,1152]{1,0:T(8,128)(2,1)}, u32[]{:S(2)}) copy-start(bf16[288,1152]{1,0:T(8,128)(2,1)} %param.31) | copy-start | bytes 1990660
  335.2 3.3 copy-start.85
  335.2 3.3 copy-start.86
  338.5 4.2 copy-start.39
  341.4 20.3 %collective-permute-start.2 = (bf16[2,256,576]{1,2,0:T(8,128)(2,1)}, bf16[2,256,576]{1,2,0:T(8,128)(2,1)}, u32[]{:S(2)}, u32[]{:S(2)}) collective-permute-start(bf16[2,256,576]{1,2,0:T(8,128)(2,1)} %maximum_maximum_fusion), channel_id=1, source_target_pairs={{4,0},{5,1},{6,2},{7,3},{12,8},{13,9},{14,10},{15,11},{20,16},{21,... | collective-permute-start | bytes 1769480 | tf_op jit(solution)/shard_map/ppermute | solution.py:568
  345.0 134.9 %reduce-scatter.16.cloned.1.call-start = ((), (), s32[]{:S(2)}) async-start(), calls=%async_computation.7 | async-start | bytes 1474560 | tf_op jit(solution)/shard_map/reduce_scatter | solution.py:709
  345.1 5.9 copy-start.87
  345.1 12.8 %copy-start.49 = (bf16[2,256,288]{1,0,2:T(2,128)(2,1)S(1)}, bf16[2,256,288]{1,0,2:T(2,128)(2,1)}, u32[]{:S(2)}) copy-start(bf16[2,256,288]{1,0,2:T(2,128)(2,1)} %copy-done.48) | copy-start | bytes 884740
  345.1 12.8 %copy-start.51 = (bf16[2,256,288]{1,0,2:T(2,128)(2,1)S(1)}, bf16[2,256,288]{1,0,2:T(2,128)(2,1)}, u32[]{:S(2)}) copy-start(bf16[2,256,288]{1,0,2:T(2,128)(2,1)} %copy-done.50) | copy-start | bytes 884740
  345.1 12.8 %copy-start.53 = (bf16[2,256,288]{1,0,2:T(2,128)(2,1)S(1)}, bf16[2,256,288]{1,0,2:T(2,128)(2,1)}, u32[]{:S(2)}) copy-start(bf16[2,256,288]{1,0,2:T(2,128)(2,1)} %copy-done.52) | copy-start | bytes 884740
  345.1 12.8 %copy-start.55 = (bf16[2,256,288]{1,0,2:T(2,128)(2,1)S(1)}, bf16[2,256,288]{1,0,2:T(2,128)(2,1)}, u32[]{:S(2)}) copy-start(bf16[2,256,288]{1,0,2:T(2,128)(2,1)} %copy-done.54) | copy-start | bytes 884740
  351.7 10.0 %copy-start.80 = (f32[256,4,72]{0,2,1:T(8,128)S(1)}, f32[256,4,72]{0,2,1:T(8,128)}, u32[]{:S(2)}) copy-start(f32[256,4,72]{0,2,1:T(8,128)} %get-tuple-element.172) | copy-start | bytes 884740
  351.7 10.0 %copy-start.81 = (f32[256,4,72]{0,2,1:T(8,128)S(1)}, f32[256,4,72]{0,2,1:T(8,128)}, u32[]{:S(2)}) copy-start(f32[256,4,72]{0,2,1:T(8,128)} %get-tuple-element.173) | copy-start | bytes 884740
  351.7 10.0 %copy-start.82 = (f32[256,4,72]{0,2,1:T(8,128)S(1)}, f32[256,4,72]{0,2,1:T(8,128)}, u32[]{:S(2)}) copy-start(f32[256,4,72]{0,2,1:T(8,128)} %get-tuple-element.175) | copy-start | bytes 884740
  351.7 10.0 %collective-permute-start.3 = (bf16[1,256,576]{1,2,0:T(8,128)(2,1)}, bf16[1,256,576]{1,2,0:T(8,128)(2,1)}, u32[]{:S(2)}, u32[]{:S(2)}) collective-permute-start(bf16[1,256,576]{1,2,0:T(8,128)(2,1)} %pad_maximum_fusion.9), channel_id=1, source_target_pairs={{0,4},{1,5},{2,6},{3,7},{8,12},{9,13},{10,14},{11,15},{16,20},{17,... | collective-permute-start | bytes 884744 | tf_op jit(solution)/shard_map/ppermute | solution.py:563
  358.9 123.1 %reduce-scatter.18.cloned.1.call-start = ((), (), s32[]{:S(2)}) async-start(), calls=%async_computation.8 | async-start | bytes 1474560 | tf_op jit(solution)/shard_map/reduce_scatter | solution.py:795
  365.2 48.3 %copy-start.123 = (bf16[288,1152]{1,0:T(8,128)(2,1)S(1)}, bf16[288,1152]{1,0:T(8,128)(2,1)}, u32[]{:S(2)}) copy-start(bf16[288,1152]{1,0:T(8,128)(2,1)} %param.29) | copy-start | bytes 1990660
  412.5 6.4 copy-start.26
  426.3 109.0 %all-gather.10.cloned.1.call-start = ((), (), s32[]{:S(2)}) async-start(), calls=%async_computation.11 | async-start | bytes 1327104 | tf_op jit(solution)/shard_map/all_gather | solution.py:739
  426.9 111.9 %reduce-scatter.26.cloned.1.call-start = ((), (), s32[]{:S(2)}) async-start(), calls=%async_computation.14 | async-start | bytes 2985984
  438.4 140.6 %reduce-scatter.24.cloned.1.call-start = ((), (), s32[]{:S(2)}) async-start(), calls=%async_computation.13 | async-start | bytes 2985984
  449.2 177.1 %reduce-scatter.22.cloned.1.call-start = ((), (), s32[]{:S(2)}) async-start(), calls=%async_computation.12 | async-start | bytes 2985984
  460.0 4.4 copy-start.70
  460.0 227.0 %reduce-scatter.28.cloned.1.call-start = ((), (), s32[]{:S(2)}) async-start(), calls=%async_computation.15 | async-start | bytes 5971968
  477.9 4.1 copy-start.92
  529.7 3.3 copy-start.71
  533.0 3.9 copy-start.5
  691.2 7.4 %copy-start.1 = (bf16[1152,1152]{1,0:T(8,128)(2,1)S(1)}, bf16[1152,1152]{1,0:T(8,128)(2,1)}, u32[]{:S(2)}) copy-start(bf16[1152,1152]{1,0:T(8,128)(2,1)} %param.37) | copy-start | bytes 7962628
  (93 other events, 170.0 us)
Sparse Core Ops, SparseCore 0:
  9.6 45.0 all-gather.7
  345.1 23.5 reduce-scatter.19
  371.6 31.7 reduce-scatter.15
  426.5 30.3 reduce-scatter.17
  458.6 22.7 all-gather.9
  484.8 46.5 reduce-scatter.25
  535.2 43.7 reduce-scatter.23
  582.5 43.7 reduce-scatter.21
  630.1 56.8 reduce-scatter.27
where the time goes:
time: 715 us; the launch traced here: 706 us
  Pallas kernels  267 us (37%)
  waiting for transfers between devices  137 us (19%)
  local copies, waits for them, and re-layouts  92.7 us (13%)
  matrix products  75.3 us (11%)
  blocking collectives  54.4 us (8%)
  other arithmetic  46.1 us (6%)
  between operations  17 us (2%)
  starting transfers between devices  15.5 us (2%)
    unnamed x13, waiting for transfers between devices  135 us
    pallas_call x3, Pallas kernels, call_backward(): pl.pallas_call(functools.partial(backward_kernel, count), out_shape=(jax....  115 us
    pallas_call x3, Pallas kernels, call_forward(): pl.pallas_call(functools.partial(forward_kernel, count), out_shape=(jax.S...  102 us
    unnamed x285, local copies, waits for them, and re-layouts  69.7 us
    dot_general x32, matrix products, dot(): lax.dot_general(first, second, (((contract_first,), (contract_second,)),...  54 us
    pallas_call x1, Pallas kernels, call_opening(): pl.pallas_call(functools.partial(opening_kernel, count, groups, frames_ax...  51 us
    all_gather x1, blocking collectives, per_device(): lax.all_gather(small, BOTH).reshape(groups, frames_axis, 11, features)  20.4 us
    psum x1, blocking collectives, per_device(): lax.psum(jnp.stack([shift_part, scale_part, gate_mlp_part]), LINE)  17.5 us
  transfers between devices with their start and end apart: 13, of which 4 were waited for; matrix products, arithmetic and copies ran while one was open for 21% of the time, Pallas kernels for 28%

commit v1 on v0

--- a/solution.py
+++ b/solution.py
@@ -19,6 +19,7 @@
 MESH = pl.DeviceIdType.MESH
 CHUNKS = 16
 LAG = 2
+FIRST_FOLD = 3
 VMEM_LIMIT = 48 * 2**20
 
 
@@ -54,6 +55,14 @@
     centred = values - jnp.mean(values, axis=-1, keepdims=True)
     spread = lax.rsqrt(jnp.mean(centred * centred, axis=-1, keepdims=True) + EPSILON)
     return centred * spread, spread
+
+
+def norm_pull(scaled, normal, spread):
+    return spread * (
+        scaled
+        - jnp.mean(scaled, axis=-1, keepdims=True)
+        - normal * jnp.mean(scaled * normal, axis=-1, keepdims=True)
+    )
 
 
 def remote(source, target, send_sem, recv_sem, where):
@@ -67,8 +76,10 @@
     )
 
 
-def greet_line(place, count):
+def greet_line(place, count, others=()):
     barrier = pltpu.get_barrier_semaphore()
+    for where in others:
+        pl.semaphore_signal(barrier, inc=1, device_id=where, device_id_type=MESH)
 
     @pl.when(place > 0)
     def _():
@@ -79,11 +90,111 @@
         pl.semaphore_signal(barrier, inc=1, device_id={LINE: place + 1}, device_id_type=MESH)
 
     pl.semaphore_wait(
-        barrier, (place > 0).astype(jnp.int32) + (place < count - 1).astype(jnp.int32)
-    )
-
-
-def line_sum(count, place, part_ref, land, cross, stage, total, sems, consume):
+        barrier, (place > 0).astype(jnp.int32) + (place < count - 1).astype(jnp.int32) + len(others)
+    )
+
+
+class Scatter:
+    def __init__(self, groups, frames_axis, sources, results, scratch):
+        pieces = len(sources)
+        self.pieces = range(pieces)
+        self.sources, self.results = sources, results
+        self.inbox, self.stage, self.kept, self.found = (scratch[i * pieces : (i + 1) * pieces] for i in range(4))
+        self.twin_send, self.twin_recv, self.peer_send, self.peer_recv = scratch[4 * pieces :]
+        self.groups, self.frames_axis = groups, frames_axis
+        self.total = groups // 2 * frames_axis
+        group = lax.axis_index(GROUP)
+        self.core = lax.rem(group, 2)
+        self.me = lax.div(group, 2) * frames_axis + lax.axis_index(FRAME)
+        self.twin = {GROUP: group + 1 - 2 * self.core}
+
+    def peer(self, step):
+        to = lax.rem(self.me + step, self.total)
+        return to, {GROUP: lax.div(to, self.frames_axis) * 2 + self.core, FRAME: lax.rem(to, self.frames_axis)}
+
+    def partners(self):
+        return [self.twin] + [self.peer(step)[1] for step in range(1, self.total)]
+
+    def block(self, piece):
+        return self.sources[piece].shape[0] // (self.groups * self.frames_axis)
+
+    def twin_copy(self, piece, high):
+        rows = self.block(piece) * self.frames_axis
+        first = pl.multiple_of((high * 2 + 1 - self.core) * rows, 16)
+        return remote(
+            self.sources[piece].at[pl.ds(first, rows)],
+            self.inbox[piece].at[pl.ds(high * rows, rows)],
+            self.twin_send.at[piece, high],
+            self.twin_recv.at[piece, high],
+            self.twin,
+        )
+
+    def peer_copy(self, piece, step):
+        return remote(
+            self.stage[piece].at[step],
+            self.found[piece].at[step],
+            self.peer_send.at[piece, step],
+            self.peer_recv.at[piece, step],
+            self.peer(step)[1],
+        )
+
+    def start(self):
+        for piece in self.pieces:
+            for high in range(self.groups // 2):
+                self.twin_copy(piece, high).start()
+
+    def fold(self, step):
+        if step == self.total - 1:
+            for piece in self.pieces:
+                for high in range(self.groups // 2):
+                    self.twin_copy(piece, high).wait_recv()
+        to = self.peer(step)[0]
+        for piece in self.pieces:
+            block = self.block(piece)
+            high, frame = lax.div(to, self.frames_axis), lax.rem(to, self.frames_axis)
+            first = ((high * 2 + self.core) * self.frames_axis + frame) * block
+            mine = self.sources[piece][pl.ds(pl.multiple_of(first, 16), block)]
+            other = self.inbox[piece][pl.ds(pl.multiple_of(to * block, 16), block)]
+            summed = mine.astype(WIDE) + other.astype(WIDE)
+            if step == 0:
+                self.kept[piece][...] = summed
+            else:
+                self.stage[piece][step] = summed.astype(NARROW)
+                self.peer_copy(piece, step).start()
+
+    def finish(self):
+        for piece in self.pieces:
+            for step in range(1, self.total):
+                self.peer_copy(piece, step).wait_recv()
+            summed = self.kept[piece][...]
+            for step in range(1, self.total):
+                summed = summed + self.found[piece][step].astype(WIDE)
+            self.results[piece][...] = summed
+        for piece in self.pieces:
+            for high in range(self.groups // 2):
+                self.twin_copy(piece, high).wait_send()
+            for step in range(1, self.total):
+                self.peer_copy(piece, step).wait_send()
+
+    @staticmethod
+    def shapes(groups, frames_axis, sources):
+        total, many = groups // 2 * frames_axis, len(sources)
+        kept = [(item.shape[0] // (groups * frames_axis), item.shape[1]) for item in sources]
+        results = [jax.ShapeDtypeStruct(shape, WIDE) for shape in kept]
+        scratch = [pltpu.VMEM((item.shape[0] // 2, item.shape[1]), NARROW) for item in sources]
+        scratch += [pltpu.VMEM((total,) + shape, NARROW) for shape in kept]
+        scratch += [pltpu.VMEM(shape, WIDE) for shape in kept]
+        scratch += [pltpu.VMEM((total,) + shape, NARROW) for shape in kept]
+        dma = pltpu.SemaphoreType.DMA
+        scratch += [dma((many, groups // 2))] * 2 + [dma((many, total))] * 2
+        return results, scratch
+
+
+def can_scatter(groups, frames_axis, width):
+    return groups % 2 == 0 and width % (16 * groups * frames_axis) == 0
+
+
+def line_sum(count, place, part_ref, land, cross, stage, total, sems, consume, aside=None):
     in_send, land_recv, cross_recv, out_send, out_recv = sems
     depth = part_ref.shape[0] // CHUNKS
     half = count // 2
@@ -156,6 +267,13 @@
         def _():
             finish(number - LAG)
 
+        if aside is not None:
+            for fold in range(aside.total):
+
+                @pl.when(number == FIRST_FOLD + fold)
+                def _():
+                    aside.fold(aside.total - 1 - fold)
+
         return carry
 
     @pl.when(is_end)
@@ -197,33 +315,36 @@
     line_sum(count, place, part_ref, land, cross, stage, out_ref, sems, consume)
 
 
-def backward_kernel(
-    count, part_ref, base_ref, grad_ref, below_ref, rows_ref,
-    moved_ref, low_ref, sums_ref, total, land, cross, stage, tally, *sems
-):
+def backward_kernel(count, groups, frames_axis, pieces, *refs):
+    part_ref, base_ref, grad_ref, below_ref, rows_ref = refs[:5]
+    sources, refs = refs[5 : 5 + pieces], refs[5 + pieces :]
+    moved_ref, low_ref, sums_ref = refs[:3]
+    results, refs = refs[3 : 3 + pieces], refs[3 + pieces :]
+    total, land, cross, stage, tally = refs[:5]
+    sems, scratch = refs[5:10], refs[10:]
     place = lax.axis_index(LINE)
-    greet_line(place, count)
+    aside = Scatter(groups, frames_axis, sources, results, scratch) if pieces else None
+    greet_line(place, count, aside.partners() if pieces else ())
+    if pieces:
+        aside.start()
     gain, gate = (rows_ref[i : i + 1] for i in range(2))
     tally[...] = jnp.zeros_like(tally)
 
     def consume(rows):
         grads = total[rows].astype(WIDE)
         normal, spread = norm_parts(base_ref[rows])
-        scaled = grads * gain
-        moved = grad_ref[rows] + spread * (
-            scaled
-            - jnp.mean(scaled, axis=-1, keepdims=True)
-            - normal * jnp.mean(scaled * normal, axis=-1, keepdims=True)
-        )
+        moved = grad_ref[rows] + norm_pull(grads * gain, normal, spread)
         moved_ref[rows] = moved
         low_ref[rows] = (gate * moved).astype(NARROW)
         for i, terms in enumerate((grads, grads * normal, moved * below_ref[rows].astype(WIDE))):
             tally[i] += jnp.sum(terms.reshape(-1, 8, terms.shape[-1]), axis=0)
 
-    line_sum(count, place, part_ref, land, cross, stage, total, sems, consume)
+    line_sum(count, place, part_ref, land, cross, stage, total, sems, consume, aside)
     sums_ref[...] = jnp.zeros_like(sums_ref)
     for i in range(3):
         sums_ref[i : i + 1] = jnp.sum(tally[i], axis=0, keepdims=True)
+    if pieces:
+        aside.finish()
 
 
 def vmem(count):
@@ -253,25 +374,224 @@
     )(part, base, rows)
 
 
-def call_backward(count, part, base, grad, below, rows):
+def call_backward(count, groups, frames_axis, part, base, grad, below, rows, sources, kernel_id):
     shape = part.shape
+    results, scratch = Scatter.shapes(groups, frames_axis, sources) if sources else ([], [])
     return pl.pallas_call(
-        functools.partial(backward_kernel, count),
+        functools.partial(backward_kernel, count, groups, frames_axis, len(sources)),
         out_shape=(
             jax.ShapeDtypeStruct(shape, WIDE),
             jax.ShapeDtypeStruct(shape, NARROW),
             jax.ShapeDtypeStruct((8, shape[1]), WIDE),
+            *results,
         ),
-        in_specs=vmem(5),
-        out_specs=tuple(vmem(3)),
+        in_specs=vmem(5 + len(sources)),
+        out_specs=tuple(vmem(3 + len(sources))),
         scratch_shapes=[pltpu.VMEM(shape, NARROW)] * 4
         + [pltpu.VMEM((3, 8, shape[1]), WIDE)]
-        + line_sems(),
+        + line_sems()
+        + scratch,
         compiler_params=pltpu.CompilerParams(
-            collective_id=2, has_side_effects=True, vmem_limit_bytes=VMEM_LIMIT
+            collective_id=kernel_id, has_side_effects=True, vmem_limit_bytes=VMEM_LIMIT
         ),
         name="backward_sum",
-    )(part, base, grad, below, rows)
+    )(part, base, grad, below, rows, *sources)
+
+
+def closing_kernel(count, groups, frames_axis, pieces, *refs):
+    part_ref, base_ref, grad_ref, small_ref, rows_ref = refs[:5]
+    sources, refs = refs[5 : 5 + pieces], refs[5 + pieces :]
+    latent_ref, every_ref = refs[:2]
+    results, refs = refs[2 : 2 + pieces], refs[2 + pieces :]
+    land, stage, line_rows, own_rows, tally = refs[:5]
+    from_left, from_right, to_left, to_right, line_send, line_recv, all_send, all_recv = refs[5:13]
+    place, group, here = (lax.axis_index(axis) for axis in (LINE, GROUP, FRAME))
+    last = count - 1
+    frames, share = latent_ref.shape[0], latent_ref.shape[1]
+    everyone = groups * frames_axis
+    rank = group * frames_axis + here
+    aside = Scatter(groups, frames_axis, sources, results, refs[13:]) if pieces else None
+
+    def member(ahead):
+        to = lax.rem(rank + ahead, everyone)
+        return {GROUP: lax.div(to, frames_axis), FRAME: lax.rem(to, frames_axis)}
+
+    def neighbour(ahead):
+        return {LINE: lax.rem(place + ahead, count)}
+
+    barrier = pltpu.get_barrier_semaphore()
+
+    def greet(ahead, carry):
+        pl.semaphore_signal(barrier, inc=1, device_id=member(ahead), device_id_type=MESH)
+        return carry
+
+    for ahead in range(1, count):
+        pl.semaphore_signal(barrier, inc=1, device_id=neighbour(ahead), device_id_type=MESH)
+    lax.fori_loop(1, everyone, greet, 0)
+    pl.semaphore_wait(barrier, last + everyone - 1)
+
+    def rows_of(owner):
+        return pl.ds(pl.multiple_of(owner * share, share), share)
+
+    def pass_on(owner, frame, right):
+        side = 0 if right else 1
+        return remote(
+            stage.at[side, owner, frame],
+            land.at[side, owner, frame],
+            (to_right if right else to_left).at[owner, frame],
+            (from_left if right else from_right).at[owner, frame],
+            {LINE: place + 1 if right else place - 1},
+        )
+
+    def relay(distance, right):
+        owner = place + distance if right else place - distance
+        source = (place == 0) if right else (place == last)
+
+        @pl.when((owner <= last) if right else (owner >= 0))
+        def _():
+            for frame in range(frames):
+                side = 0 if right else 1
+
+                @pl.when(source)
+                def _():
+                    stage[side, owner, frame] = part_ref[frame, rows_of(owner)]
+
+                @pl.when(jnp.logical_not(source))
+                def _():
+                    pass_on(owner, frame, right).wait_recv()
+                    stage[side, owner, frame] = (
+                        part_ref[frame, rows_of(owner)].astype(WIDE) + land[side, owner, frame].astype(WIDE)
+                    ).astype(NARROW)
+
+                pass_on(owner, frame, right).start()
+
+    def relay_both(distance):
+        relay(distance, True)
+        relay(distance, False)
+
+    if pieces:
+        aside.start()
+    relay_both(last)
+
+    tally[...] = jnp.zeros_like(tally)
+    depth = 32
+    blocks = base_ref.shape[1] // depth
+
+    def add_rows(number, carry):
+        frame, rows = lax.div(number, blocks), pl.ds(pl.multiple_of(lax.rem(number, blocks) * depth, depth), depth)
+        normal = norm_parts(base_ref[frame, rows])[0]
+        grads = part_ref[frame, rows].astype(WIDE)
+        for i, terms in enumerate((grads, grads * normal)):
+            tally[i] += jnp.sum(terms.reshape(-1, 8, terms.shape[-1]), axis=0)
+        return carry
+
+    lax.fori_loop(0, frames * blocks, add_rows, 0)
+    line_rows[place] = small_ref[0:8]
+    for i in range(2):
+        line_rows[place, i : i + 1] = jnp.sum(tally[i], axis=0, keepdims=True)
+
+    def line_copy(ahead):
+        return remote(
+            line_rows.at[place], line_rows.at[place], line_send.at[ahead], line_recv.at[ahead], neighbour(ahead)
+        )
+
+    def all_copy(ahead):
+        return remote(
+            own_rows, every_ref.at[rank], all_send.at[ahead], all_recv.at[ahead], member(ahead)
+        )
+
+    for ahead in range(1, count):
+        line_copy(ahead).start()
+    for distance in range(last - 1, 0, -1):
+        relay_both(distance)
+        if pieces and distance == last - 1:
+            for fold in range(aside.total):
+                aside.fold(aside.total - 1 - fold)
+    for ahead in range(1, count):
+        line_copy(ahead).wait_recv()
+    summed = line_rows[0]
+    for i in range(1, count):
+        summed = summed + line_rows[i]
+    own_rows[0:8] = summed
+    own_rows[8:16] = small_ref[8:16]
+    every_ref[rank] = own_rows[...]
+
+    def send_rows(ahead, carry):
+        all_copy(ahead).start()
+        return carry
+
+    lax.fori_loop(1, everyone, send_rows, 0)
+
+    own = rows_of(place)
+    for frame in range(frames):
+        for right in (True, False):
+            @pl.when((place > 0) if right else (place < last))
+            def _():
+                pass_on(place, frame, right).wait_recv()
+
+        left_part = jnp.where(place > 0, land[0, place, frame].astype(WIDE), 0.0)
+        right_part = jnp.where(place < last, land[1, place, frame].astype(WIDE), 0.0)
+        grads = part_ref[frame, own].astype(WIDE) + left_part + right_part
+        normal, spread = norm_parts(base_ref[frame, own])
+        latent_ref[frame] = (
+            grad_ref[frame, own] + norm_pull(grads * rows_ref[0:1], normal, spread)
+        ).astype(NARROW)
+
+    for owner in range(count):
+        for frame in range(frames):
+
+            @pl.when(owner > place)
+            def _():
+                pass_on(owner, frame, True).wait_send()
+
+            @pl.when(owner < place)
+            def _():
+                pass_on(owner, frame, False).wait_send()
+
+    for ahead in range(1, count):
+        line_copy(ahead).wait_send()
+
+    def settle(ahead, carry):
+        all_copy(ahead).wait_recv()
+        all_copy(ahead).wait_send()
+        return carry
+
+    lax.fori_loop(1, everyone, settle, 0)
+    if pieces:
+        aside.finish()
+
+
+def call_closing(count, groups, frames_axis, part, base, grad, small, rows, sources):
+    frames, patches, features = part.shape
+    everyone = groups * frames_axis
+    share = patches // count
+    results, scratch = Scatter.shapes(groups, frames_axis, sources) if sources else ([], [])
+    dma = pltpu.SemaphoreType.DMA
+    return pl.pallas_call(
+        functools.partial(closing_kernel, count, groups, frames_axis, len(sources)),
+        out_shape=(
+            jax.ShapeDtypeStruct((frames, share, features), NARROW),
+            jax.ShapeDtypeStruct((everyone, 16, features), WIDE),
+            *results,
+        ),
+        in_specs=vmem(5 + len(sources)),
+        out_specs=tuple(vmem(2 + len(sources))),
+        scratch_shapes=[
+            pltpu.VMEM((2, count, frames, share, features), NARROW),
+            pltpu.VMEM((2, count, frames, share, features), NARROW),
+            pltpu.VMEM((count, 8, features), WIDE),
+            pltpu.VMEM((16, features), WIDE),
+            pltpu.VMEM((2, 8, features), WIDE),
+        ]
+        + [dma((count, frames))] * 4
+        + [dma((count,))] * 2
+        + [dma((everyone,))] * 2
+        + scratch,
+        compiler_params=pltpu.CompilerParams(
+            collective_id=4, has_side_effects=True, vmem_limit_bytes=VMEM_LIMIT
+        ),
+        name="closing",
+    )(part, base, grad, small, rows, *sources)
 
 
 def opening_kernel(
@@ -474,6 +794,334 @@
     )(latent, act, ada, captions)
 
 
+STAGES = 4
+MIDDLE_ROWS = 32
+MIDDLE_LAG = 2
+
+
+def gelu_both(values):
+    square = values * values
+    bent = jnp.tanh(0.7978845608028654 * (values + 0.044715 * values * square))
+    slope = 0.5 * (1.0 + bent) + 0.5 * values * (1.0 - bent * bent) * (
+        0.7978845608028654 * (1.0 + 3.0 * 0.044715 * square)
+    )
+    return 0.5 * values * (1.0 + bent), slope
+
+
+def middle_kernel(
+    count, frames, first_ref, base_ref, cotangent_ref, rows_ref, bias_ref,
+    keys_ref, values_ref, query_w, out_w, up_w, down_w,
+    base_three, grad_two, low_two, low_three, low_four, normed_three, normed_four,
+    active, grad_inner, heads_out, grad_query, grad_keys, grad_values, sums_ref,
+    base_two, grad_three, branch_two, query, grad_heads, part, mixed, tally,
+    land, cross, stage, total, in_send, land_recv, cross_recv, out_send, out_recv,
+):
+    place = lax.axis_index(LINE)
+    greet_line(place, count)
+    half = count // 2
+    left = place < half
+    level = jnp.where(left, place, count - 1 - place)
+    inner = jnp.where(left, place + 1, place - 1)
+    outer = jnp.where(left, place - 1, place + 1)
+    is_end, is_middle = level == 0, level == half - 1
+    inside = jnp.logical_not(is_end)
+    patches = base_ref.shape[0] // frames
+    chunks = patches // MIDDLE_ROWS
+    slots = STAGES * frames
+    scale = HD ** (-0.5)
+    width = bias_ref.shape[2]
+    local = query_w.shape[0]
+    half_heads = local // HD // 2
+    tile = up_w.shape[1] // 3
+    gate_two, cross_gain, gain_three, shift_three, gate_three = (rows_ref[i : i + 1] for i in range(5))
+
+    def where_of(slot, chunk):
+        rows = pl.ds(pl.multiple_of(lax.rem(slot, frames) * patches + chunk * MIDDLE_ROWS, MIDDLE_ROWS), MIDDLE_ROWS)
+        return lax.rem(lax.div(slot, frames), 2), rows
+
+    def inward(slot, chunk):
+        side, rows = where_of(slot, chunk)
+        return remote(
+            stage.at[side, rows], land.at[side, rows], in_send.at[slot, chunk], land_recv.at[slot, chunk], {LINE: inner}
+        )
+
+    def across(slot, chunk):
+        side, rows = where_of(slot, chunk)
+        return remote(
+            stage.at[side, rows], cross.at[side, rows], in_send.at[slot, chunk], cross_recv.at[slot, chunk], {LINE: inner}
+        )
+
+    def outward(slot, chunk):
+        side, rows = where_of(slot, chunk)
+        return remote(
+            total.at[side, rows], total.at[side, rows], out_send.at[slot, chunk], out_recv.at[slot, chunk], {LINE: outer}
+        )
+
+    def own_part(slot, rows):
+        return jnp.where(slot < frames, first_ref[rows], part[rows])
+
+    def send_in(slot, chunk):
+        @pl.when(is_middle)
+        def _():
+            across(slot, chunk).start()
+
+        @pl.when(jnp.logical_not(is_middle))
+        def _():
+            inward(slot, chunk).start()
+
+    def sent(slot, chunk):
+        @pl.when(is_middle)
+        def _():
+            across(slot, chunk).wait_send()
+
+        @pl.when(jnp.logical_not(is_middle))
+        def _():
+            inward(slot, chunk).wait_send()
+
+        @pl.when(inside)
+        def _():
+            outward(slot, chunk).wait_send()
+
+    def free(slot, chunk):
+        @pl.when(slot >= 2 * frames)
+        def _():
+            sent(slot - 2 * frames, chunk)
+
+    def gather_in(slot, chunk):
+        side, rows = where_of(slot, chunk)
+        free(slot, chunk)
+        inward(slot, chunk).wait_recv()
+        stage[side, rows] = (own_part(slot, rows).astype(WIDE) + land[side, rows].astype(WIDE)).astype(NARROW)
+        send_in(slot, chunk)
+
+    def add_rows(which, terms):
+        tally[which] += jnp.sum(terms.reshape(-1, 8, terms.shape[-1]), axis=0)
+
+    def consume(slot, rows, summed):
+        number = lax.div(slot, frames)
+
+        @pl.when(number == 0)
+        def _():
+            branch_two[rows] = summed
+            moved = base_ref[rows] + gate_two * summed.astype(WIDE)
+            base_two[rows] = moved
+            normed_three[rows] = (norm_parts(moved)[0] * cross_gain).astype(NARROW)
+
+        @pl.when(number == 1)
+        def _():
+            moved = base_two[rows] + summed.astype(WIDE)
+            base_three[rows] = moved
+            normed_four[rows] = (norm_parts(moved)[0] * gain_three + shift_three).astype(NARROW)
+            low_four[rows] = (gate_three * cotangent_ref[rows].astype(WIDE)).astype(NARROW)
+
+        @pl.when(number == 2)
+        def _():
+            grads = summed.astype(WIDE)
+            normal, spread = norm_parts(base_three[rows])
+            moved = cotangent_ref[rows].astype(WIDE) + norm_pull(grads * gain_three, normal, spread)
+            grad_three[rows] = moved
+            low_three[rows] = moved.astype(NARROW)
+            add_rows(0, grads)
+            add_rows(1, grads * normal)
+
+        @pl.when(number == 3)
+        def _():
+            grads = summed.astype(WIDE)
+            normal, spread = norm_parts(base_two[rows])
+            moved = grad_three[rows] + norm_pull(grads * cross_gain, normal, spread)
+            grad_two[rows] = moved
+            low_two[rows] = (gate_two * moved).astype(NARROW)
+            add_rows(2, grads * normal)
+            add_rows(3, moved * branch_two[rows].astype(WIDE))
+
+    def finish(slot, chunk):
+        side, rows = where_of(slot, chunk)
+
+        @pl.when(is_middle)
+        def _():
+            across(slot, chunk).wait_recv()
+            total[side, rows] = (stage[side, rows].astype(WIDE) + cross[side, rows].astype(WIDE)).astype(NARROW)
+
+        @pl.when(jnp.logical_not(is_middle))
+        def _():
+            outward(slot, chunk).wait_recv()
+
+        @pl.when(inside)
+        def _():
+            outward(slot, chunk).start()
+
+        consume(slot, rows, total[side, rows])
+
+    def head_rows(head):
+        return pl.ds(head * width, width)
+
+    def probs_of(stream, asked, head):
+        scores = scale * dot(asked, keys_ref[head_rows(head)], 1, 1) + bias_ref[stream, 0:1]
+        raised = jnp.exp(scores - jnp.max(scores, axis=-1, keepdims=True))
+        return raised / jnp.sum(raised, axis=-1, keepdims=True)
+
+    def cross_forward(piece, stream, rows):
+        if piece == 0:
+            query[rows] = dot(normed_three[rows], query_w[...], 1, 1).astype(NARROW)
+        elif piece in (1, 2):
+            asked = query[rows]
+            found = jnp.zeros((patches, local), WIDE) if piece == 1 else mixed[...]
+            for head in range((piece - 1) * half_heads, piece * half_heads):
+                probs = probs_of(stream, asked, head).astype(NARROW)
+                found = found + dot(probs, values_ref[head_rows(head)], 1, 0)
+            if piece == 1:
+                mixed[...] = found
+            else:
+                heads_out[rows] = found.astype(NARROW)
+        elif piece == 3:
+            part[rows] = dot(heads_out[rows], out_w[...], 1, 0).astype(NARROW)
+
+    def feed_forward(piece, stream, rows):
+        if piece < 3:
+            span = slice(piece * tile, (piece + 1) * tile)
+            inner_values = dot(normed_four[rows], up_w[:, span], 1, 0)
+            pulled = dot(low_four[rows], down_w[span], 1, 1)
+            raised, slope = gelu_both(inner_values)
+            active[rows, span] = raised.astype(NARROW)
+            grad_inner[rows, span] = (pulled * slope).astype(NARROW)
+        else:
+            third = up_w.shape[0] // 3
+            span = slice((piece - 3) * third, (piece - 2) * third)
+            part[rows, span] = dot(grad_inner[rows], up_w[span], 1, 1).astype(NARROW)
+
+    def cross_backward(piece, stream, rows):
+        if piece == 0:
+            grad_heads[rows] = dot(low_three[rows], out_w[...], 1, 1).astype(NARROW)
+        elif piece in (1, 2):
+            asked, given = query[rows], grad_heads[rows]
+            found = jnp.zeros((patches, local), WIDE) if piece == 1 else mixed[...]
+            for head in range((piece - 1) * half_heads, piece * half_heads):
+                spot = head_rows(head)
+                probs = probs_of(stream, asked, head)
+                pulled = dot(given, values_ref[spot], 1, 1)
+                grad_scores = probs * (pulled - jnp.sum(pulled * probs, axis=-1, keepdims=True))
+                grad_scores = grad_scores.astype(NARROW)
+                found = found + dot(grad_scores, keys_ref[spot], 1, 0)
+                grad_keys[spot] += dot(grad_scores, asked, 0, 0)
+                grad_values[spot] += dot(probs.astype(NARROW), given, 0, 0)
+            if piece == 1:
+                mixed[...] = found
+            else:
+                grad_query[rows] = (scale * found).astype(NARROW)
+        elif piece == 3:
+            part[rows] = dot(grad_query[rows], query_w[...], 1, 0).astype(NARROW)
+
+    tally[...] = jnp.zeros_like(tally)
+    grad_keys[...] = jnp.zeros_like(grad_keys)
+    grad_values[...] = jnp.zeros_like(grad_values)
+
+    def step(number, carry):
+        slot, chunk = lax.div(number, chunks), lax.rem(number, chunks)
+        before = slot - 1
+
+        @pl.when(is_end & (chunk == 0))
+        def _():
+            @pl.when(slot < slots)
+            def _():
+                def begin(item, inner_carry):
+                    side, rows = where_of(slot, item)
+                    free(slot, item)
+                    stage[side, rows] = own_part(slot, rows)
+                    send_in(slot, item)
+                    return inner_carry
+
+                lax.fori_loop(0, chunks, begin, 0)
+
+            @pl.when(slot > 0)
+            def _():
+                def end(item, inner_carry):
+                    finish(before, item)
+                    return inner_carry
+
+                lax.fori_loop(0, chunks, end, 0)
+
+        @pl.when(inside & (slot < slots))
+        def _():
+            gather_in(slot, chunk)
+
+            @pl.when(chunk >= MIDDLE_LAG)
+            def _():
+                finish(slot, chunk - MIDDLE_LAG)
+
+        @pl.when(inside & (slot > 0) & (chunk < MIDDLE_LAG))
+        def _():
+            finish(before, chunks - MIDDLE_LAG + chunk)
+
+        stream = lax.rem(jnp.maximum(before, 0), frames)
+        rows = pl.ds(pl.multiple_of(stream * patches, patches), patches)
+        for which, work in enumerate((cross_forward, feed_forward, cross_backward)):
+
+            @pl.when((slot > 0) & (lax.div(jnp.maximum(before, 0), frames) == which))
+            def _():
+                for piece in range(6 if which == 1 else 4):
+
+                    @pl.when(chunk == MIDDLE_LAG + piece)
+                    def _():
+                        work(piece, stream, rows)
+
+        return carry
+
+    lax.fori_loop(0, slots * chunks + MIDDLE_LAG, step, 0)
+
+    def settle(number, carry):
+        sent(lax.div(number, chunks), lax.rem(number, chunks))
+        return carry
+
+    lax.fori_loop((slots - 2 * frames) * chunks, slots * chunks, settle, 0)
+    sums_ref[...] = jnp.zeros_like(sums_ref)
+    for i in range(4):
+        sums_ref[i : i + 1] = jnp.sum(tally[i], axis=0, keepdims=True)
+
+
+def call_middle(count, frames, first, base, cotangent, rows, bias, keys, values, query_w, out_w, up_w, down_w):
+    tokens, features = first.shape
+    local, hidden = query_w.shape[0], up_w.shape[1]
+    chunks = tokens // frames // MIDDLE_ROWS
+
+    def wide(*shape):
+        return jax.ShapeDtypeStruct(shape, WIDE)
+
+    def narrow(*shape):
+        return jax.ShapeDtypeStruct(shape, NARROW)
+
+    results = (
+        [wide(tokens, features)] * 2
+        + [narrow(tokens, features)] * 5
+        + [narrow(tokens, hidden)] * 2
+        + [narrow(tokens, local)] * 2
+        + [wide(*keys.shape)] * 2
+        + [wide(8, features)]
+    )
+    sem = pltpu.SemaphoreType.DMA((STAGES * frames, chunks))
+    return pl.pallas_call(
+        functools.partial(middle_kernel, count, frames),
+        out_shape=tuple(results),
+        in_specs=vmem(11),
+        out_specs=tuple(vmem(len(results))),
+        scratch_shapes=[
+            pltpu.VMEM((tokens, features), WIDE),
+            pltpu.VMEM((tokens, features), WIDE),
+            pltpu.VMEM((tokens, features), NARROW),
+            pltpu.VMEM((tokens, local), NARROW),
+            pltpu.VMEM((tokens, local), NARROW),
+            pltpu.VMEM((tokens, features), NARROW),
+            pltpu.VMEM((tokens // frames, local), WIDE),
+            pltpu.VMEM((4, 8, features), WIDE),
+        ]
+        + [pltpu.VMEM((2, tokens, features), NARROW)] * 4
+        + [sem] * 5,
+        compiler_params=pltpu.CompilerParams(
+            collective_id=7, has_side_effects=True, vmem_limit_bytes=60 * 2**20
+        ),
+        name="middle",
+    )(first, base, cotangent, rows, bias, keys, values, query_w, out_w, up_w, down_w)
+
+
 def attend_scores(query, keys, key_valid):
     raw_scores = HD ** (-0.5) * jnp.einsum("fphe,fqhe->fhpq", query, keys, preferred_element_type=WIDE)
     if key_valid is None:
@@ -569,6 +1217,8 @@
 
 
 def sum_matrix_grads(pieces):
+    if not pieces:
+        return []
     packed = jnp.concatenate([piece.astype(NARROW) for piece in pieces], axis=1)
     summed = lax.psum_scatter(packed, BOTH, scatter_dimension=0, tiled=True).astype(WIDE)
     found, start = [], 0
@@ -619,8 +1269,6 @@
         jnp.transpose(ada_weight, (1, 0, 2)), caption_here,
     )
     base_zero, spatial_hidden = flat(base_grid), flat(normed_grid)
-    cotangent_full = flat(lax.all_gather(cotangent[0], LINE, axis=1, tiled=True))
-
     text_part = dot(caption_here, caption_proj, 1, 0).astype(NARROW)
     text_rows = lax.all_gather(text_part, LINE, axis=1, tiled=True)
 
@@ -641,6 +1289,9 @@
         rows_of(mods[2], 1.0 + mods[4], mods[3]),
     )
 
+    cotangent_here, temporal_hidden = lax.optimization_barrier((cotangent[0], temporal_hidden))
+    cotangent_full = flat(lax.all_gather(cotangent_here, LINE, axis=1, tiled=True))
+
     temporal_packed = dot(temporal_hidden, temporal_in, 1, 1).astype(NARROW)
     temporal_query = heads(temporal_packed[:, 0:local])
     own_pair = grid(temporal_packed[:, local:])
@@ -663,74 +1314,45 @@
     )
     temporal_probs = temporal_weights(temporal_query, temporal_keys, allowed, frames)
     temporal_flat = flat(temporal_mix(temporal_probs, temporal_values, frames).astype(NARROW))
-    temporal_out, base_two, cross_hidden = call_forward(
-        count,
-        dot(temporal_flat, temporal_outproj, 1, 0).astype(NARROW),
-        base_one,
-        rows_of(mods[5], cross_gain.astype(WIDE), jnp.zeros((features,), WIDE)),
-    )
-
-    cross_packed = dot(cross_hidden, query_in, 1, 1).astype(NARROW)
     text_packed = dot(text_rows, keyval_in, 1, 1).astype(NARROW)
-
-    def each_frame(values):
-        return jnp.broadcast_to(split_heads(values)[None], (frames, slots, local // HD, HD))
-
-    text_keys, text_values = (each_frame(text_packed[:, i * local : (i + 1) * local]) for i in range(2))
+    slot_pad = -slots % 128
     slot_index = jnp.arange(slots)
     key_valid = (own_clip[:, None] == (slot_index // text_length)[None, :]) & (
         slot_index % text_length < jnp.repeat(text_counts[0], text_length)
     )[None, :]
-    cross_queries = heads(cross_packed)
-    cross_heads, cross_logs = attend_forward(cross_queries, text_keys, text_values, key_valid)
-    cross_flat = flat(cross_heads)
-    cross_out, base_three, mlp_hidden = call_forward(
-        count,
-        dot(cross_flat, cross_outproj, 1, 0).astype(NARROW),
-        base_two,
-        rows_of(jnp.ones((features,), WIDE), 1.0 + mods[7], mods[6]),
-    )
-
-    mlp_inner = dot(mlp_hidden, mlp_up, 1, 0)
-    mlp_active, gelu_pull = jax.vjp(gelu_tanh, mlp_inner)
-    mlp_low = mlp_active.astype(NARROW)
-    grad_four = cotangent_full.astype(WIDE)
-    grad_mlp_low = (mods[8] * grad_four).astype(NARROW)
-    grad_active = dot(grad_mlp_low, mlp_down, 1, 1)
-    grad_inner = gelu_pull(grad_active)[0].astype(NARROW)
-    grad_three, grad_cross_low, sums_mlp = call_backward(
-        count,
-        dot(grad_inner, mlp_up, 1, 1).astype(NARROW),
-        base_three,
-        grad_four,
-        cross_out,
-        rows_of(1.0 + mods[7], jnp.ones((features,), WIDE)),
-    )
-    mlp_out = lax.psum_scatter(
-        grid(dot(mlp_low, mlp_down, 1, 0).astype(NARROW)), LINE, scatter_dimension=1, tiled=True
-    ).astype(WIDE)
+    bias = jnp.pad(jnp.where(key_valid, 0.0, NEGATIVE), ((0, 0), (0, slot_pad)), constant_values=NEGATIVE)
+    bias = jnp.broadcast_to(bias[:, None], (frames, 8, slots + slot_pad))
+    head_mask = (jnp.arange(local) // HD)[None, :] == jnp.arange(local // HD)[:, None]
+
+    def by_head(values):
+        padded = jnp.pad(values, ((0, slot_pad), (0, 0)))
+        return jnp.where(head_mask[:, None], padded[None], 0).reshape(-1, local)
+
+    def from_heads(values):
+        kept = jnp.where(head_mask[:, None], values.reshape(local // HD, -1, local), 0.0)
+        return jnp.sum(kept, axis=0)[0:slots]
+
+    (
+        base_three, grad_two, grad_temporal_low, grad_cross_low, grad_mlp_low, cross_hidden, mlp_hidden,
+        mlp_low, grad_inner, cross_flat, grad_cross_packed, text_grad_keys, text_grad_values, sums_middle,
+    ) = call_middle(
+        count, frames, dot(temporal_flat, temporal_outproj, 1, 0).astype(NARROW), base_one, cotangent_full,
+        rows_of(mods[5], cross_gain.astype(WIDE), 1.0 + mods[7], mods[6], mods[8]), bias,
+        by_head(text_packed[:, :local]), by_head(text_packed[:, local:]),
+        query_in, cross_outproj, mlp_up, mlp_down,
+    )
+
+    inside = can_scatter(groups, frames_axis, features)
+
+    def matrix_grad(first, second):
+        return dot(first, second, 0, 0).astype(NARROW)
+
+    mlp_part = dot(mlp_low, mlp_down, 1, 0).astype(NARROW)
+    mlp_out = lax.psum_scatter(grid(mlp_part), LINE, scatter_dimension=1, tiled=True).astype(WIDE)
     output = (own(base_three) + mods[8] * mlp_out).astype(NARROW)[None]
     gate_mlp_part = jnp.sum(cotangent[0].astype(WIDE) * mlp_out, axis=(0, 1))
-    grad_up, grad_down = sum_matrix_grads(
-        [dot(mlp_hidden, grad_inner, 0, 0), dot(grad_mlp_low, mlp_low, 0, 0)]
-    )
-
-    grad_cross_heads = dot(grad_cross_low, cross_outproj, 1, 1).astype(NARROW)
-    cross_grad_query, text_grad_keys, text_grad_values = attend_backward(
-        cross_queries, text_keys, text_values, key_valid, cross_logs, heads(grad_cross_heads)
-    )
-    grad_cross_packed = flat(cross_grad_query).astype(NARROW)
-    grad_two, grad_temporal_low, sums_cross = call_backward(
-        count,
-        dot(grad_cross_packed, query_in, 1, 0).astype(NARROW),
-        base_two,
-        grad_three,
-        temporal_out,
-        rows_of(cross_gain.astype(WIDE), mods[5]),
-    )
     grad_text_packed = jnp.concatenate(
-        [jnp.sum(part, axis=0).reshape(slots, local) for part in (text_grad_keys, text_grad_values)],
-        axis=1,
+        [HD ** (-0.5) * from_heads(text_grad_keys), from_heads(text_grad_values)], axis=1
     )
     text_high, text_rest = split_pair(grad_text_packed)
     grad_keyval_part = dot(text_rows, text_high, 0, 0) + dot(text_rows, text_rest, 0, 0)
@@ -741,13 +1363,6 @@
     text_all_high, text_all_rest = split_pair(text_grad_wide)
     caption_rows = caption_share.reshape(groups * slots, -1)
     grad_caption = dot(caption_rows, text_all_high, 0, 0) + dot(caption_rows, text_all_rest, 0, 0)
-    grad_query_cross, grad_outproj_cross, grad_keyval_cross = sum_matrix_grads(
-        [
-            dot(cross_hidden, grad_cross_packed, 0, 0),
-            dot(grad_cross_low, cross_flat, 0, 0),
-            grad_keyval_part,
-        ]
-    )
 
     grad_temporal_heads = dot(grad_temporal_low, temporal_outproj, 1, 1).astype(NARROW)
     temporal_grad_query, near_grad_keys, near_grad_values = temporal_backward(
@@ -774,17 +1389,13 @@
     grad_temporal_packed = jnp.concatenate(
         [flat(temporal_grad_query).astype(NARROW), flat(own_grads).astype(NARROW)], axis=1
     )
-    grad_one, grad_spatial_low, sums_temporal = call_backward(
-        count,
-        dot(grad_temporal_packed, temporal_in, 1, 0).astype(NARROW),
-        base_one,
-        grad_two,
-        spatial_out,
-        rows_of(1.0 + mods[4], mods[2]),
-    )
-    grad_inproj_temporal, grad_outproj_temporal = sum_matrix_grads(
-        [dot(temporal_hidden, grad_temporal_packed, 0, 0), dot(grad_temporal_low, temporal_flat, 0, 0)]
-    )
+    early = [matrix_grad(mlp_hidden, grad_inner), matrix_grad(grad_mlp_low, mlp_low)]
+    found = call_backward(
+        count, groups, frames_axis, dot(grad_temporal_packed, temporal_in, 1, 0).astype(NARROW), base_one,
+        grad_two, spatial_out, rows_of(1.0 + mods[4], mods[2]), early if inside else [], 2,
+    )
+    grad_one, grad_spatial_low, sums_temporal = found[:3]
+    grad_up, grad_down = found[3:] if inside else sum_matrix_grads(early)
 
     grad_spatial_heads = dot(grad_spatial_low, spatial_outproj, 1, 1).astype(NARROW)
     spatial_grads = attend_backward(
@@ -792,37 +1403,40 @@
     )
     grad_spatial_packed = jnp.concatenate([flat(part) for part in spatial_grads], axis=1).astype(NARROW)
     grad_spatial_part = dot(grad_spatial_packed, spatial_in, 1, 0).astype(NARROW)
-    grad_spatial_normed = lax.psum_scatter(
-        grid(grad_spatial_part), LINE, scatter_dimension=1, tiled=True
-    ).astype(WIDE)
-    normal, spread = norm_parts(own(base_zero))
-    scaled = grad_spatial_normed * (1.0 + mods[1])
-    grad_latent = own(grad_one) + spread * (
-        scaled
-        - jnp.mean(scaled, axis=-1, keepdims=True)
-        - normal * jnp.mean(scaled * normal, axis=-1, keepdims=True)
-    )
-    shift_part = jnp.sum(grad_spatial_normed, axis=(0, 1))
-    scale_part = jnp.sum(grad_spatial_normed * normal, axis=(0, 1))
-    grad_inproj_spatial, grad_outproj_spatial = sum_matrix_grads(
-        [dot(spatial_hidden, grad_spatial_packed, 0, 0), dot(grad_spatial_low, spatial_flat, 0, 0)]
-    )
-
-    shift_spatial, scale_spatial, gate_mlp = lax.psum(
-        jnp.stack([shift_part, scale_part, gate_mlp_part]), LINE
-    )
     side_row = jnp.pad(jnp.concatenate([cond_row, chosen]), (0, features - local - chosen.shape[0]))
+    blank = jnp.zeros((features,), WIDE)
     small = jnp.stack(
-        [
-            shift_spatial, scale_spatial, sums_temporal[2], sums_temporal[0], sums_temporal[1],
-            sums_cross[2], sums_mlp[0], sums_mlp[1], gate_mlp, sums_cross[1], side_row,
+        [blank, blank, gate_mlp_part]
+        + [blank] * 5
+        + [
+            sums_temporal[2], sums_temporal[0], sums_temporal[1], sums_middle[3], sums_middle[0],
+            sums_middle[1], sums_middle[2], side_row,
         ]
     )
-    small_all = lax.all_gather(small, BOTH).reshape(groups, frames_axis, 11, features)
-    modulation_grad = jnp.sum(small_all[:, :, 0:9], axis=1)
-    grad_gain = jnp.sum(small_all[:, :, 9], axis=(0, 1))
-    cond_all = small_all[:, 0, 10, 0:local]
-    chosen_all = small_all[:, 0, 10, local : local + chosen.shape[0]]
+    late = [
+        matrix_grad(cross_hidden, grad_cross_packed),
+        matrix_grad(grad_cross_low, cross_flat),
+        grad_keyval_part.astype(NARROW),
+        matrix_grad(temporal_hidden, grad_temporal_packed),
+        matrix_grad(grad_temporal_low, temporal_flat),
+        matrix_grad(spatial_hidden, grad_spatial_packed),
+        matrix_grad(grad_spatial_low, spatial_flat),
+    ]
+    found = call_closing(
+        count, groups, frames_axis, grid(grad_spatial_part), grid(base_zero), grid(grad_one), small,
+        rows_of(1.0 + mods[1]), late if inside else [],
+    )
+    grad_latent, small_all = found[:2]
+    late_grads = found[2:] if inside else sum_matrix_grads(late)
+    grad_query_cross, grad_outproj_cross, grad_keyval_cross = late_grads[:3]
+    grad_inproj_temporal, grad_outproj_temporal, grad_inproj_spatial, grad_outproj_spatial = late_grads[3:]
+
+    small_all = small_all.reshape(groups, frames_axis, 16, features)
+    small_sums = jnp.sum(small_all, axis=1)
+    modulation_grad = jnp.stack([small_sums[:, i] for i in (0, 1, 8, 9, 10, 11, 12, 13, 2)], axis=1)
+    grad_gain = jnp.sum(small_sums[:, 14], axis=0)
+    cond_all = small_all[:, 0, 15, 0:local]
+    chosen_all = small_all[:, 0, 15, local : local + chosen.shape[0]]
     act_all, swish_pull = jax.vjp(swish_act, cond_all)
     act_all = act_all.astype(NARROW).astype(WIDE)
     column = features // (groups * frames_axis)
@@ -838,7 +1452,7 @@
 
     return (
         output,
-        grad_latent.astype(NARROW)[None],
+        grad_latent[None],
         grad_table,
         grad_ada,
         unpack(grad_inproj_spatial, 3),

time: 715 us -> 580 us (0.81)
  waiting for transfers between devices: 137 us -> 0.1 us
  Pallas kernels: 267 us -> 342 us
  blocking collectives: 54.4 us -> 15.6 us
  other arithmetic: 46.1 us -> 31.5 us
  local copies, waits for them, and re-layouts: 92.7 us -> 81.6 us
    pallas_call x3, Pallas kernels: 115 us -> 271 us  [the longest x1 134 us: call_middle(): pl.pallas_call(functools.partial(middle_kernel, count, frames), out_shape...]
    unnamed x13 -> x4, waiting for transfers between devices: 135 us -> 0.07 us
    pallas_call x3 -> x1, Pallas kernels: 102 us -> 36.8 us  [call_forward(): pl.pallas_call(functools.partial(forward_kernel, count), out_shape=(jax.S...]
    unnamed x285 -> x236, local copies, waits for them, and re-layouts: 69.7 us -> 31.1 us
    all_gather x1 -> x0, blocking collectives: 20.4 us -> none  [per_device(): lax.all_gather(small, BOTH).reshape(groups, frames_axis, 11, features)]
    psum x1 -> x0, blocking collectives: 17.5 us -> none  [per_device(): lax.psum(jnp.stack([shift_part, scale_part, gate_mlp_part]), LINE)]
    pallas_call x1, Pallas kernels: 51 us -> 34.4 us  [call_opening(): pl.pallas_call(functools.partial(opening_kernel, count, groups, frames_ax...]
    convert_element_type x1 -> x6, local copies, waits for them, and re-layouts: 0.31 us -> 14.8 us  [matrix_grad(): return dot(first, second, 0, 0).astype(NARROW)]
  transfers between devices with their start and end apart: 13 -> 8, of which waited for: 4 -> 0; matrix products, arithmetic and copies ran while one was open for 21% -> 20% of each run, Pallas kernels for 28% -> 24%
where the time goes in v1:
time: 580 us; the launch traced here: 571 us
  Pallas kernels  342 us (59%)
  local copies, waits for them, and re-layouts  81.6 us (14%)
  matrix products  70.5 us (12%)
  other arithmetic  31.5 us (5%)
  between operations  16.3 us (3%)
  blocking collectives  15.6 us (3%)
  starting transfers between devices  12.8 us (2%)
    pallas_call x1, Pallas kernels, call_middle(): pl.pallas_call(functools.partial(middle_kernel, count, frames), out_shape...  134 us
    pallas_call x1, Pallas kernels, call_closing(): pl.pallas_call(functools.partial(closing_kernel, count, groups, frames_ax...  76.7 us
    pallas_call x1, Pallas kernels, call_backward(): pl.pallas_call(functools.partial(backward_kernel, count, groups, frames_a...  60.8 us
    dot_general x25, matrix products, dot(): lax.dot_general(first, second, (((contract_first,), (contract_second,)),...  51.4 us
    pallas_call x1, Pallas kernels, call_forward(): pl.pallas_call(functools.partial(forward_kernel, count), out_shape=(jax.S...  36.8 us
    pallas_call x1, Pallas kernels, call_opening(): pl.pallas_call(functools.partial(opening_kernel, count, groups, frames_ax...  34.4 us
    unnamed x236, local copies, waits for them, and re-layouts  31.1 us
    all_gather x1, blocking collectives, per_device(): text_rows = lax.all_gather(text_part, LINE, axis=1, tiled=True)  15.6 us
  transfers between devices with their start and end apart: 8, of which 0 were waited for; matrix products, arithmetic and copies ran while one was open for 20% of the time, Pallas kernels for 24%

profile of v1, /device:TPU:0, one launch (start us, length us, event | category | flops | bytes accessed | tf_op | source)
XLA Modules:
  0.0 570.7 jit_solution(9488547462682814906)
XLA Ops:
  9.3 1.5 copy-done.4
  11.8 34.4 %opening.1 = (f32[2,256,1152]{2,1,0:T(8,128)}, bf16[2,256,1152]{2,1,0:T(8,128)(2,1)S(1)}, f32[16,1152]{1,0:T(8,128)S(1)}, bf16[4,240,512]{2,1,0:T(8,128)(2,1)S(1)}) custom-call(bf16[2,64,1152]{2,1,0:T(8,128)(2,1)S(1)} %bitcast.352, bf16[16,288]{1,0:T(8,128)(2,1)S(1)} %broadcast_in_dim.125.act_ref, bf16[9,288,1152]{2,1,0:T(8,128)(2,1)} %bitcast.359, ...), custom_call_target="tpu_custom_call" | custom-call | tf_op jit(solution)/shard_map/opening/pallas_call | solution.py:765
  49.2 1.7 reshape_reshape.18
  51.0 1.7 reshape_reshape.20
  52.7 1.7 reshape_reshape.19
  54.5 1.5 multiply_reduce_fusion.1
  58.3 1.9 convolution_convert_fusion.8.part_ref
  61.5 36.8 %forward_sum.1 = (bf16[512,1152]{1,0:T(8,128)(2,1)S(1)}, f32[512,1152]{1,0:T(8,128)S(1)}, bf16[512,1152]{1,0:T(8,128)(2,1)S(1)}) custom-call(bf16[512,1152]{1,0:T(8,128)(2,1)S(1)} %copy-done.9, f32[512,1152]{1,0:T(8,128)} %bitcast.360, f32[8,1152]{1,0:T(8,128)S(1)} %stack.65.rows_ref), custom_call_target="tpu_custom_call" | custom-call | tf_op jit(solution)/shard_map/forward_sum/pallas_call | solution.py:360
  102.0 3.3 convolution_convert_fusion.13
  108.2 2.6 reshape.472
  110.9 6.0 %collective-permute-start = (bf16[2,256,576]{1,0,2:T(2,128)(2,1)}, bf16[2,256,576]{1,0,2:T(2,128)(2,1)}, u32[]{:S(2)}, u32[]{:S(2)}) collective-permute-start(bf16[2,256,576]{1,0,2:T(2,128)(2,1)} %reshape.472), channel_id=1, source_target_pairs={{0,4},{1,5},{2,6},{3,7},{8,12},{9,13},{10,14},{11,15},{16,20},{17,... | collective-permute-start | bytes 1769480 | tf_op jit(solution)/shard_map/ppermute | solution.py:1211
  118.1 1.7 fusion.95
  127.2 2.5 convolution_convert_fusion.20
  129.6 15.6 %all_gather.13 = bf16[240,1152]{0,1:T(8,128)(2,1)S(1)} all-gather(bf16[240,288]{0,1:T(8,128)(2,1)S(1)} %convolution_convert_fusion.20), channel_id=1, replica_groups=mesh['group'=4,'frame'=2,'tensor'=4] {'tensor'}, dimensions={1}, use_global_device_ids=true | all-gather | bytes 691200 | tf_op jit(solution)/shard_map/all_gather | solution.py:1273
  151.6 5.4 pad_maximum_fusion.4
  160.4 1.9 convolution_convert_fusion.7.first_ref
  162.9 133.6 %middle.1 = (f32[512,1152]{1,0:T(8,128)}, f32[512,1152]{1,0:T(8,128)}, bf16[512,1152]{1,0:T(8,128)(2,1)}, bf16[512,1152]{1,0:T(8,128)(2,1)}, bf16[512,1152]{1,0:...) custom-call(bf16[512,1152]{1,0:T(8,128)(2,1)} %convolution_convert_f, ...), custom_call_target="tpu_custom_call" | custom-call | tf_op jit(solution)/shard_map/middle/pallas_call | solution.py:1101
  298.8 1.8 convolution_convert_fusion.17
  303.2 2.7 fusion.22
  310.1 1.5 copy.222.refs_5_
  311.7 2.9 convolution_convert_fusion.11
  314.6 2.4 copy.223.refs_6_
  317.0 1.7 fusion.28
  318.7 2.1 fusion.34
  321.6 3.9 collective-permute-start.3
  330.1 1.7 fusion
  332.1 4.9 convolution_convert_fusion.refs_6_
  339.2 2.9 convolution_convert_fusion.6
  342.0 1.8 convolution_add_fusion
  343.8 2.7 copy.221.refs_7_
  346.6 5.0 convolution_convert_fusion.1.refs_5_
  354.3 2.6 convolution_convert_fusion.3
  356.9 1.5 convolution_convert_fusion.5.refs_0_
  358.5 60.8 %backward_sum.1 = (f32[512,1152]{1,0:T(8,128)}, bf16[512,1152]{1,0:T(8,128)(2,1)S(1)}, f32[8,1152]{1,0:T(8,128)S(1)}, f32[144,1152]{1,0:T(8,128)S(1)}, f32[144,1152]{1,0:T(8,128)S(1)}) custom-call(bf16[512,1152]{1,0:T(8,128)(2,1)S(1)} %convolution_convert_fusion.5.refs_0_, f32[512,1152]{1,0:T(8,128)} %copy-done.2, f32[512,1152]{1,0:T(8,128)} %get-tuple-element.62.refs_2_, ...), custom_call_target="tpu_custom_call" | custom-call | tf_op jit(solution)/shard_map/backward_sum/pallas_call | solution.py:380
  424.4 2.9 fusion.9
  428.7 4.1 copy.224.refs_8_
  432.8 2.3 copy.227.refs_11_
  436.5 2.5 multiply_reduce_fusion
  442.7 2.6 convolution_convert_fusion.2
  445.3 4.1 copy.226.refs_10_
  449.4 4.4 convolution_convert_fusion.4
  453.9 2.0 fusion.17
  457.2 76.7 %closing.1 = (bf16[2,64,1152]{2,1,0:T(8,128)(2,1)S(1)}, f32[8,16,1152]{2,1,0:T(8,128)S(1)}, f32[144,288]{1,0:T(8,128)S(1)}, f32[144,288]{1,0:T(8,128)S(1)}, f32[...) custom-call(bf16[2,256,1152]{2,1,0:T(8,128)(2,1)} %bitcast.407, ...), custom_call_target="tpu_custom_call" | custom-call | tf_op jit(solution)/shard_map/closing/pallas_call | solution.py:570
  538.5 2.1 reshape.513
  540.6 1.7 reshape.511
  544.5 7.4 %convolution_bitcast_fusion.2 = f32[4,288]{1,0:T(4,128)S(1)} fusion(f32[4,9,1152]{2,0,1:T(4,128)S(1)} %constant_dynamic-update-slice_fusion.5, bf16[288,9,1152]{2,0,1:T(8,128)(2,1)} %param.27), kind=kOutput, calls=%fused_computation.50 | convolution fusion | flops 143327232 | bytes 6142464 | tf_op jit(solution)/shard_map/ckd,gkd->gc/dot_general | solution.py:1446
  552.8 2.5 fusion.53
  555.3 1.6 convert_reduce_fusion
  (362 shorter events, 80.8 us)
Async XLA Ops:
  7.2 120.0 %copy-start = (bf16[4096,288]{0,1:T(8,128)(2,1)S(1)}, bf16[4096,288]{0,1:T(8,128)(2,1)}, u32[]{:S(2)}) copy-start(bf16[4096,288]{0,1:T(8,128)(2,1)} %param.32) | copy-start | bytes 7077892
  7.2 155.1 %all-gather.5.cloned.1.call-start = ((), (), s32[]{:S(2)}) async-start(), calls=%async_computation.2 | async-start | bytes 1474560 | tf_op jit(solution)/shard_map/all_gather | solution.py:1293
  11.8 35.1 %copy-start.101 = (bf16[1152,3,288]{0,2,1:T(8,128)(2,1)S(1)}, bf16[1152,3,288]{0,2,1:T(8,128)(2,1)}, u32[]{:S(2)}) copy-start(bf16[1152,3,288]{0,2,1:T(8,128)(2,1)} %param.28) | copy-start | bytes 5971972
  102.0 351.9 %reduce-scatter.5.cloned.1.call-start = ((), (), s32[]{:S(2)}) async-start(), calls=%async_computation.4 | async-start | bytes 737280 | tf_op jit(solution)/shard_map/reduce_scatter | solution.py:1360
  106.1 44.1 %collective-permute-start.1 = (bf16[1,256,576]{1,2,0:T(8,128)(2,1)}, bf16[1,256,576]{1,2,0:T(8,128)(2,1)}, u32[]{:S(2)}, u32[]{:S(2)}) collective-permute-start(bf16[1,256,576]{1,2,0:T(8,128)(2,1)} %slice_bitcast_fusion), channel_id=1, source_target_pairs={{4,0},{5,1},{6,2},{7,3},{12,8},{13,9},{14,10},{15,11},{20,16},{21,... | collective-permute-start | bytes 884744 | tf_op jit(solution)/shard_map/ppermute | solution.py:1216
  110.9 40.7 %collective-permute-start = (bf16[2,256,576]{1,0,2:T(2,128)(2,1)}, bf16[2,256,576]{1,0,2:T(2,128)(2,1)}, u32[]{:S(2)}, u32[]{:S(2)}) collective-permute-start(bf16[2,256,576]{1,0,2:T(2,128)(2,1)} %reshape.472), channel_id=1, source_target_pairs={{0,4},{1,5},{2,6},{3,7},{8,12},{9,13},{10,14},{11,15},{16,20},{17,... | collective-permute-start | bytes 1769480 | tf_op jit(solution)/shard_map/ppermute | solution.py:1211
  127.2 18.1 %copy-start.37 = (bf16[1152,2,288]{0,2,1:T(8,128)(2,1)S(1)}, bf16[1152,2,288]{0,2,1:T(8,128)(2,1)}, u32[]{:S(2)}) copy-start(bf16[1152,2,288]{0,2,1:T(8,128)(2,1)} %param.35) | copy-start | bytes 3981316
  145.9 2.9 copy-start.91
  148.2 3.4 copy-start.41
  151.6 5.5 copy-start.63
  162.9 135.9 %copy-start.104 = (bf16[288,1152]{1,0:T(8,128)(2,1)S(1)}, bf16[288,1152]{1,0:T(8,128)(2,1)}, u32[]{:S(2)}) copy-start(bf16[288,1152]{1,0:T(8,128)(2,1)} %param.31) | copy-start | bytes 1990660
  296.6 4.1 copy-start.58
  303.2 3.5 copy-start.46
  303.2 3.5 copy-start.48
  305.9 2.8 copy-start.57
  305.9 2.8 copy-start.70
  311.6 5.3 copy-start.69
  311.7 5.3 copy-start.86
  311.7 5.3 copy-start.87
  311.7 5.3 copy-start.88
  311.7 5.3 copy-start.89
  311.7 5.3 copy-start.90
  314.6 4.1 copy-start.81
  314.6 4.1 copy-start.82
  314.6 4.1 copy-start.83
  314.6 4.1 copy-start.84
  314.6 4.1 copy-start.85
  318.7 8.9 %copy-start.54 = (f32[1024,288]{1,0:T(8,128)S(1)}, f32[1024,288]{1,0:T(8,128)}, u32[]{:S(2)}) copy-start(f32[1024,288]{1,0:T(8,128)} %get-tuple-element.75) | copy-start | bytes 3538948
  318.7 8.9 %copy-start.55 = (f32[1024,288]{1,0:T(8,128)S(1)}, f32[1024,288]{1,0:T(8,128)}, u32[]{:S(2)}) copy-start(f32[1024,288]{1,0:T(8,128)} %get-tuple-element.76) | copy-start | bytes 3538948
  318.7 8.9 %copy-start.92 = (pred[4,288]{1,0:T(4,128)(4,1)S(1)}, pred[4,288]{1,0:T(4,128)(4,1)}, u32[]{:S(2)}) copy-start(pred[4,288]{1,0:T(4,128)(4,1)} %iota_compare_fusion.1) | copy-start | bytes 3460
  321.6 30.0 %collective-permute-start.3 = (bf16[1,256,576]{1,2,0:T(8,128)(2,1)}, bf16[1,256,576]{1,2,0:T(8,128)(2,1)}, u32[]{:S(2)}, u32[]{:S(2)}) collective-permute-start(bf16[1,256,576]{1,2,0:T(8,128)(2,1)} %pad_maximum_fusion.5), channel_id=1, source_target_pairs={{0,4},{1,5},{2,6},{3,7},{8,12},{9,13},{10,14},{11,15},{16,20},{17,... | collective-permute-start | bytes 884744 | tf_op jit(solution)/shard_map/ppermute | solution.py:1211
  326.3 25.3 %collective-permute-start.2 = (bf16[2,256,576]{1,2,0:T(8,128)(2,1)}, bf16[2,256,576]{1,2,0:T(8,128)(2,1)}, u32[]{:S(2)}, u32[]{:S(2)}) collective-permute-start(bf16[2,256,576]{1,2,0:T(8,128)(2,1)} %maximum_maximum_fusion), channel_id=1, source_target_pairs={{4,0},{5,1},{6,2},{7,3},{12,8},{13,9},{14,10},{15,11},{20,16},{21,... | collective-permute-start | bytes 1769480 | tf_op jit(solution)/shard_map/ppermute | solution.py:1216
  331.8 122.1 %reduce-scatter.3.cloned.1.call-start = ((), (), s32[]{:S(2)}) async-start(), calls=%async_computation.3 | async-start | bytes 1474560 | tf_op jit(solution)/shard_map/reduce_scatter | solution.py:1351
  332.0 4.9 copy-start.36
  332.1 4.9 copy-start.40
  346.5 208.8 %all-gather.7.cloned.1.call-start = ((), (), s32[]{:S(2)}) async-start(), calls=%async_computation.5 | async-start | bytes 1327104 | tf_op jit(solution)/shard_map/all_gather | solution.py:1361
  346.6 5.0 copy-start.64
  346.6 5.0 copy-start.65
  346.6 5.0 copy-start.66
  346.6 5.0 copy-start.67
  358.5 63.5 %copy-start.106 = (bf16[288,1152]{1,0:T(8,128)(2,1)S(1)}, bf16[288,1152]{1,0:T(8,128)(2,1)}, u32[]{:S(2)}) copy-start(bf16[288,1152]{1,0:T(8,128)(2,1)} %param.29) | copy-start | bytes 1990660
  424.3 3.0 copy-start.6
  424.3 3.0 copy-start.62
  449.4 4.5 copy-start.60
  537.5 5.7 copy-start.68
  558.8 3.5 copy-start.13
  559.5 3.6 copy-start.11
  560.9 3.1 copy-start.1
  (69 other events, 105.9 us)
Sparse Core Ops, SparseCore 0:
  102.1 29.8 all-gather.4
  331.9 22.2 reduce-scatter.4
  356.5 44.2 reduce-scatter.2
  454.0 26.9 all-gather.6

commit v2 on v1

--- a/solution.py
+++ b/solution.py
@@ -19,7 +19,6 @@
 MESH = pl.DeviceIdType.MESH
 CHUNKS = 16
 LAG = 2
-FIRST_FOLD = 3
 VMEM_LIMIT = 48 * 2**20
 
 
@@ -76,7 +75,7 @@
     )
 
 
-def greet_line(place, count, others=()):
+def greet_line(place, count, more=0, others=()):
     barrier = pltpu.get_barrier_semaphore()
     for where in others:
         pl.semaphore_signal(barrier, inc=1, device_id=where, device_id_type=MESH)
@@ -90,18 +89,17 @@
         pl.semaphore_signal(barrier, inc=1, device_id={LINE: place + 1}, device_id_type=MESH)
 
     pl.semaphore_wait(
-        barrier, (place > 0).astype(jnp.int32) + (place < count - 1).astype(jnp.int32) + len(others)
+        barrier, (place > 0).astype(jnp.int32) + (place < count - 1).astype(jnp.int32) + len(others) + more
     )
 
 
 class Scatter:
-    def __init__(self, groups, frames_axis, sources, results, scratch):
-        pieces = len(sources)
-        self.pieces = range(pieces)
-        self.sources, self.results = sources, results
-        self.inbox, self.stage, self.kept, self.found = (scratch[i * pieces : (i + 1) * pieces] for i in range(4))
-        self.twin_send, self.twin_recv, self.peer_send, self.peer_recv = scratch[4 * pieces :]
+    def __init__(self, groups, frames_axis, source, scratch):
+        self.source = source
+        self.inbox, self.stage, self.found, self.kept = scratch[:4]
+        self.twin_send, self.twin_recv, self.peer_send, self.peer_recv = scratch[4:8]
         self.groups, self.frames_axis = groups, frames_axis
+        self.block = source.shape[0] // (groups * frames_axis)
         self.total = groups // 2 * frames_axis
         group = lax.axis_index(GROUP)
         self.core = lax.rem(group, 2)
@@ -115,86 +113,317 @@
     def partners(self):
         return [self.twin] + [self.peer(step)[1] for step in range(1, self.total)]
 
-    def block(self, piece):
-        return self.sources[piece].shape[0] // (self.groups * self.frames_axis)
-
-    def twin_copy(self, piece, high):
-        rows = self.block(piece) * self.frames_axis
+    def twin_copy(self, high):
+        rows = self.block * self.frames_axis
         first = pl.multiple_of((high * 2 + 1 - self.core) * rows, 16)
         return remote(
-            self.sources[piece].at[pl.ds(first, rows)],
-            self.inbox[piece].at[pl.ds(high * rows, rows)],
-            self.twin_send.at[piece, high],
-            self.twin_recv.at[piece, high],
+            self.source.at[pl.ds(first, rows)],
+            self.inbox.at[pl.ds(high * rows, rows)],
+            self.twin_send.at[high],
+            self.twin_recv.at[high],
             self.twin,
         )
 
-    def peer_copy(self, piece, step):
+    def peer_copy(self, step):
         return remote(
-            self.stage[piece].at[step],
-            self.found[piece].at[step],
-            self.peer_send.at[piece, step],
-            self.peer_recv.at[piece, step],
+            self.stage.at[step - 1],
+            self.found.at[step - 1],
+            self.peer_send.at[step],
+            self.peer_recv.at[step],
             self.peer(step)[1],
         )
 
     def start(self):
-        for piece in self.pieces:
-            for high in range(self.groups // 2):
-                self.twin_copy(piece, high).start()
+        for high in range(self.groups // 2):
+            self.twin_copy(high).start()
 
     def fold(self, step):
         if step == self.total - 1:
-            for piece in self.pieces:
-                for high in range(self.groups // 2):
-                    self.twin_copy(piece, high).wait_recv()
+            for high in range(self.groups // 2):
+                self.twin_copy(high).wait_recv()
         to = self.peer(step)[0]
-        for piece in self.pieces:
-            block = self.block(piece)
-            high, frame = lax.div(to, self.frames_axis), lax.rem(to, self.frames_axis)
-            first = ((high * 2 + self.core) * self.frames_axis + frame) * block
-            mine = self.sources[piece][pl.ds(pl.multiple_of(first, 16), block)]
-            other = self.inbox[piece][pl.ds(pl.multiple_of(to * block, 16), block)]
-            summed = mine.astype(WIDE) + other.astype(WIDE)
-            if step == 0:
-                self.kept[piece][...] = summed
-            else:
-                self.stage[piece][step] = summed.astype(NARROW)
-                self.peer_copy(piece, step).start()
-
-    def finish(self):
-        for piece in self.pieces:
+        high, frame = lax.div(to, self.frames_axis), lax.rem(to, self.frames_axis)
+        first = ((high * 2 + self.core) * self.frames_axis + frame) * self.block
+        mine = self.source[pl.ds(pl.multiple_of(first, 16), self.block)]
+        other = self.inbox[pl.ds(pl.multiple_of(to * self.block, 16), self.block)]
+        summed = mine.astype(WIDE) + other.astype(WIDE)
+        if step == 0:
+            self.kept[...] = summed
+        else:
+            self.stage[step - 1] = summed.astype(NARROW)
+            self.peer_copy(step).start()
+
+    def fold_all(self):
+        for step in range(self.total - 1, -1, -1):
+            self.fold(step)
+
+    def finish(self, results):
+        for step in range(1, self.total):
+            self.peer_copy(step).wait_recv()
+        start = 0
+        for result in results:
+            span = slice(start, start + result.shape[1])
+            summed = self.kept[:, span]
             for step in range(1, self.total):
-                self.peer_copy(piece, step).wait_recv()
-            summed = self.kept[piece][...]
-            for step in range(1, self.total):
-                summed = summed + self.found[piece][step].astype(WIDE)
-            self.results[piece][...] = summed
-        for piece in self.pieces:
-            for high in range(self.groups // 2):
-                self.twin_copy(piece, high).wait_send()
-            for step in range(1, self.total):
-                self.peer_copy(piece, step).wait_send()
+                summed = summed + self.found[step - 1, :, span].astype(WIDE)
+            result[...] = summed
+            start += result.shape[1]
+        for high in range(self.groups // 2):
+            self.twin_copy(high).wait_send()
+        for step in range(1, self.total):
+            self.peer_copy(step).wait_send()
 
     @staticmethod
-    def shapes(groups, frames_axis, sources):
-        total, many = groups // 2 * frames_axis, len(sources)
-        kept = [(item.shape[0] // (groups * frames_axis), item.shape[1]) for item in sources]
-        results = [jax.ShapeDtypeStruct(shape, WIDE) for shape in kept]
-        scratch = [pltpu.VMEM((item.shape[0] // 2, item.shape[1]), NARROW) for item in sources]
-        scratch += [pltpu.VMEM((total,) + shape, NARROW) for shape in kept]
-        scratch += [pltpu.VMEM(shape, WIDE) for shape in kept]
-        scratch += [pltpu.VMEM((total,) + shape, NARROW) for shape in kept]
+    def scratch(groups, frames_axis, width, columns):
+        total, block = groups // 2 * frames_axis, width // (groups * frames_axis)
         dma = pltpu.SemaphoreType.DMA
-        scratch += [dma((many, groups // 2))] * 2 + [dma((many, total))] * 2
-        return results, scratch
+        return (
+            [pltpu.VMEM((width // 2, columns), NARROW)]
+            + [pltpu.VMEM((total - 1, block, columns), NARROW)] * 2
+            + [pltpu.VMEM((block, columns), WIDE)]
+            + [dma((groups // 2,))] * 2
+            + [dma((total,))] * 2
+        )
 
 
 def can_scatter(groups, frames_axis, width):
     return groups % 2 == 0 and width % (16 * groups * frames_axis) == 0
 
 
-def line_sum(count, place, part_ref, land, cross, stage, total, sems, consume, aside=None):
+class Products:
+    def __init__(self, groups, frames_axis, pairs, results, scratch, scattered):
+        self.pairs, self.results, self.scattered = pairs, results, scattered
+        self.source = scratch[0] if scattered else None
+        self.aside = Scatter(groups, frames_axis, self.source, scratch[1:]) if scattered else None
+
+    def product(self, i):
+        first, second = self.pairs[i]
+        found = dot(first[...], second[...], 0, 0).astype(NARROW)
+        if self.scattered:
+            start = sum(item.shape[1] for _, item in self.pairs[:i])
+            self.source[:, start : start + second.shape[1]] = found
+        else:
+            self.results[i][...] = found
+
+    def work(self):
+        found = [functools.partial(self.product, i) for i in range(len(self.pairs))]
+        return found + ([self.aside.start] if self.scattered else [])
+
+    def partners(self):
+        return self.aside.partners() if self.scattered else []
+
+    def finish(self):
+        if self.scattered:
+            self.aside.finish(self.results)
+
+    @staticmethod
+    def shapes(groups, frames_axis, columns, features):
+        if not can_scatter(groups, frames_axis, features):
+            return [jax.ShapeDtypeStruct((features, n), NARROW) for n in columns], []
+        block = features // (groups * frames_axis)
+        results = [jax.ShapeDtypeStruct((block, n), WIDE) for n in columns]
+        source = [pltpu.VMEM((features, sum(columns)), NARROW)]
+        return results, source + Scatter.scratch(groups, frames_axis, features, sum(columns))
+
+
+class GroupExchange:
+    def __init__(self, groups, frames_axis, source, every, scratch):
+        self.groups, self.frames_axis = groups, frames_axis
+        self.source, self.every = source, every
+        self.near, self.frame_send, self.frame_recv, self.group_send, self.group_recv = scratch
+        self.group, self.frame = lax.axis_index(GROUP), lax.axis_index(FRAME)
+
+    def frame_copy(self, step):
+        return remote(
+            self.source,
+            self.near.at[step - 1],
+            self.frame_send.at[step],
+            self.frame_recv.at[step],
+            {FRAME: lax.rem(self.frame + step, self.frames_axis)},
+        )
+
+    def group_copy(self, step):
+        own = self.every.at[self.group]
+        return remote(
+            own,
+            own,
+            self.group_send.at[step],
+            self.group_recv.at[step],
+            {GROUP: lax.rem(self.group + step, self.groups)},
+        )
+
+    def partners(self):
+        return [
+            {FRAME: lax.rem(self.frame + step, self.frames_axis)} for step in range(1, self.frames_axis)
+        ] + [{GROUP: lax.rem(self.group + step, self.groups)} for step in range(1, self.groups)]
+
+    def start(self):
+        for step in range(1, self.frames_axis):
+            self.frame_copy(step).start()
+
+    def spread(self):
+        for step in range(1, self.frames_axis):
+            self.frame_copy(step).wait_recv()
+        summed = self.source[...].astype(WIDE)
+        for step in range(1, self.frames_axis):
+            summed = summed + self.near[step - 1].astype(WIDE)
+        self.every[self.group] = summed.astype(NARROW)
+        for step in range(1, self.groups):
+            self.group_copy(step).start()
+
+    def finish(self):
+        for step in range(1, self.frames_axis):
+            self.frame_copy(step).wait_send()
+        for step in range(1, self.groups):
+            self.group_copy(step).wait_recv()
+            self.group_copy(step).wait_send()
+
+    @staticmethod
+    def scratch(groups, frames_axis, shape):
+        dma = pltpu.SemaphoreType.DMA
+        return (
+            [pltpu.VMEM((max(frames_axis - 1, 1),) + shape, NARROW)]
+            + [dma((frames_axis,))] * 2
+            + [dma((groups,))] * 2
+        )
+
+
+def grad_tile(first, second, result, start, size):
+    result[start : start + size] = dot(first[:, start : start + size], second[...], 0, 0).astype(NARROW)
+
+
+def can_scatter(groups, frames_axis, width):
+    return groups % 2 == 0 and width % (16 * groups * frames_axis) == 0
+
+
+class LineGather:
+    def __init__(self, count, place, slot_of, sems):
+        self.count, self.place, self.last, self.slot_of = count, place, count - 1, slot_of
+        self.up_send, self.down_send, self.arrived = sems
+
+    def shift(self, owner, up):
+        slot = self.slot_of(owner)
+        to = self.place + 1 if up else self.place - 1
+        sent = (self.up_send if up else self.down_send).at[owner]
+        return remote(slot, slot, sent, self.arrived.at[owner], {LINE: to})
+
+    def start(self):
+        @pl.when(self.place < self.last)
+        def _():
+            self.shift(self.place, True).start()
+
+        @pl.when(self.place > 0)
+        def _():
+            self.shift(self.place, False).start()
+
+    def arrive(self, distance):
+        @pl.when(self.place >= distance)
+        def _():
+            self.shift(self.place - distance, True).wait_recv()
+
+            @pl.when(self.place < self.last)
+            def _():
+                self.shift(self.place - distance, True).start()
+
+        @pl.when(self.place + distance <= self.last)
+        def _():
+            self.shift(self.place + distance, False).wait_recv()
+
+            @pl.when(self.place > 0)
+            def _():
+                self.shift(self.place + distance, False).start()
+
+    def settle(self):
+        for owner in range(self.count):
+
+            @pl.when((self.place < self.last) & (owner <= self.place))
+            def _():
+                self.shift(owner, True).wait_send()
+
+            @pl.when((self.place > 0) & (owner >= self.place))
+            def _():
+                self.shift(owner, False).wait_send()
+
+
+class LineScatter:
+    def __init__(self, count, place, pieces, value_of, land, stage, sems):
+        self.count, self.place, self.last, self.pieces = count, place, count - 1, pieces
+        self.value_of, self.land, self.stage = value_of, land, stage
+        self.from_left, self.from_right, self.to_left, self.to_right = sems
+
+    def pass_on(self, owner, piece, right):
+        side = 0 if right else 1
+        return remote(
+            self.stage.at[side, owner, piece],
+            self.land.at[side, owner, piece],
+            (self.to_right if right else self.to_left).at[owner, piece],
+            (self.from_left if right else self.from_right).at[owner, piece],
+            {LINE: self.place + 1 if right else self.place - 1},
+        )
+
+    def relay(self, distance, right, chosen=None):
+        owner = self.place + distance if right else self.place - distance
+        source = (self.place == 0) if right else (self.place == self.last)
+        side = 0 if right else 1
+
+        @pl.when((owner <= self.last) if right else (owner >= 0))
+        def _():
+            for piece in chosen if chosen is not None else range(self.pieces):
+
+                @pl.when(source)
+                def _():
+                    self.stage[side, owner, piece] = self.value_of(owner, piece)
+
+                @pl.when(jnp.logical_not(source))
+                def _():
+                    self.pass_on(owner, piece, right).wait_recv()
+                    self.stage[side, owner, piece] = (
+                        self.value_of(owner, piece).astype(WIDE) + self.land[side, owner, piece].astype(WIDE)
+                    ).astype(NARROW)
+
+                self.pass_on(owner, piece, right).start()
+
+    def relay_both(self, distance, chosen=None):
+        self.relay(distance, True, chosen)
+        self.relay(distance, False, chosen)
+
+    def total(self, piece):
+        place = self.place
+
+        @pl.when(place > 0)
+        def _():
+            self.pass_on(place, piece, True).wait_recv()
+
+        @pl.when(place < self.last)
+        def _():
+            self.pass_on(place, piece, False).wait_recv()
+
+        left_part = jnp.where(place > 0, self.land[0, place, piece].astype(WIDE), 0.0)
+        right_part = jnp.where(place < self.last, self.land[1, place, piece].astype(WIDE), 0.0)
+        return self.value_of(place, piece).astype(WIDE) + left_part + right_part
+
+    def settle(self):
+        for owner in range(self.count):
+            for piece in range(self.pieces):
+
+                @pl.when(owner > self.place)
+                def _():
+                    self.pass_on(owner, piece, True).wait_send()
+
+                @pl.when(owner < self.place)
+                def _():
+                    self.pass_on(owner, piece, False).wait_send()
+
+
+def gather_sems(count):
+    return [pltpu.SemaphoreType.DMA((count,))] * 3
+
+
+def scatter_sems(count, pieces):
+    return [pltpu.SemaphoreType.DMA((count, pieces))] * 4
+
+
+def line_sum(count, place, part_ref, land, cross, stage, total, sems, consume, early=(), folds=()):
     in_send, land_recv, cross_recv, out_send, out_recv = sems
     depth = part_ref.shape[0] // CHUNKS
     half = count // 2
@@ -259,6 +488,12 @@
         return carry
 
     def step(number, carry):
+        for i, work in enumerate(early):
+
+            @pl.when(jnp.logical_not(is_end) & (number == i))
+            def _():
+                work()
+
         @pl.when(jnp.logical_not(is_end) & (number < CHUNKS))
         def _():
             gather_in(number)
@@ -267,18 +502,19 @@
         def _():
             finish(number - LAG)
 
-        if aside is not None:
-            for fold in range(aside.total):
-
-                @pl.when(number == FIRST_FOLD + fold)
-                def _():
-                    aside.fold(aside.total - 1 - fold)
+        for i, work in enumerate(folds):
+
+            @pl.when(number == len(early) + 1 + i)
+            def _():
+                work()
 
         return carry
 
     @pl.when(is_end)
     def _():
         lax.fori_loop(0, CHUNKS, begin, 0)
+        for work in early:
+            work()
 
     lax.fori_loop(0, CHUNKS + LAG, step, 0)
 
@@ -315,18 +551,24 @@
     line_sum(count, place, part_ref, land, cross, stage, out_ref, sems, consume)
 
 
-def backward_kernel(count, groups, frames_axis, pieces, *refs):
-    part_ref, base_ref, grad_ref, below_ref, rows_ref = refs[:5]
-    sources, refs = refs[5 : 5 + pieces], refs[5 + pieces :]
-    moved_ref, low_ref, sums_ref = refs[:3]
-    results, refs = refs[3 : 3 + pieces], refs[3 + pieces :]
+def fold_works(products):
+    aside = products.aside
+    return [functools.partial(aside.fold, aside.total - 1 - i) for i in range(aside.total)] if aside else []
+
+
+def backward_kernel(count, groups, frames_axis, many, scattered, *refs):
+    part_ref, base_ref, grad_ref, below_ref, rows_ref, text_ref = refs[:6]
+    factors, refs = refs[6 : 6 + 2 * many], refs[6 + 2 * many :]
+    moved_ref, low_ref, sums_ref, text_all = refs[:4]
+    results, refs = refs[4 : 4 + many], refs[4 + many :]
     total, land, cross, stage, tally = refs[:5]
-    sems, scratch = refs[5:10], refs[10:]
+    sems, exchange_scratch, scratch = refs[5:10], refs[10:15], refs[15:]
     place = lax.axis_index(LINE)
-    aside = Scatter(groups, frames_axis, sources, results, scratch) if pieces else None
-    greet_line(place, count, aside.partners() if pieces else ())
-    if pieces:
-        aside.start()
+    pairs = list(zip(factors[0::2], factors[1::2]))
+    products = Products(groups, frames_axis, pairs, results, scratch, scattered)
+    exchange = GroupExchange(groups, frames_axis, text_ref, text_all, exchange_scratch)
+    greet_line(place, count, 0, exchange.partners() + products.partners())
+    exchange.start()
     gain, gate = (rows_ref[i : i + 1] for i in range(2))
     tally[...] = jnp.zeros_like(tally)
 
@@ -339,12 +581,16 @@
         for i, terms in enumerate((grads, grads * normal, moved * below_ref[rows].astype(WIDE))):
             tally[i] += jnp.sum(terms.reshape(-1, 8, terms.shape[-1]), axis=0)
 
-    line_sum(count, place, part_ref, land, cross, stage, total, sems, consume, aside)
+    folds = fold_works(products)
+    line_sum(
+        count, place, part_ref, land, cross, stage, total, sems, consume,
+        products.work(), folds[:1] + [exchange.spread] + folds[1:],
+    )
     sums_ref[...] = jnp.zeros_like(sums_ref)
     for i in range(3):
         sums_ref[i : i + 1] = jnp.sum(tally[i], axis=0, keepdims=True)
-    if pieces:
-        aside.finish()
+    products.finish()
+    exchange.finish()
 
 
 def vmem(count):
@@ -374,43 +620,90 @@
     )(part, base, rows)
 
 
-def call_backward(count, groups, frames_axis, part, base, grad, below, rows, sources, kernel_id):
+def call_backward(count, groups, frames_axis, part, base, grad, below, rows, text, pairs):
     shape = part.shape
-    results, scratch = Scatter.shapes(groups, frames_axis, sources) if sources else ([], [])
+    columns = [second.shape[1] for _, second in pairs]
+    results, scratch = Products.shapes(groups, frames_axis, columns, shape[1])
     return pl.pallas_call(
-        functools.partial(backward_kernel, count, groups, frames_axis, len(sources)),
+        functools.partial(backward_kernel, count, groups, frames_axis, len(pairs), bool(scratch)),
         out_shape=(
             jax.ShapeDtypeStruct(shape, WIDE),
             jax.ShapeDtypeStruct(shape, NARROW),
             jax.ShapeDtypeStruct((8, shape[1]), WIDE),
+            jax.ShapeDtypeStruct((groups,) + text.shape, NARROW),
             *results,
         ),
-        in_specs=vmem(5 + len(sources)),
-        out_specs=tuple(vmem(3 + len(sources))),
+        in_specs=vmem(6 + 2 * len(pairs)),
+        out_specs=tuple(vmem(4 + len(results))),
         scratch_shapes=[pltpu.VMEM(shape, NARROW)] * 4
         + [pltpu.VMEM((3, 8, shape[1]), WIDE)]
         + line_sems()
+        + GroupExchange.scratch(groups, frames_axis, text.shape)
         + scratch,
         compiler_params=pltpu.CompilerParams(
-            collective_id=kernel_id, has_side_effects=True, vmem_limit_bytes=VMEM_LIMIT
+            collective_id=2, has_side_effects=True, vmem_limit_bytes=VMEM_LIMIT
         ),
         name="backward_sum",
-    )(part, base, grad, below, rows, *sources)
-
-
-def closing_kernel(count, groups, frames_axis, pieces, *refs):
-    part_ref, base_ref, grad_ref, small_ref, rows_ref = refs[:5]
-    sources, refs = refs[5 : 5 + pieces], refs[5 + pieces :]
-    latent_ref, every_ref = refs[:2]
-    results, refs = refs[2 : 2 + pieces], refs[2 + pieces :]
-    land, stage, line_rows, own_rows, tally = refs[:5]
-    from_left, from_right, to_left, to_right, line_send, line_recv, all_send, all_recv = refs[5:13]
+    )(part, base, grad, below, rows, text, *(item for pair in pairs for item in pair))
+
+
+def head_mask(head, shape):
+    lane = lax.broadcasted_iota(jnp.int32, shape, len(shape) - 1)
+    return (lane >= head * HD) & (lane < (head + 1) * HD)
+
+
+def spread_heads(values, result):
+    rows = values.shape[0]
+    for head in range(values.shape[1] // HD):
+        kept = jnp.where(head_mask(head, values.shape), values.astype(WIDE), 0.0)
+        result[head * rows : (head + 1) * rows] = kept.astype(NARROW)
+
+
+def collect_heads(values, rows):
+    found = jnp.zeros((rows, values.shape[1]), WIDE)
+    for head in range(values.shape[0] // rows):
+        found = jnp.where(head_mask(head, found.shape), values[head * rows : (head + 1) * rows], found)
+    return found
+
+
+def spatial_backward(given, asked, keys, values, key_rows, value_rows, probs_low, scores_low):
+    rows, scale = asked.shape[0], HD ** (-0.5)
+    heads = asked.shape[1] // HD
+    spread_heads(keys, key_rows)
+    spread_heads(values, value_rows)
+    for head in range(heads):
+        spot = slice(head * rows, (head + 1) * rows)
+        scores = scale * dot(asked, key_rows[spot], 1, 1)
+        raised = jnp.exp(scores - jnp.max(scores, axis=-1, keepdims=True))
+        probs = raised * (1.0 / jnp.sum(raised, axis=-1, keepdims=True))
+        pulled = dot(given, value_rows[spot], 1, 1)
+        moved = probs * (pulled - jnp.sum(pulled * probs, axis=-1, keepdims=True))
+        probs_low[:, spot] = probs.astype(NARROW)
+        scores_low[:, spot] = moved.astype(NARROW)
+    grad_query = scale * dot(scores_low[...], key_rows[...], 1, 0)
+    grad_keys = scale * collect_heads(dot(scores_low[...], asked, 0, 0), rows)
+    grad_values = collect_heads(dot(probs_low[...], given, 0, 0), rows)
+    return grad_query, grad_keys, grad_values
+
+
+def closing_kernel(count, groups, frames_axis, frames, scattered, *refs):
+    (
+        low_ref, base_ref, grad_ref, small_ref, rows_ref, packed_ref, heads_ref, hidden_ref, in_ref, out_ref,
+        latent_ref, every_ref, in_result, out_result,
+        part_ref, grad_packed, key_rows, value_rows, probs_low, scores_low,
+        land, stage, line_rows, own_rows, tally,
+    ) = refs[:25]
+    line_send, line_recv, all_send, all_recv = refs[29:33]
     place, group, here = (lax.axis_index(axis) for axis in (LINE, GROUP, FRAME))
     last = count - 1
-    frames, share = latent_ref.shape[0], latent_ref.shape[1]
+    share = latent_ref.shape[1]
+    local = out_ref.shape[0]
     everyone = groups * frames_axis
     rank = group * frames_axis + here
-    aside = Scatter(groups, frames_axis, sources, results, refs[13:]) if pieces else None
+    products = Products(
+        groups, frames_axis, [(hidden_ref, grad_packed), (low_ref, heads_ref)], [in_result, out_result],
+        refs[33:], scattered,
+    )
 
     def member(ahead):
         to = lax.rem(rank + ahead, everyone)
@@ -433,45 +726,24 @@
     def rows_of(owner):
         return pl.ds(pl.multiple_of(owner * share, share), share)
 
-    def pass_on(owner, frame, right):
-        side = 0 if right else 1
-        return remote(
-            stage.at[side, owner, frame],
-            land.at[side, owner, frame],
-            (to_right if right else to_left).at[owner, frame],
-            (from_left if right else from_right).at[owner, frame],
-            {LINE: place + 1 if right else place - 1},
-        )
-
-    def relay(distance, right):
-        owner = place + distance if right else place - distance
-        source = (place == 0) if right else (place == last)
-
-        @pl.when((owner <= last) if right else (owner >= 0))
-        def _():
-            for frame in range(frames):
-                side = 0 if right else 1
-
-                @pl.when(source)
-                def _():
-                    stage[side, owner, frame] = part_ref[frame, rows_of(owner)]
-
-                @pl.when(jnp.logical_not(source))
-                def _():
-                    pass_on(owner, frame, right).wait_recv()
-                    stage[side, owner, frame] = (
-                        part_ref[frame, rows_of(owner)].astype(WIDE) + land[side, owner, frame].astype(WIDE)
-                    ).astype(NARROW)
-
-                pass_on(owner, frame, right).start()
-
-    def relay_both(distance):
-        relay(distance, True)
-        relay(distance, False)
-
-    if pieces:
-        aside.start()
-    relay_both(last)
+    passing = LineScatter(
+        count, place, frames, lambda owner, frame: part_ref[frame, rows_of(owner)], land, stage, refs[25:29]
+    )
+    patches = base_ref.shape[1]
+    for frame in range(frames):
+        rows = slice(frame * patches, (frame + 1) * patches)
+        given = dot(low_ref[rows], out_ref[...], 1, 1).astype(NARROW)
+        asked, keys, values = (packed_ref[rows, i * local : (i + 1) * local] for i in range(3))
+        parts = jnp.zeros(part_ref.shape[1:], WIDE)
+        found = spatial_backward(given, asked, keys, values, key_rows, value_rows, probs_low, scores_low)
+        for i, item in enumerate(found):
+            low = item.astype(NARROW)
+            grad_packed[rows, i * local : (i + 1) * local] = low
+            parts = parts + dot(low, in_ref[i * local : (i + 1) * local], 1, 0)
+        part_ref[frame] = parts.astype(NARROW)
+        passing.relay_both(last, (frame,))
+    for work in products.work():
+        work()
 
     tally[...] = jnp.zeros_like(tally)
     depth = 32
@@ -503,10 +775,9 @@
     for ahead in range(1, count):
         line_copy(ahead).start()
     for distance in range(last - 1, 0, -1):
-        relay_both(distance)
-        if pieces and distance == last - 1:
-            for fold in range(aside.total):
-                aside.fold(aside.total - 1 - fold)
+        passing.relay_both(distance)
+        if scattered and distance == last - 1:
+            products.aside.fold_all()
     for ahead in range(1, count):
         line_copy(ahead).wait_recv()
     summed = line_rows[0]
@@ -524,30 +795,13 @@
 
     own = rows_of(place)
     for frame in range(frames):
-        for right in (True, False):
-            @pl.when((place > 0) if right else (place < last))
-            def _():
-                pass_on(place, frame, right).wait_recv()
-
-        left_part = jnp.where(place > 0, land[0, place, frame].astype(WIDE), 0.0)
-        right_part = jnp.where(place < last, land[1, place, frame].astype(WIDE), 0.0)
-        grads = part_ref[frame, own].astype(WIDE) + left_part + right_part
+        grads = passing.total(frame)
         normal, spread = norm_parts(base_ref[frame, own])
         latent_ref[frame] = (
             grad_ref[frame, own] + norm_pull(grads * rows_ref[0:1], normal, spread)
         ).astype(NARROW)
 
-    for owner in range(count):
-        for frame in range(frames):
-
-            @pl.when(owner > place)
-            def _():
-                pass_on(owner, frame, True).wait_send()
-
-            @pl.when(owner < place)
-            def _():
-                pass_on(owner, frame, False).wait_send()
-
+    passing.settle()
     for ahead in range(1, count):
         line_copy(ahead).wait_send()
 
@@ -557,33 +811,40 @@
         return carry
 
     lax.fori_loop(1, everyone, settle, 0)
-    if pieces:
-        aside.finish()
-
-
-def call_closing(count, groups, frames_axis, part, base, grad, small, rows, sources):
-    frames, patches, features = part.shape
+    products.finish()
+
+
+def call_closing(count, groups, frames_axis, low, base, grad, small, rows, packed, heads, hidden, in_w, out_w):
+    frames, patches, features = base.shape
     everyone = groups * frames_axis
     share = patches // count
-    results, scratch = Scatter.shapes(groups, frames_axis, sources) if sources else ([], [])
+    local = out_w.shape[0]
+    results, scratch = Products.shapes(groups, frames_axis, [packed.shape[1], local], features)
     dma = pltpu.SemaphoreType.DMA
+    wide_keys = local // HD * patches
     return pl.pallas_call(
-        functools.partial(closing_kernel, count, groups, frames_axis, len(sources)),
+        functools.partial(closing_kernel, count, groups, frames_axis, frames, bool(scratch)),
         out_shape=(
             jax.ShapeDtypeStruct((frames, share, features), NARROW),
             jax.ShapeDtypeStruct((everyone, 16, features), WIDE),
             *results,
         ),
-        in_specs=vmem(5 + len(sources)),
-        out_specs=tuple(vmem(2 + len(sources))),
+        in_specs=vmem(10),
+        out_specs=tuple(vmem(4)),
         scratch_shapes=[
+            pltpu.VMEM((frames, patches, features), NARROW),
+            pltpu.VMEM(packed.shape, NARROW),
+            pltpu.VMEM((wide_keys, local), NARROW),
+            pltpu.VMEM((wide_keys, local), NARROW),
+            pltpu.VMEM((patches, wide_keys), NARROW),
+            pltpu.VMEM((patches, wide_keys), NARROW),
             pltpu.VMEM((2, count, frames, share, features), NARROW),
             pltpu.VMEM((2, count, frames, share, features), NARROW),
             pltpu.VMEM((count, 8, features), WIDE),
             pltpu.VMEM((16, features), WIDE),
             pltpu.VMEM((2, 8, features), WIDE),
         ]
-        + [dma((count, frames))] * 4
+        + scatter_sems(count, frames)
         + [dma((count,))] * 2
         + [dma((everyone,))] * 2
         + scratch,
@@ -591,7 +852,7 @@
             collective_id=4, has_side_effects=True, vmem_limit_bytes=VMEM_LIMIT
         ),
         name="closing",
-    )(part, base, grad, small, rows, *sources)
+    )(low, base, grad, small, rows, packed, heads, hidden, in_w, out_w)
 
 
 def opening_kernel(
@@ -796,7 +1057,7 @@
 
 STAGES = 4
 MIDDLE_ROWS = 32
-MIDDLE_LAG = 2
+MIDDLE_LAG = 3
 
 
 def gelu_both(values):
@@ -808,16 +1069,26 @@
     return 0.5 * values * (1.0 + bent), slope
 
 
-def middle_kernel(
-    count, frames, first_ref, base_ref, cotangent_ref, rows_ref, bias_ref,
-    keys_ref, values_ref, query_w, out_w, up_w, down_w,
-    base_three, grad_two, low_two, low_three, low_four, normed_three, normed_four,
-    active, grad_inner, heads_out, grad_query, grad_keys, grad_values, sums_ref,
-    base_two, grad_three, branch_two, query, grad_heads, part, mixed, tally,
-    land, cross, stage, total, in_send, land_recv, cross_recv, out_send, out_recv,
-):
+def middle_kernel(count, groups, frames_axis, frames, scattered, *refs):
+    (
+        first_ref, base_ref, cotangent_ref, rows_ref, bias_ref,
+        keys_ref, values_ref, query_w, out_w, up_w, down_w,
+        base_three, grad_two, low_two, low_three, normed_three, heads_out, grad_query,
+        grad_keys, grad_values, sums_ref, extra_part, up_result, down_result,
+        normed_four, low_four, active, grad_inner, base_two, branch_two, query, grad_heads, part, mixed, tally,
+        land, stage, total, cross, in_send, land_recv, cross_recv, out_send, out_recv, *scratch,
+    ) = refs
     place = lax.axis_index(LINE)
-    greet_line(place, count)
+    if scattered:
+        up_grad, down_grad, *scratch = scratch
+        asides = [
+            Scatter(groups, frames_axis, source, scratch[i * 8 : (i + 1) * 8])
+            for i, source in enumerate((up_grad, down_grad))
+        ]
+        greet_line(place, count, 0, asides[0].partners())
+    else:
+        up_grad, down_grad, asides = up_result, down_result, []
+        greet_line(place, count)
     half = count // 2
     left = place < half
     level = jnp.where(left, place, count - 1 - place)
@@ -840,21 +1111,21 @@
         return lax.rem(lax.div(slot, frames), 2), rows
 
     def inward(slot, chunk):
-        side, rows = where_of(slot, chunk)
+        rows = where_of(slot, chunk)[1]
         return remote(
-            stage.at[side, rows], land.at[side, rows], in_send.at[slot, chunk], land_recv.at[slot, chunk], {LINE: inner}
+            stage.at[rows], land.at[rows], in_send.at[slot, chunk], land_recv.at[slot, chunk], {LINE: inner}
         )
 
     def across(slot, chunk):
         side, rows = where_of(slot, chunk)
         return remote(
-            stage.at[side, rows], cross.at[side, rows], in_send.at[slot, chunk], cross_recv.at[slot, chunk], {LINE: inner}
+            stage.at[rows], cross.at[side, rows], in_send.at[slot, chunk], cross_recv.at[slot, chunk], {LINE: inner}
         )
 
     def outward(slot, chunk):
-        side, rows = where_of(slot, chunk)
+        rows = where_of(slot, chunk)[1]
         return remote(
-            total.at[side, rows], total.at[side, rows], out_send.at[slot, chunk], out_recv.at[slot, chunk], {LINE: outer}
+            total.at[rows], total.at[rows], out_send.at[slot, chunk], out_recv.at[slot, chunk], {LINE: outer}
         )
 
     def own_part(slot, rows):
@@ -883,15 +1154,15 @@
             outward(slot, chunk).wait_send()
 
     def free(slot, chunk):
-        @pl.when(slot >= 2 * frames)
-        def _():
-            sent(slot - 2 * frames, chunk)
+        @pl.when(slot >= frames)
+        def _():
+            sent(slot - frames, chunk)
 
     def gather_in(slot, chunk):
-        side, rows = where_of(slot, chunk)
+        rows = where_of(slot, chunk)[1]
         free(slot, chunk)
         inward(slot, chunk).wait_recv()
-        stage[side, rows] = (own_part(slot, rows).astype(WIDE) + land[side, rows].astype(WIDE)).astype(NARROW)
+        stage[rows] = (own_part(slot, rows).astype(WIDE) + land[rows].astype(WIDE)).astype(NARROW)
         send_in(slot, chunk)
 
     def add_rows(which, terms):
@@ -919,7 +1190,7 @@
             grads = summed.astype(WIDE)
             normal, spread = norm_parts(base_three[rows])
             moved = cotangent_ref[rows].astype(WIDE) + norm_pull(grads * gain_three, normal, spread)
-            grad_three[rows] = moved
+            grad_two[rows] = moved
             low_three[rows] = moved.astype(NARROW)
             add_rows(0, grads)
             add_rows(1, grads * normal)
@@ -928,7 +1199,7 @@
         def _():
             grads = summed.astype(WIDE)
             normal, spread = norm_parts(base_two[rows])
-            moved = grad_three[rows] + norm_pull(grads * cross_gain, normal, spread)
+            moved = grad_two[rows] + norm_pull(grads * cross_gain, normal, spread)
             grad_two[rows] = moved
             low_two[rows] = (gate_two * moved).astype(NARROW)
             add_rows(2, grads * normal)
@@ -940,7 +1211,7 @@
         @pl.when(is_middle)
         def _():
             across(slot, chunk).wait_recv()
-            total[side, rows] = (stage[side, rows].astype(WIDE) + cross[side, rows].astype(WIDE)).astype(NARROW)
+            total[rows] = (stage[rows].astype(WIDE) + cross[side, rows].astype(WIDE)).astype(NARROW)
 
         @pl.when(jnp.logical_not(is_middle))
         def _():
@@ -950,7 +1221,7 @@
         def _():
             outward(slot, chunk).start()
 
-        consume(slot, rows, total[side, rows])
+        consume(slot, rows, total[rows])
 
     def head_rows(head):
         return pl.ds(head * width, width)
@@ -1011,6 +1282,36 @@
         elif piece == 3:
             part[rows] = dot(grad_query[rows], query_w[...], 1, 0).astype(NARROW)
 
+    def up_tile(number):
+        grad_tile(normed_four, grad_inner, up_grad, number * third, third)
+
+    def down_tile(number):
+        grad_tile(low_four, active, down_grad, number * third, third)
+
+    def extra(frame):
+        rows = slice(frame * patches, (frame + 1) * patches)
+        extra_part[rows] = dot(active[rows], down_w[...], 1, 0).astype(NARROW)
+
+    third = up_w.shape[0] // 3
+    late = {}
+
+    def later(slot, chunk, work, *args):
+        late.setdefault((slots - 3 + slot, chunk), []).append(functools.partial(work, *args))
+
+    for i, spot in enumerate(((0, 0), (0, 1), (0, 2))):
+        later(*spot, up_tile, i)
+    for i, spot in enumerate(((0, 7), (1, 0), (1, 1))):
+        later(*spot, down_tile, i)
+    if asides:
+        later(0, 2, asides[0].start)
+        later(1, 1, asides[1].start)
+        spots = (((1, 2), (1, 7), (2, 0), (2, 1)), ((2, 2), (2, 3), (2, 4), (2, 5)))
+        for aside, places in zip(asides, spots):
+            for i in range(aside.total):
+                later(*places[min(i, 3)], aside.fold, aside.total - 1 - i)
+    for frame in range(frames):
+        later(2, 6 + min(frame, 1), extra, frame)
+
     tally[...] = jnp.zeros_like(tally)
     grad_keys[...] = jnp.zeros_like(grad_keys)
     grad_values[...] = jnp.zeros_like(grad_values)
@@ -1024,13 +1325,21 @@
             @pl.when(slot < slots)
             def _():
                 def begin(item, inner_carry):
-                    side, rows = where_of(slot, item)
+                    rows = where_of(slot, item)[1]
                     free(slot, item)
-                    stage[side, rows] = own_part(slot, rows)
+                    stage[rows] = own_part(slot, rows)
                     send_in(slot, item)
                     return inner_carry
 
                 lax.fori_loop(0, chunks, begin, 0)
+
+            for late_slot in sorted({spot[0] for spot in late}):
+
+                @pl.when(slot == late_slot)
+                def _():
+                    for late_chunk in range(MIDDLE_LAG):
+                        for work in late.get((late_slot, late_chunk), ()):
+                            work()
 
             @pl.when(slot > 0)
             def _():
@@ -1060,9 +1369,16 @@
             def _():
                 for piece in range(6 if which == 1 else 4):
 
-                    @pl.when(chunk == MIDDLE_LAG + piece)
+                    @pl.when(chunk == jnp.minimum(MIDDLE_LAG + piece, chunks - 1))
                     def _():
                         work(piece, stream, rows)
+
+        for (late_slot, late_chunk), works in late.items():
+
+            @pl.when((slot == late_slot) & (chunk == late_chunk) & (inside | (late_chunk >= MIDDLE_LAG)))
+            def _():
+                for work in works:
+                    work()
 
         return carry
 
@@ -1072,16 +1388,21 @@
         sent(lax.div(number, chunks), lax.rem(number, chunks))
         return carry
 
-    lax.fori_loop((slots - 2 * frames) * chunks, slots * chunks, settle, 0)
+    lax.fori_loop((slots - frames) * chunks, slots * chunks, settle, 0)
     sums_ref[...] = jnp.zeros_like(sums_ref)
     for i in range(4):
         sums_ref[i : i + 1] = jnp.sum(tally[i], axis=0, keepdims=True)
-
-
-def call_middle(count, frames, first, base, cotangent, rows, bias, keys, values, query_w, out_w, up_w, down_w):
+    for aside, result in zip(asides, (up_result, down_result)):
+        aside.finish([result])
+
+
+def call_middle(
+    count, groups, frames_axis, frames, first, base, cotangent, rows, bias, keys, values, query_w, out_w, up_w, down_w
+):
     tokens, features = first.shape
     local, hidden = query_w.shape[0], up_w.shape[1]
     chunks = tokens // frames // MIDDLE_ROWS
+    scattered = can_scatter(groups, frames_axis, features)
 
     def wide(*shape):
         return jax.ShapeDtypeStruct(shape, WIDE)
@@ -1089,22 +1410,25 @@
     def narrow(*shape):
         return jax.ShapeDtypeStruct(shape, NARROW)
 
+    found, scratch = Products.shapes(groups, frames_axis, [hidden], features)
+    scratch = scratch[:1] * 2 + scratch[1:] * 2
     results = (
         [wide(tokens, features)] * 2
-        + [narrow(tokens, features)] * 5
-        + [narrow(tokens, hidden)] * 2
+        + [narrow(tokens, features)] * 3
         + [narrow(tokens, local)] * 2
         + [wide(*keys.shape)] * 2
-        + [wide(8, features)]
+        + [wide(8, features), narrow(tokens, features)]
+        + found * 2
     )
     sem = pltpu.SemaphoreType.DMA((STAGES * frames, chunks))
     return pl.pallas_call(
-        functools.partial(middle_kernel, count, frames),
+        functools.partial(middle_kernel, count, groups, frames_axis, frames, scattered),
         out_shape=tuple(results),
         in_specs=vmem(11),
         out_specs=tuple(vmem(len(results))),
-        scratch_shapes=[
-            pltpu.VMEM((tokens, features), WIDE),
+        scratch_shapes=[pltpu.VMEM((tokens, features), NARROW)] * 2
+        + [pltpu.VMEM((tokens, hidden), NARROW)] * 2
+        + [
             pltpu.VMEM((tokens, features), WIDE),
             pltpu.VMEM((tokens, features), NARROW),
             pltpu.VMEM((tokens, local), NARROW),
@@ -1113,107 +1437,364 @@
             pltpu.VMEM((tokens // frames, local), WIDE),
             pltpu.VMEM((4, 8, features), WIDE),
         ]
-        + [pltpu.VMEM((2, tokens, features), NARROW)] * 4
-        + [sem] * 5,
+        + [pltpu.VMEM((tokens, features), NARROW)] * 3
+        + [pltpu.VMEM((2, tokens, features), NARROW)]
+        + [sem] * 5
+        + scratch,
         compiler_params=pltpu.CompilerParams(
-            collective_id=7, has_side_effects=True, vmem_limit_bytes=60 * 2**20
+            collective_id=7, has_side_effects=True, vmem_limit_bytes=62 * 2**20
         ),
         name="middle",
     )(first, base, cotangent, rows, bias, keys, values, query_w, out_w, up_w, down_w)
 
 
-def attend_scores(query, keys, key_valid):
-    raw_scores = HD ** (-0.5) * jnp.einsum("fphe,fqhe->fhpq", query, keys, preferred_element_type=WIDE)
-    if key_valid is None:
-        return raw_scores
-    return jnp.where(key_valid[:, None, None, :], raw_scores, NEGATIVE)
-
-
-def attend_forward(query, keys, values, key_valid):
-    scores = attend_scores(query, keys, key_valid)
-    row_max = jnp.max(scores, axis=-1, keepdims=True)
-    shifted = jnp.exp(scores - row_max)
-    row_total = jnp.sum(shifted, axis=-1, keepdims=True)
-    probs_low = (shifted / row_total).astype(NARROW)
+def greet_frames(here, frames_axis):
+    found = (here > 0).astype(jnp.int32) + (here < frames_axis - 1).astype(jnp.int32)
+    barrier = pltpu.get_barrier_semaphore()
+
+    @pl.when(here > 0)
+    def _():
+        pl.semaphore_signal(barrier, inc=1, device_id={FRAME: here - 1}, device_id_type=MESH)
+
+    @pl.when(here < frames_axis - 1)
+    def _():
+        pl.semaphore_signal(barrier, inc=1, device_id={FRAME: here + 1}, device_id_type=MESH)
+
+    return found
+
+
+def head_columns(local):
+    feature = lax.broadcasted_iota(jnp.int32, (local, 128), 0)
+    first = lax.broadcasted_iota(jnp.int32, (local, 128), 1) * HD
+    return jnp.where((feature >= first) & (feature < first + HD), 1.0, 0.0).astype(NARROW)
+
+
+def per_head(values, columns):
+    high, rest = split_pair(values)
+    return dot(high, columns, 1, 0) + dot(rest, columns, 1, 0)
+
+
+def over_features(values, columns):
+    high, rest = split_pair(values)
+    return dot(high, columns, 1, 1) + dot(rest, columns, 1, 1)
+
+
+def window_probs(query, keys_of, bias_of, columns):
+    scores = [
+        HD ** (-0.5) * per_head(query * keys_of(offset), columns) + bias_of(offset) for offset in range(WIN)
+    ]
+    highest = functools.reduce(jnp.maximum, scores)
+    raised = [jnp.exp(item - highest) for item in scores]
+    whole = 1.0 / sum(raised[1:], raised[0])
+    return [item * whole for item in raised]
+
+
+def temporal_forward_kernel(
+    count, frames_axis, frames, hidden_ref, in_ref, out_ref, bias_ref, cotangent_ref, text_ref,
+    query_ref, keys_ref, values_ref, heads_ref, part_ref, cotangent_full, text_full,
+    halo_send, halo_recv, *sems,
+):
+    place, here = lax.axis_index(LINE), lax.axis_index(FRAME)
+    patches = hidden_ref.shape[0] // frames
+    local = heads_ref.shape[1]
+    share = cotangent_ref.shape[1]
+    last = count - 1
+    greet_line(place, count, greet_frames(here, frames_axis))
+    cells = (keys_ref, values_ref)
+
+    def shares(owner):
+        return cotangent_full.at[:, pl.ds(pl.multiple_of(owner * share, share), share)]
+
+    moving = [
+        LineGather(count, place, shares, sems[0:3]),
+        LineGather(count, place, lambda owner: text_full.at[owner], sems[3:6]),
+    ]
+    cotangent_full[:, pl.ds(pl.multiple_of(place * share, share), share)] = cotangent_ref[...]
+    text_full[place] = text_ref[...]
+    for item in moving:
+        item.start()
+
+    def halo(which, item):
+        source = 2 + (frames - 2 + which if which < 2 else 0)
+        target = which if which < 2 else frames + 2
+        to = here + 1 if which < 2 else here - 1
+        ref = cells[item]
+        return remote(
+            ref.at[source], ref.at[target], halo_send.at[which, item], halo_recv.at[which, item], {FRAME: to}
+        )
+
+    has_next, has_previous = here < frames_axis - 1, here > 0
+
+    def frame_rows(frame):
+        return slice(frame * patches, (frame + 1) * patches)
+
+    for frame in range(frames):
+        for item in range(2):
+            rows = slice((1 + item) * local, (2 + item) * local)
+            cells[item][2 + frame] = dot(hidden_ref[frame_rows(frame)], in_ref[rows], 1, 1).astype(NARROW)
+            for which in range(3):
+                if (frames - 2 + which if which < 2 else 0) == frame:
+
+                    @pl.when(has_next if which < 2 else has_previous)
+                    def _():
+                        halo(which, item).start()
+
+    query_ref[...] = dot(hidden_ref[...], in_ref[0:local], 1, 1).astype(NARROW)
+    for distance in range(1, last):
+        for item in moving:
+            item.arrive(distance)
+    for item in range(2):
+
+        @pl.when(has_previous)
+        def _():
+            halo(0, item).wait_recv()
+            halo(1, item).wait_recv()
+
+        @pl.when(jnp.logical_not(has_previous))
+        def _():
+            cells[item][0:2] = jnp.zeros((2,) + cells[item].shape[1:], NARROW)
+
+        @pl.when(has_next)
+        def _():
+            halo(2, item).wait_recv()
+
+        @pl.when(jnp.logical_not(has_next))
+        def _():
+            cells[item][frames + 2] = jnp.zeros(cells[item].shape[1:], NARROW)
+
+    columns = head_columns(local)
+    for frame in range(frames):
+        probs = window_probs(
+            query_ref[frame_rows(frame)].astype(WIDE),
+            lambda offset: keys_ref[frame + offset].astype(WIDE),
+            lambda offset: bias_ref[frame * WIN + offset : frame * WIN + offset + 1],
+            columns,
+        )
+        mixed = over_features(probs[0], columns) * values_ref[frame].astype(WIDE)
+        for offset in range(1, WIN):
+            mixed = mixed + over_features(probs[offset], columns) * values_ref[frame + offset].astype(WIDE)
+        heads_ref[frame_rows(frame)] = mixed.astype(NARROW)
+        part_ref[frame_rows(frame)] = dot(mixed.astype(NARROW), out_ref[...], 1, 0).astype(NARROW)
+    for item in moving:
+        item.arrive(last)
+        item.settle()
+    for item in range(2):
+
+        @pl.when(has_next)
+        def _():
+            halo(0, item).wait_send()
+            halo(1, item).wait_send()
+
+        @pl.when(has_previous)
+        def _():
+            halo(2, item).wait_send()
+
+
+def call_temporal_forward(count, frames_axis, hidden, in_w, out_w, bias, cotangent, text):
+    tokens, features = hidden.shape
+    frames, share = cotangent.shape[:2]
+    local = out_w.shape[0]
+    patches = tokens // frames
+
+    def narrow(*shape):
+        return jax.ShapeDtypeStruct(shape, NARROW)
+
+    results = (
+        [narrow(tokens, local)]
+        + [narrow(frames + 3, patches, local)] * 2
+        + [narrow(tokens, local), narrow(tokens, features)]
+        + [narrow(frames, share * count, features), narrow(count, *text.shape)]
+    )
+    return pl.pallas_call(
+        functools.partial(temporal_forward_kernel, count, frames_axis, frames),
+        out_shape=tuple(results),
+        in_specs=vmem(6),
+        out_specs=tuple(vmem(len(results))),
+        scratch_shapes=[pltpu.SemaphoreType.DMA((3, 2))] * 2 + gather_sems(count) * 2,
+        compiler_params=pltpu.CompilerParams(
+            collective_id=8, has_side_effects=True, vmem_limit_bytes=VMEM_LIMIT
+        ),
+        name="temporal_forward",
+    )(hidden, in_w, out_w, bias, cotangent, text)
+
+
+def temporal_backward_kernel(
+    count, groups, frames_axis, frames, scattered,
+    grad_ref, in_ref, out_ref, bias_ref, query_ref, keys_ref, values_ref,
+    extra_ref, text_keys, text_values, text_w, text_rows, cross_hidden, cross_grad, cross_low, cross_heads,
+    grad_packed, part_ref, extra_own, text_own, query_result, keyval_result, out_result,
+    near_keys, near_values, rim_out, rim_in, halo_send, halo_recv, text_ref, text_low,
+    extra_land, extra_stage, text_land, text_stage, *sems,
+):
+    products = Products(
+        groups, frames_axis, [(cross_hidden, cross_grad), (text_rows, text_low), (cross_low, cross_heads)],
+        [query_result, keyval_result, out_result], sems[8:], scattered,
+    )
+    place, here = lax.axis_index(LINE), lax.axis_index(FRAME)
+    patches = grad_ref.shape[0] // frames
+    local = out_ref.shape[0]
+    share = extra_own.shape[1]
+    last = count - 1
+    greet_line(place, count, greet_frames(here, frames_axis), products.partners())
+
+    def shares(owner, frame):
+        return extra_ref[frame, pl.ds(pl.multiple_of(owner * share, share), share)]
+
+    moving = [
+        LineScatter(count, place, frames, shares, extra_land, extra_stage, sems[0:4]),
+        LineScatter(count, place, 1, lambda owner, piece: text_ref[owner], text_land, text_stage, sems[4:8]),
+    ]
+    moving[0].relay_both(last)
+    near = (near_keys, near_values)
+    slots = text_low.shape[0]
+    text_parts = jnp.zeros((slots, grad_ref.shape[1]), WIDE)
+    for item, (source, factor) in enumerate(((text_keys, HD ** (-0.5)), (text_values, 1.0))):
+        low = (factor * collect_heads(source[...], slots)).astype(NARROW)
+        text_low[:, item * local : (item + 1) * local] = low
+        text_parts = text_parts + dot(low, text_w[item * local : (item + 1) * local], 1, 0)
+    text_parts = text_parts.astype(NARROW)
+    for owner in range(count):
+        text_ref[owner] = text_parts[:, owner * local : (owner + 1) * local]
+    moving[1].relay_both(last)
+
+
+    def halo(which):
+        to = here - 1 if which < 2 else here + 1
+        return remote(
+            rim_out.at[which], rim_in.at[which], halo_send.at[which], halo_recv.at[which], {FRAME: to}
+        )
+
+    has_next, has_previous = here < frames_axis - 1, here > 0
+
+    def frame_rows(frame):
+        return slice(frame * patches, (frame + 1) * patches)
+
+    columns = head_columns(local)
+    seen = set()
+
+    def add(item, cell, terms):
+        if (item, cell) in seen:
+            near[item][cell] += terms
+        else:
+            near[item][cell] = terms
+        seen.add((item, cell))
+
+    for frame in range(frames):
+        given = dot(grad_ref[frame_rows(frame)], out_ref[...], 1, 1).astype(NARROW).astype(WIDE)
+        asked = query_ref[frame_rows(frame)].astype(WIDE)
+        probs = window_probs(
+            asked,
+            lambda offset: keys_ref[frame + offset].astype(WIDE),
+            lambda offset: bias_ref[frame * WIN + offset : frame * WIN + offset + 1],
+            columns,
+        )
+        pulled = [per_head(given * values_ref[frame + offset].astype(WIDE), columns) for offset in range(WIN)]
+        shared = sum((probs[i] * pulled[i] for i in range(1, WIN)), probs[0] * pulled[0])
+        found = jnp.zeros((patches, local), WIDE)
+        for offset in range(WIN):
+            scores = HD ** (-0.5) * over_features(probs[offset] * (pulled[offset] - shared), columns)
+            found = found + scores * keys_ref[frame + offset].astype(WIDE)
+            add(0, frame + offset, scores * asked)
+            add(1, frame + offset, over_features(probs[offset], columns) * given)
+        grad_packed[frame_rows(frame), 0:local] = found.astype(NARROW)
+
+    for which in range(3):
+
+        @pl.when(has_previous if which < 2 else has_next)
+        def _():
+            for item in range(2):
+                span = slice(item * local, (item + 1) * local)
+                rim_out[which, :, span] = near[item][which if which < 2 else frames + 2].astype(NARROW)
+            halo(which).start()
+
+    folds = fold_works(products)
+    for work in products.work():
+        work()
+    for distance in range(last - 1, 0, -1):
+        for item in moving:
+            item.relay_both(distance)
+        for work in folds if distance == last - 1 else ():
+            work()
+
+    for which in range(3):
+
+        @pl.when(has_next if which < 2 else has_previous)
+        def _():
+            halo(which).wait_recv()
+            for item in range(2):
+                span = slice(item * local, (item + 1) * local)
+                near[item][2 + (frames - 2 + which if which < 2 else 0)] += rim_in[which, :, span].astype(WIDE)
+
+    for frame in range(frames):
+        rows = frame_rows(frame)
+        parts = dot(grad_packed[rows, 0:local], in_ref[0:local], 1, 0)
+        for item in range(2):
+            values = near[item][2 + frame].astype(NARROW)
+            grad_packed[rows, (1 + item) * local : (2 + item) * local] = values
+            parts = parts + dot(values, in_ref[(1 + item) * local : (2 + item) * local], 1, 0)
+        part_ref[rows] = parts.astype(NARROW)
+
+    for frame in range(frames):
+        extra_own[frame] = moving[0].total(frame)
+    text_own[...] = moving[1].total(0).astype(NARROW)
+    for item in moving:
+        item.settle()
+    for which in range(3):
+
+        @pl.when(has_previous if which < 2 else has_next)
+        def _():
+            halo(which).wait_send()
+
+    products.finish()
+
+
+def call_temporal_backward(
+    count, groups, frames_axis, grad, in_w, out_w, bias, query, keys, values, extra, text_keys, text_values, text_w,
+    text_rows, *cross_pairs,
+):
+    tokens, features = grad.shape
+    frames, patches = extra.shape[:2]
+    local = out_w.shape[0]
+    share = patches // count
+    slots = text_rows.shape[0]
+
+    def narrow(*shape):
+        return jax.ShapeDtypeStruct(shape, NARROW)
+
+    found, scratch = Products.shapes(groups, frames_axis, [local, 2 * local, local], features)
+    results = (
+        [narrow(tokens, 3 * local)]
+        + [narrow(tokens, features), jax.ShapeDtypeStruct((frames, share, features), WIDE)]
+        + [narrow(slots, local)]
+        + found
+    )
+    return pl.pallas_call(
+        functools.partial(temporal_backward_kernel, count, groups, frames_axis, frames, bool(scratch)),
+        out_shape=tuple(results),
+        in_specs=vmem(16),
+        out_specs=tuple(vmem(len(results))),
+        scratch_shapes=[pltpu.VMEM((frames + 3, patches, local), WIDE)] * 2
+        + [pltpu.VMEM((3, patches, 2 * local), NARROW)] * 2
+        + [pltpu.SemaphoreType.DMA((3,))] * 2
+        + [pltpu.VMEM((count, slots, local), NARROW), pltpu.VMEM((slots, 2 * local), NARROW)]
+        + [pltpu.VMEM((2, count, frames, share, features), NARROW)] * 2
+        + [pltpu.VMEM((2, count, 1, slots, local), NARROW)] * 2
+        + scatter_sems(count, frames)
+        + scatter_sems(count, 1)
+        + scratch,
+        compiler_params=pltpu.CompilerParams(
+            collective_id=9, has_side_effects=True, vmem_limit_bytes=VMEM_LIMIT
+        ),
+        name="temporal_backward",
+    )(grad, in_w, out_w, bias, query, keys, values, extra, text_keys, text_values, text_w, text_rows, *cross_pairs)
+
+
+def attend_forward(query, keys, values):
+    scores = HD ** (-0.5) * jnp.einsum("fphe,fqhe->fhpq", query, keys, preferred_element_type=WIDE)
+    shifted = jnp.exp(scores - jnp.max(scores, axis=-1, keepdims=True))
+    probs_low = (shifted / jnp.sum(shifted, axis=-1, keepdims=True)).astype(NARROW)
     heads_out = jnp.einsum("fhpq,fqhe->fphe", probs_low, values, preferred_element_type=WIDE)
-    return (heads_out.astype(NARROW), row_max + jnp.log(row_total))
-
-
-def attend_backward(query, keys, values, key_valid, log_total, grad_out):
-    probs = jnp.exp(attend_scores(query, keys, key_valid) - log_total)
-    grad_probs = jnp.einsum("fphe,fqhe->fhpq", grad_out, values, preferred_element_type=WIDE)
-    grad_values = jnp.einsum("fhpq,fphe->fqhe", probs.astype(NARROW), grad_out, preferred_element_type=WIDE)
-    grad_scores = probs * (grad_probs - jnp.sum(grad_probs * probs, axis=-1, keepdims=True))
-    grad_scores = grad_scores.astype(NARROW)
-    grad_query = HD ** (-0.5) * jnp.einsum("fhpq,fqhe->fphe", grad_scores, keys, preferred_element_type=WIDE)
-    grad_keys = HD ** (-0.5) * jnp.einsum("fhpq,fphe->fqhe", grad_scores, query, preferred_element_type=WIDE)
-    return (grad_query, grad_keys, grad_values)
-
-
-def over_heads(first, second):
-    return jnp.einsum("fphe,fphe->fhp", first, second, precision=HIGHEST, preferred_element_type=WIDE)
-
-
-def by_heads(weights, values):
-    return jnp.einsum("fhp,fphe->fphe", weights, values, precision=HIGHEST)
-
-
-def temporal_weights(query, keys, allowed, frames):
-    score_list = []
-    for offset in range(WIN):
-        raw_scores = HD ** (-0.5) * jnp.einsum(
-            "fphe,fphe->fhp", query, keys[offset : offset + frames], preferred_element_type=WIDE
-        )
-        score_list.append(jnp.where(allowed[offset][:, None, None], raw_scores, NEGATIVE))
-    scores = jnp.stack(score_list)
-    shifted = jnp.exp(scores - jnp.max(scores, axis=0, keepdims=True))
-    return shifted / jnp.sum(shifted, axis=0, keepdims=True)
-
-
-def temporal_mix(probs, values, frames):
-    values_wide = values.astype(WIDE)
-    mixed = by_heads(probs[0], values_wide[0:frames])
-    for offset in range(1, WIN):
-        mixed = mixed + by_heads(probs[offset], values_wide[offset : offset + frames])
-    return mixed
-
-
-def temporal_backward(query, keys, values, probs, grad_out, frames):
-    query_wide, keys_wide = query.astype(WIDE), keys.astype(WIDE)
-    values_wide, grad_wide = values.astype(WIDE), grad_out.astype(WIDE)
-    grad_probs = jnp.stack(
-        [over_heads(grad_wide, values_wide[offset : offset + frames]) for offset in range(WIN)]
-    )
-    grad_scores = probs * (grad_probs - jnp.sum(grad_probs * probs, axis=0, keepdims=True))
-    grad_query = jnp.zeros(query.shape, WIDE)
-    for offset in range(WIN):
-        grad_query = grad_query + HD ** (-0.5) * by_heads(
-            grad_scores[offset], keys_wide[offset : offset + frames]
-        )
-
-    def near_sums(weights, sources):
-        found = []
-        for cell in range(frames + WIN - 1):
-            terms = [
-                by_heads(weights[offset][cell - offset : cell - offset + 1], sources[cell - offset : cell - offset + 1])
-                for offset in range(WIN)
-                if 0 <= cell - offset < frames
-            ]
-            found.append(sum(terms[1:], terms[0]))
-        return found
-
-    grad_keys = near_sums(HD ** (-0.5) * grad_scores, query_wide)
-    return (grad_query, grad_keys, near_sums(probs, grad_wide))
-
-
-def to_next(cells):
-    ends = lax.axis_size(FRAME) - 1
-    return lax.ppermute(cells, FRAME, [(i, i + 1) for i in range(ends)])
-
-
-def to_previous(cells):
-    ends = lax.axis_size(FRAME) - 1
-    return lax.ppermute(cells, FRAME, [(i + 1, i) for i in range(ends)])
+    return heads_out.astype(NARROW)
 
 
 def sum_matrix_grads(pieces):
@@ -1270,7 +1851,6 @@
     )
     base_zero, spatial_hidden = flat(base_grid), flat(normed_grid)
     text_part = dot(caption_here, caption_proj, 1, 0).astype(NARROW)
-    text_rows = lax.all_gather(text_part, LINE, axis=1, tiled=True)
 
     def rows_of(*rows):
         filled = [jnp.zeros((features,), WIDE)] * (8 - len(rows))
@@ -1280,7 +1860,7 @@
     spatial_query, spatial_keys, spatial_values = (
         heads(spatial_packed[:, i * local : (i + 1) * local]) for i in range(3)
     )
-    spatial_heads, spatial_logs = attend_forward(spatial_query, spatial_keys, spatial_values, None)
+    spatial_heads = attend_forward(spatial_query, spatial_keys, spatial_values)
     spatial_flat = flat(spatial_heads)
     spatial_out, base_one, temporal_hidden = call_forward(
         count,
@@ -1289,17 +1869,6 @@
         rows_of(mods[2], 1.0 + mods[4], mods[3]),
     )
 
-    cotangent_here, temporal_hidden = lax.optimization_barrier((cotangent[0], temporal_hidden))
-    cotangent_full = flat(lax.all_gather(cotangent_here, LINE, axis=1, tiled=True))
-
-    temporal_packed = dot(temporal_hidden, temporal_in, 1, 1).astype(NARROW)
-    temporal_query = heads(temporal_packed[:, 0:local])
-    own_pair = grid(temporal_packed[:, local:])
-    near = jnp.concatenate(
-        [to_next(own_pair[frames - 2 :]), own_pair, to_previous(own_pair[0:1])], axis=0
-    )
-    temporal_keys = split_heads(near[:, :, 0:local])
-    temporal_values = split_heads(near[:, :, local:])
     first_frame = lax.axis_index(FRAME) * frames
     clip_near = lax.dynamic_slice_in_dim(
         jnp.pad(clip_ids[0], (2, 2), constant_values=-1), first_frame, frames + 4
@@ -1310,99 +1879,64 @@
             (clip_near[offset : offset + frames] == own_clip)
             & ((window_mask[0][:, offset] == 1) | (offset == 2))
             for offset in range(WIN)
-        ]
-    )
-    temporal_probs = temporal_weights(temporal_query, temporal_keys, allowed, frames)
-    temporal_flat = flat(temporal_mix(temporal_probs, temporal_values, frames).astype(NARROW))
+        ],
+        axis=1,
+    )
+    window_bias = jnp.broadcast_to(jnp.where(allowed, 0.0, NEGATIVE).reshape(-1, 1), (frames * WIN, 128))
+    (
+        temporal_query, temporal_keys, temporal_values, temporal_flat, temporal_part, cotangent_full, text_full,
+    ) = call_temporal_forward(
+        count, frames_axis, temporal_hidden, temporal_in, temporal_outproj, window_bias, cotangent[0], text_part
+    )
+    cotangent_full = flat(cotangent_full)
+    text_rows = jnp.transpose(text_full, (1, 0, 2)).reshape(slots, features)
+
+    slot_pad = -slots % 128
+    text_rows = jnp.pad(text_rows, ((0, slot_pad), (0, 0)))
     text_packed = dot(text_rows, keyval_in, 1, 1).astype(NARROW)
-    slot_pad = -slots % 128
     slot_index = jnp.arange(slots)
     key_valid = (own_clip[:, None] == (slot_index // text_length)[None, :]) & (
         slot_index % text_length < jnp.repeat(text_counts[0], text_length)
     )[None, :]
     bias = jnp.pad(jnp.where(key_valid, 0.0, NEGATIVE), ((0, 0), (0, slot_pad)), constant_values=NEGATIVE)
     bias = jnp.broadcast_to(bias[:, None], (frames, 8, slots + slot_pad))
-    head_mask = (jnp.arange(local) // HD)[None, :] == jnp.arange(local // HD)[:, None]
+    mask_of_head = (jnp.arange(local) // HD)[None, :] == jnp.arange(local // HD)[:, None]
 
     def by_head(values):
-        padded = jnp.pad(values, ((0, slot_pad), (0, 0)))
-        return jnp.where(head_mask[:, None], padded[None], 0).reshape(-1, local)
-
-    def from_heads(values):
-        kept = jnp.where(head_mask[:, None], values.reshape(local // HD, -1, local), 0.0)
-        return jnp.sum(kept, axis=0)[0:slots]
+        return jnp.where(mask_of_head[:, None], values[None], 0).reshape(-1, local)
 
     (
-        base_three, grad_two, grad_temporal_low, grad_cross_low, grad_mlp_low, cross_hidden, mlp_hidden,
-        mlp_low, grad_inner, cross_flat, grad_cross_packed, text_grad_keys, text_grad_values, sums_middle,
+        base_three, grad_two, grad_temporal_low, grad_cross_low, cross_hidden, cross_flat, grad_cross_packed,
+        text_grad_keys, text_grad_values, sums_middle, mlp_part, grad_up, grad_down,
     ) = call_middle(
-        count, frames, dot(temporal_flat, temporal_outproj, 1, 0).astype(NARROW), base_one, cotangent_full,
+        count, groups, frames_axis, frames, temporal_part, base_one, cotangent_full,
         rows_of(mods[5], cross_gain.astype(WIDE), 1.0 + mods[7], mods[6], mods[8]), bias,
         by_head(text_packed[:, :local]), by_head(text_packed[:, local:]),
         query_in, cross_outproj, mlp_up, mlp_down,
     )
 
-    inside = can_scatter(groups, frames_axis, features)
-
-    def matrix_grad(first, second):
-        return dot(first, second, 0, 0).astype(NARROW)
-
-    mlp_part = dot(mlp_low, mlp_down, 1, 0).astype(NARROW)
-    mlp_out = lax.psum_scatter(grid(mlp_part), LINE, scatter_dimension=1, tiled=True).astype(WIDE)
+    def summed(found):
+        return found if can_scatter(groups, frames_axis, features) else sum_matrix_grads(found)
+
+    grad_up, grad_down = summed([grad_up, grad_down])
+
+    grad_temporal_packed, temporal_grad_part, mlp_out, text_grad, *found = call_temporal_backward(
+        count, groups, frames_axis, grad_temporal_low, temporal_in, temporal_outproj, window_bias,
+        temporal_query, temporal_keys, temporal_values, grid(mlp_part), text_grad_keys, text_grad_values,
+        keyval_in, text_rows, cross_hidden, grad_cross_packed, grad_cross_low, cross_flat,
+    )
+    grad_query_cross, grad_keyval_cross, grad_outproj_cross = summed(found)
     output = (own(base_three) + mods[8] * mlp_out).astype(NARROW)[None]
     gate_mlp_part = jnp.sum(cotangent[0].astype(WIDE) * mlp_out, axis=(0, 1))
-    grad_text_packed = jnp.concatenate(
-        [HD ** (-0.5) * from_heads(text_grad_keys), from_heads(text_grad_values)], axis=1
-    )
-    text_high, text_rest = split_pair(grad_text_packed)
-    grad_keyval_part = dot(text_rows, text_high, 0, 0) + dot(text_rows, text_rest, 0, 0)
-    text_grad_part = dot(text_high, keyval_in, 1, 0) + dot(text_rest, keyval_in, 1, 0)
-    text_grad = lax.psum_scatter(text_grad_part.astype(NARROW), LINE, scatter_dimension=1, tiled=True)
-    text_grad_all = lax.all_gather(text_grad, BOTH).reshape(groups, frames_axis, slots, local)
-    text_grad_wide = jnp.sum(text_grad_all.astype(WIDE), axis=1).reshape(groups * slots, local)
-    text_all_high, text_all_rest = split_pair(text_grad_wide)
+    grad_one, grad_spatial_low, sums_temporal, text_grad_all, *found = call_backward(
+        count, groups, frames_axis, temporal_grad_part, base_one, grad_two, spatial_out,
+        rows_of(1.0 + mods[4], mods[2]), text_grad,
+        [(temporal_hidden, grad_temporal_packed), (grad_temporal_low, temporal_flat)],
+    )
+    grad_inproj_temporal, grad_outproj_temporal = summed(found)
     caption_rows = caption_share.reshape(groups * slots, -1)
-    grad_caption = dot(caption_rows, text_all_high, 0, 0) + dot(caption_rows, text_all_rest, 0, 0)
-
-    grad_temporal_heads = dot(grad_temporal_low, temporal_outproj, 1, 1).astype(NARROW)
-    temporal_grad_query, near_grad_keys, near_grad_values = temporal_backward(
-        temporal_query, temporal_keys, temporal_values, temporal_probs, heads(grad_temporal_heads), frames
-    )
-
-    def joined(first, last):
-        return jnp.concatenate(
-            [
-                jnp.concatenate([part[cell].reshape(1, patches, local) for cell in range(first, last)], axis=0)
-                for part in (near_grad_keys, near_grad_values)
-            ],
-            axis=2,
-        )
-
-    from_next = to_previous(joined(0, 2).astype(NARROW)).astype(WIDE)
-    from_previous = to_next(joined(frames + 2, frames + 3).astype(NARROW)).astype(WIDE)
-    own_grads = joined(2, 2 + frames)
-    own_grads = (
-        own_grads
-        + jnp.pad(from_next, ((frames - 2, 0), (0, 0), (0, 0)))
-        + jnp.pad(from_previous, ((0, frames - 1), (0, 0), (0, 0)))
-    )
-    grad_temporal_packed = jnp.concatenate(
-        [flat(temporal_grad_query).astype(NARROW), flat(own_grads).astype(NARROW)], axis=1
-    )
-    early = [matrix_grad(mlp_hidden, grad_inner), matrix_grad(grad_mlp_low, mlp_low)]
-    found = call_backward(
-        count, groups, frames_axis, dot(grad_temporal_packed, temporal_in, 1, 0).astype(NARROW), base_one,
-        grad_two, spatial_out, rows_of(1.0 + mods[4], mods[2]), early if inside else [], 2,
-    )
-    grad_one, grad_spatial_low, sums_temporal = found[:3]
-    grad_up, grad_down = found[3:] if inside else sum_matrix_grads(early)
-
-    grad_spatial_heads = dot(grad_spatial_low, spatial_outproj, 1, 1).astype(NARROW)
-    spatial_grads = attend_backward(
-        spatial_query, spatial_keys, spatial_values, None, spatial_logs, heads(grad_spatial_heads)
-    )
-    grad_spatial_packed = jnp.concatenate([flat(part) for part in spatial_grads], axis=1).astype(NARROW)
-    grad_spatial_part = dot(grad_spatial_packed, spatial_in, 1, 0).astype(NARROW)
+    grad_caption = dot(caption_rows, text_grad_all[:, 0:slots].reshape(groups * slots, local), 0, 0)
+
     side_row = jnp.pad(jnp.concatenate([cond_row, chosen]), (0, features - local - chosen.shape[0]))
     blank = jnp.zeros((features,), WIDE)
     small = jnp.stack(
@@ -1413,23 +1947,11 @@
             sums_middle[1], sums_middle[2], side_row,
         ]
     )
-    late = [
-        matrix_grad(cross_hidden, grad_cross_packed),
-        matrix_grad(grad_cross_low, cross_flat),
-        grad_keyval_part.astype(NARROW),
-        matrix_grad(temporal_hidden, grad_temporal_packed),
-        matrix_grad(grad_temporal_low, temporal_flat),
-        matrix_grad(spatial_hidden, grad_spatial_packed),
-        matrix_grad(grad_spatial_low, spatial_flat),
-    ]
-    found = call_closing(
-        count, groups, frames_axis, grid(grad_spatial_part), grid(base_zero), grid(grad_one), small,
-        rows_of(1.0 + mods[1]), late if inside else [],
-    )
-    grad_latent, small_all = found[:2]
-    late_grads = found[2:] if inside else sum_matrix_grads(late)
-    grad_query_cross, grad_outproj_cross, grad_keyval_cross = late_grads[:3]
-    grad_inproj_temporal, grad_outproj_temporal, grad_inproj_spatial, grad_outproj_spatial = late_grads[3:]
+    grad_latent, small_all, *found = call_closing(
+        count, groups, frames_axis, grad_spatial_low, grid(base_zero), grid(grad_one), small,
+        rows_of(1.0 + mods[1]), spatial_packed, spatial_flat, spatial_hidden, spatial_in, spatial_outproj,
+    )
+    grad_inproj_spatial, grad_outproj_spatial = summed(found)
 
     small_all = small_all.reshape(groups, frames_axis, 16, features)
     small_sums = jnp.sum(small_all, axis=1)

time: 580 us -> 463 us (0.80)
  matrix products: 70.5 us -> 24.9 us
  local copies, waits for them, and re-layouts: 81.6 us -> 39.9 us
  Pallas kernels: 342 us -> 382 us
  other arithmetic: 31.5 us -> 5.35 us
  blocking collectives: 15.6 us -> 0 us
  between operations: 16.3 us -> 2.46 us
  starting transfers between devices: 12.8 us -> 0 us
    pallas_call x1 -> x3, Pallas kernels: 134 us -> 226 us  [the longest x1 150 us: call_middle(): pl.pallas_call(functools.partial(middle_kernel, count, groups, frames_axi...]
    dot_general x25 -> x5, matrix products: 51.4 us -> 10.1 us  [dot(): lax.dot_general(first, second, (((contract_first,), (contract_second,)),...]
    pallas_call x1, Pallas kernels: 76.7 us -> 39.8 us  [call_closing(): pl.pallas_call(functools.partial(closing_kernel, count, groups, frames_ax...]
    pallas_call x1, Pallas kernels: 60.8 us -> 45 us  [call_backward(): pl.pallas_call(functools.partial(backward_kernel, count, groups, frames_a...]
    all_gather x1 -> x0, blocking collectives: 15.6 us -> none  [per_device(): text_rows = lax.all_gather(text_part, LINE, axis=1, tiled=True)]
    convert_element_type x8 -> x2, local copies, waits for them, and re-layouts: 15.2 us -> 0.46 us  [the longest x1 0.31 us: attend_forward(): return heads_out.astype(NARROW)]
    ppermute x4 -> x0, starting transfers between devices: 12.4 us -> none  [the longest x2 9.89 us: to_next(): return lax.ppermute(cells, FRAME, [(i, i + 1) for i in range(ends)])]
    dot_general x5 -> x0, matrix products: 7.72 us -> none  [the longest x1 2.94 us: attend_backward(): jnp.einsum('fhpq,fphe->fqhe', probs.astype(NARROW), grad_out, preferred_e...]
  transfers between devices with their start and end apart: 8 -> 0, of which waited for: 0 -> 0; matrix products, arithmetic and copies ran while one was open for 20% -> 0% of each run, Pallas kernels for 24% -> 0%
where the time goes in v2:
time: 463 us; the launch traced here: 454 us
  Pallas kernels  382 us (83%)
  local copies, waits for them, and re-layouts  39.9 us (9%)
  matrix products  24.9 us (5%)
  other arithmetic  5.35 us (1%)
    pallas_call x1, Pallas kernels, call_middle(): pl.pallas_call(functools.partial(middle_kernel, count, groups, frames_axi...  150 us
    pallas_call x1, Pallas kernels, call_backward(): pl.pallas_call(functools.partial(backward_kernel, count, groups, frames_a...  45 us
    pallas_call x1, Pallas kernels, call_temporal_backward(): pl.pallas_call(functools.partial(temporal_backward_kernel, count, groups,...  43.4 us
    pallas_call x1, Pallas kernels, call_closing(): pl.pallas_call(functools.partial(closing_kernel, count, groups, frames_ax...  39.8 us
    pallas_call x1, Pallas kernels, call_forward(): pl.pallas_call(functools.partial(forward_kernel, count), out_shape=(jax.S...  36.9 us
    pallas_call x1, Pallas kernels, call_opening(): pl.pallas_call(functools.partial(opening_kernel, count, groups, frames_ax...  34.3 us
    pallas_call x1, Pallas kernels, call_temporal_forward(): pl.pallas_call(functools.partial(temporal_forward_kernel, count, frames_a...  32.6 us
    unnamed x116, local copies, waits for them, and re-layouts  29.8 us

profile of v2, /device:TPU:0, one launch (start us, length us, event | category | flops | bytes accessed | tf_op | source)
XLA Modules:
  0.0 454.2 jit_solution(12981116829300780501)
XLA Ops:
  1.3 0.8 multiply_reduce_fusion.2
  2.1 1.5 copy-done.3
  3.7 1.0 copy-done.27
  4.6 34.3 %opening.1 = (f32[2,256,1152]{2,1,0:T(8,128)}, bf16[2,256,1152]{2,1,0:T(8,128)(2,1)S(1)}, f32[16,1152]{1,0:T(8,128)S(1)}, bf16[4,240,512]{2,1,0:T(8,128)(2,1)S(1)}) custom-call(bf16[2,64,1152]{2,1,0:T(8,128)(2,1)S(1)} %bitcast.92, bf16[16,288]{1,0:T(8,128)(2,1)S(1)} %broadcast_in_dim.85.act_ref, bf16[9,288,1152]{2,1,0:T(8,128)(2,1)} %bitcast.97, ...), custom_call_target="tpu_custom_call" | custom-call | tf_op jit(solution)/shard_map/opening/pallas_call | solution.py:1026
  39.0 1.5 convolution_convert_fusion.1.refs_5_
  41.6 2.2 fusion.51
  44.1 2.0 fusion.2
  46.4 0.9 convolution_convert_fusion.part_ref
  47.5 36.9 %forward_sum.1 = (bf16[512,1152]{1,0:T(8,128)(2,1)S(1)}, f32[512,1152]{1,0:T(8,128)S(1)}, bf16[512,1152]{1,0:T(8,128)(2,1)S(1)}) custom-call(bf16[512,1152]{1,0:T(8,128)(2,1)S(1)} %convolution_convert_fusion.part_ref, f32[512,1152]{1,0:T(8,128)} %bitcast.98, f32[8,1152]{1,0:T(8,128)S(1)} %stack.50.rows_ref), custom_call_target="tpu_custom_call" | custom-call | tf_op jit(solution)/shard_map/forward_sum/pallas_call | solution.py:606
  84.3 1.4 copy-done
  85.8 1.0 copy-done.1
  86.8 1.0 copy-done.6
  88.5 3.1 convolution_convert_fusion.4
  91.9 32.6 %temporal_forward.1 = (bf16[512,288]{1,0:T(8,128)(2,1)S(1)}, bf16[5,256,288]{2,1,0:T(8,128)(2,1)S(1)}, bf16[5,256,288]{2,1,0:T(8,128)(2,1)S(1)}, bf16[512,288]{1...) custom-call(bf16[512,1152]{1,0:T(8,128)(2,1)} %copy-done.1, ...), custom_call_target="tpu_custom_call" | custom-call | tf_op jit(solution)/shard_map/temporal_forward/pallas_call | solution.py:1608
  124.5 1.0 copy-done.7
  125.6 1.1 copy-done.12
  126.6 0.9 copy-done.14
  127.6 0.7 copy-done.21
  128.3 1.1 copy.107
  129.4 1.3 copy.108
  130.8 2.1 convolution_convert_fusion.2
  133.3 1.4 broadcast_select_fusion
  136.3 149.5 %middle.1 = (f32[512,1152]{1,0:T(8,128)}, f32[512,1152]{1,0:T(8,128)}, bf16[512,1152]{1,0:T(8,128)(2,1)}, bf16[512,1152]{1,0:T(8,128)(2,1)}, bf16[512,1152]{1,0:...) custom-call(bf16[512,1152]{1,0:T(8,128)(2,1)} %copy-done.7, ...), custom_call_target="tpu_custom_call" | custom-call | tf_op jit(solution)/shard_map/middle/pallas_call | solution.py:1424
  285.8 1.1 pad.18.text_rows
  287.0 1.2 copy-done.13
  288.1 1.0 copy-done.22
  289.1 1.0 copy-done.23
  290.1 1.0 copy-done.24
  291.1 43.4 %temporal_backward.1 = (bf16[512,864]{1,0:T(8,128)(2,1)S(1)}, bf16[512,1152]{1,0:T(8,128)(2,1)}, f32[2,64,1152]{2,1,0:T(8,128)S(1)}, bf16[256,288]{1,0:T(8,128)(...) custom-call(bf16[512,1152]{1,0:T(8,128)(2,1)} %get-tuple-element.68.grad_ref.refs_8_, ...), custom_call_target="tpu_custom_call" | custom-call | tf_op jit(solution)/shard_map/temporal_backward/pallas_call | solution.py:1771
  335.3 1.4 copy-done.10
  336.8 45.0 %backward_sum.1 = (f32[512,1152]{1,0:T(8,128)}, bf16[512,1152]{1,0:T(8,128)(2,1)S(1)}, f32[8,1152]{1,0:T(8,128)S(1)}, bf16[4,256,288]{2,1,0:T(8,128)(2,1)S(1)}, ...) custom-call(bf16[512,1152]{1,0:T(8,128)(2,1)S(1)} %copy-done.10, f32[512,1152]{1,0:T(8,128)} %copy-done, ...), custom_call_target="tpu_custom_call" | custom-call | tf_op jit(solution)/shard_map/backward_sum/pallas_call | solution.py:627
  381.8 1.0 copy-done.8
  383.5 0.9 copy-done.38
  384.4 1.9 multiply_reduce_fusion.1
  386.8 1.3 copy-done.5
  388.1 1.3 copy-done.9
  389.3 39.8 %closing.1 = (bf16[2,64,1152]{2,1,0:T(8,128)(2,1)S(1)}, f32[8,16,1152]{2,1,0:T(8,128)S(1)}, f32[144,864]{1,0:T(8,128)S(1)}, f32[144,288]{1,0:T(8,128)S(1)}) custom-call(bf16[512,1152]{1,0:T(8,128)(2,1)S(1)} %copy-done.9, f32[2,256,1152]{2,1,0:T(8,128)} %get-tuple-element.60.refs_1_, f32[2,256,1152]{2,1,0:T(8,128)} %bitcast.104, ...), custom_call_target="tpu_custom_call" | custom-call | tf_op jit(solution)/shard_map/closing/pallas_call | solution.py:825
  429.2 0.8 copy-done.17
  431.5 2.5 fusion.18
  434.0 2.5 convolution_bitcast_fusion
  436.9 0.9 copy.118
  437.7 7.4 %convolution_bitcast_fusion.1 = f32[4,288]{1,0:T(4,128)S(1)} fusion(f32[4,9,1152]{2,0,1:T(4,128)S(1)} %copy_dynamic-update-slice_fusion.2, bf16[288,9,1152]{2,0,1:T(8,128)(2,1)} %param.27), kind=kOutput, calls=%fused_computation.12 | convolution fusion | flops 143327232 | bytes 6142464 | tf_op jit(solution)/shard_map/ckd,gkd->gc/dot_general | solution.py:1968
  445.3 0.8 fusion.21
  446.6 0.9 copy.119
  447.4 1.1 reshape.193
  448.5 0.7 copy.179
  452.0 0.8 copy.184
  452.9 0.8 copy.185
  (148 shorter events, 11.9 us)
Async XLA Ops:
  1.3 0.8 copy-start.48
  2.1 1.5 copy-start.3
  3.7 1.0 copy-start.27
  4.6 34.3 %copy-start.40 = (bf16[1152,3,288]{0,2,1:T(8,128)(2,1)S(1)}, bf16[1152,3,288]{0,2,1:T(8,128)(2,1)}, u32[]{:S(2)}) copy-start(bf16[1152,3,288]{0,2,1:T(8,128)(2,1)} %param.28) | copy-start | bytes 5971972
  39.0 1.5 copy-start.4
  39.0 1.5 copy-start.36
  44.0 2.4 copy-start.15
  46.4 1.0 copy-start.41
  47.3 40.5 %copy-start.50 = (s32[1,4]{1,0:T(1,128)S(1)}, s32[1,4]{1,0:T(1,128)}, u32[]{:S(2)}) copy-start(s32[1,4]{1,0:T(1,128)} %param.23) | copy-start | bytes 52
  47.3 40.6 %copy-start.46 = (s32[1,2,4]{2,1,0:T(2,128)S(1)}, s32[1,2,4]{2,1,0:T(2,128)}, u32[]{:S(2)}) copy-start(s32[1,2,4]{2,1,0:T(2,128)} %param.24) | copy-start | bytes 100
  84.3 1.4 copy-start
  85.8 1.0 copy-start.1
  86.8 1.0 copy-start.6
  88.5 3.3 copy-start.2
  88.5 3.3 copy-start.11
  124.5 1.1 copy-start.7
  125.5 1.1 copy-start.12
  126.6 0.9 copy-start.14
  128.3 4.6 %copy-start.19 = (bf16[512,288]{1,0:T(8,128)(2,1)}, bf16[512,288]{1,0:T(8,128)(2,1)S(1)}, u32[]{:S(2)}) copy-start(bf16[512,288]{1,0:T(8,128)(2,1)S(1)} %get-tuple-element.85.refs_9_) | copy-start | bytes 884740
  130.7 3.9 copy-start.39
  132.9 1.8 copy-start.47
  132.9 2.5 copy-start.51
  286.9 1.2 copy-start.13
  288.1 1.0 copy-start.22
  289.1 1.0 copy-start.23
  290.1 1.0 copy-start.24
  291.1 44.2 %copy-start.20 = (bf16[512,288]{1,0:T(8,128)(2,1)S(1)}, bf16[512,288]{1,0:T(8,128)(2,1)}, u32[]{:S(2)}) copy-start(bf16[512,288]{1,0:T(8,128)(2,1)} %copy-done.19) | copy-start | bytes 884740
  335.3 46.5 %copy-start.25 = (f32[144,576]{1,0:T(8,128)}, f32[144,576]{1,0:T(8,128)S(1)}, u32[]{:S(2)}) copy-start(f32[144,576]{1,0:T(8,128)S(1)} %get-tuple-element.99) | copy-start | bytes 995332
  335.3 46.5 %copy-start.30 = (f32[144,288]{1,0:T(8,128)}, f32[144,288]{1,0:T(8,128)S(1)}, u32[]{:S(2)}) copy-start(f32[144,288]{1,0:T(8,128)S(1)} %get-tuple-element.218) | copy-start | bytes 497668
  335.3 1.5 copy-start.10
  336.8 49.6 %copy-start.45 = (f32[8,1152]{1,0:T(8,128)S(1)}, f32[8,1152]{1,0:T(8,128)}, u32[]{:S(2)}) copy-start(f32[8,1152]{1,0:T(8,128)} %get-tuple-element.89) | copy-start | bytes 110596
  336.8 49.6 %copy-start.49 = (f32[8]{0:T(128)S(1)}, f32[8]{0:T(128)}, u32[]{:S(2)}) copy-start(f32[8]{0:T(128)} %copy-done.48) | copy-start | bytes 100
  381.8 1.0 copy-start.8
  383.5 0.9 copy-start.38
  383.5 3.0 copy-start.42
  383.5 3.3 copy-start.16
  386.8 1.3 copy-start.5
  388.1 1.3 copy-start.9
  429.2 0.8 copy-start.17
  430.6 3.3 copy-start.37
  431.5 5.0 %copy-start.18 = (f32[144,864]{1,0:T(8,128)S(1)}, f32[144,864]{1,0:T(8,128)}, u32[]{:S(2)}) copy-start(f32[144,864]{1,0:T(8,128)} %copy-done.17) | copy-start | bytes 1492996
  445.2 2.3 copy-start.26
  446.1 3.2 copy-start.35
  446.5 3.4 copy-start.33
  446.5 4.1 copy-start.31
  446.5 4.8 %copy-start.29 = (f32[144,288]{1,0:T(8,128)S(1)}, f32[144,288]{1,0:T(8,128)}, u32[]{:S(2)}) copy-start(f32[144,288]{1,0:T(8,128)} %copy-done.28) | copy-start | bytes 497668
  447.4 4.6 %copy-start.44 = (f32[144,1152]{1,0:T(8,128)S(1)}, f32[144,1152]{1,0:T(8,128)}, u32[]{:S(2)}) copy-start(f32[144,1152]{1,0:T(8,128)} %get-tuple-element.221) | copy-start | bytes 1990660
  448.5 4.3 copy-start.43
  (4 other events, 2.8 us)

commit v3 on v2

--- a/solution.py
+++ b/solution.py
@@ -191,39 +191,43 @@
 
 
 class Products:
-    def __init__(self, groups, frames_axis, pairs, results, scratch, scattered):
-        self.pairs, self.results, self.scattered = pairs, results, scattered
-        self.source = scratch[0] if scattered else None
-        self.aside = Scatter(groups, frames_axis, self.source, scratch[1:]) if scattered else None
+    def __init__(self, pairs, result):
+        self.pairs, self.result = pairs, result
 
     def product(self, i):
         first, second = self.pairs[i]
-        found = dot(first[...], second[...], 0, 0).astype(NARROW)
-        if self.scattered:
-            start = sum(item.shape[1] for _, item in self.pairs[:i])
-            self.source[:, start : start + second.shape[1]] = found
-        else:
-            self.results[i][...] = found
+        start = sum(item.shape[1] for _, item in self.pairs[:i])
+        self.result[:, start : start + second.shape[1]] = dot(first[...], second[...], 0, 0).astype(NARROW)
 
     def work(self):
-        found = [functools.partial(self.product, i) for i in range(len(self.pairs))]
-        return found + ([self.aside.start] if self.scattered else [])
+        return [functools.partial(self.product, i) for i in range(len(self.pairs))]
+
+
+class Scatters:
+    def __init__(self, groups, frames_axis, sources, widths, results, scratch):
+        self.items, self.results = [], []
+        for i, source in enumerate(sources):
+            self.items.append(Scatter(groups, frames_axis, source, scratch[8 * i : 8 * i + 8]))
+            self.results.append(results[: len(widths[i])])
+            results = results[len(widths[i]) :]
 
     def partners(self):
-        return self.aside.partners() if self.scattered else []
+        return self.items[0].partners()
+
+    def folds(self, i):
+        item = self.items[i]
+        return [functools.partial(item.fold, item.total - 1 - step) for step in range(item.total)]
 
     def finish(self):
-        if self.scattered:
-            self.aside.finish(self.results)
+        for item, results in zip(self.items, self.results):
+            item.finish(results)
 
     @staticmethod
-    def shapes(groups, frames_axis, columns, features):
-        if not can_scatter(groups, frames_axis, features):
-            return [jax.ShapeDtypeStruct((features, n), NARROW) for n in columns], []
+    def shapes(groups, frames_axis, features, widths):
         block = features // (groups * frames_axis)
-        results = [jax.ShapeDtypeStruct((block, n), WIDE) for n in columns]
-        source = [pltpu.VMEM((features, sum(columns)), NARROW)]
-        return results, source + Scatter.scratch(groups, frames_axis, features, sum(columns))
+        results = [jax.ShapeDtypeStruct((block, n), WIDE) for columns in widths for n in columns]
+        scratch = [Scatter.scratch(groups, frames_axis, features, sum(columns)) for columns in widths]
+        return results, sum(scratch, [])
 
 
 class GroupExchange:
@@ -296,6 +300,52 @@
     return groups % 2 == 0 and width % (16 * groups * frames_axis) == 0
 
 
+def vmem(count):
+    return [pl.BlockSpec(memory_space=pltpu.VMEM)] * count
+
+
+class Fetch:
+    def __init__(self, sources, held, sems):
+        self.copies = [
+            pltpu.make_async_copy(source, target, sems.at[i]) for i, (source, target) in enumerate(zip(sources, held))
+        ]
+        self.waiting = list(range(len(self.copies)))
+        for copy in self.copies:
+            copy.start()
+
+    def __call__(self, *which):
+        for i in which or tuple(self.waiting):
+            self.copies[i].wait()
+            self.waiting.remove(i)
+
+    def again(self, *which):
+        for i in which:
+            self.copies[i].wait()
+
+
+def fetching_call(kernel, operands, out_shape, scratch_shapes, kernel_id, name):
+    many = len(operands)
+
+    def body(*refs):
+        sources, rest = refs[:many], refs[many : -many - 1]
+        held, sems = refs[-many - 1 : -1], refs[-1]
+        kernel(Fetch(sources, held, sems), *held, *rest)
+
+    return pl.pallas_call(
+        body,
+        out_shape=tuple(out_shape),
+        in_specs=[pl.BlockSpec(memory_space=pl.ANY)] * many,
+        out_specs=tuple(vmem(len(out_shape))),
+        scratch_shapes=list(scratch_shapes)
+        + [pltpu.VMEM(item.shape, item.dtype) for item in operands]
+        + [pltpu.SemaphoreType.DMA((many,))],
+        compiler_params=pltpu.CompilerParams(
+            collective_id=kernel_id, has_side_effects=True, vmem_limit_bytes=62 * 2**20
+        ),
+        name=name,
+    )(*operands)
+
+
 class LineGather:
     def __init__(self, count, place, slot_of, sems):
         self.count, self.place, self.last, self.slot_of = count, place, count - 1, slot_of
@@ -537,10 +587,11 @@
 
 
 def forward_kernel(
-    count, part_ref, base_ref, rows_ref, out_ref, next_ref, normed_ref, land, cross, stage, *sems
+    count, fetch, part_ref, base_ref, rows_ref, out_ref, next_ref, normed_ref, land, cross, stage, *sems
 ):
     place = lax.axis_index(LINE)
     greet_line(place, count)
+    fetch()
     gate, gain, shift = (rows_ref[i : i + 1] for i in range(3))
 
     def consume(rows):
@@ -551,24 +602,27 @@
     line_sum(count, place, part_ref, land, cross, stage, out_ref, sems, consume)
 
 
-def fold_works(products):
-    aside = products.aside
-    return [functools.partial(aside.fold, aside.total - 1 - i) for i in range(aside.total)] if aside else []
-
-
-def backward_kernel(count, groups, frames_axis, many, scattered, *refs):
-    part_ref, base_ref, grad_ref, below_ref, rows_ref, text_ref = refs[:6]
-    factors, refs = refs[6 : 6 + 2 * many], refs[6 + 2 * many :]
-    moved_ref, low_ref, sums_ref, text_all = refs[:4]
-    results, refs = refs[4 : 4 + many], refs[4 + many :]
-    total, land, cross, stage, tally = refs[:5]
-    sems, exchange_scratch, scratch = refs[5:10], refs[10:15], refs[15:]
+def backward_kernel(count, groups, frames_axis, widths, fetch, *refs):
+    part_ref, base_ref, grad_ref, below_ref, rows_ref, *refs = refs
+    pairs, refs = [refs[0:2], refs[2:4]], refs[4:]
+    sources, refs = refs[: len(widths) - 1], refs[max(len(widths) - 1, 0) :]
+    moved_ref, low_ref, sums_ref, *refs = refs
+    many = sum(len(columns) for columns in widths)
+    results, refs = refs[:many], refs[many:]
+    product_ref, total, land, cross, stage, tally, *refs = refs
+    sems, scratch = refs[:5], refs[5:]
     place = lax.axis_index(LINE)
-    pairs = list(zip(factors[0::2], factors[1::2]))
-    products = Products(groups, frames_axis, pairs, results, scratch, scattered)
-    exchange = GroupExchange(groups, frames_axis, text_ref, text_all, exchange_scratch)
-    greet_line(place, count, 0, exchange.partners() + products.partners())
-    exchange.start()
+    early = Products(pairs, product_ref).work()
+    scatters = Scatters(
+        groups, frames_axis, [*sources, product_ref] if widths else [], widths, results, scratch
+    )
+    greet_line(place, count, 0, scatters.partners() if widths else ())
+    fetch()
+    folds = []
+    if widths:
+        scatters.items[0].start()
+        early = scatters.folds(0) + early + [scatters.items[-1].start]
+        folds = scatters.folds(len(widths) - 1)
     gain, gate = (rows_ref[i : i + 1] for i in range(2))
     tally[...] = jnp.zeros_like(tally)
 
@@ -581,20 +635,11 @@
         for i, terms in enumerate((grads, grads * normal, moved * below_ref[rows].astype(WIDE))):
             tally[i] += jnp.sum(terms.reshape(-1, 8, terms.shape[-1]), axis=0)
 
-    folds = fold_works(products)
-    line_sum(
-        count, place, part_ref, land, cross, stage, total, sems, consume,
-        products.work(), folds[:1] + [exchange.spread] + folds[1:],
-    )
+    line_sum(count, place, part_ref, land, cross, stage, total, sems, consume, early, folds)
     sums_ref[...] = jnp.zeros_like(sums_ref)
     for i in range(3):
         sums_ref[i : i + 1] = jnp.sum(tally[i], axis=0, keepdims=True)
-    products.finish()
-    exchange.finish()
-
-
-def vmem(count):
-    return [pl.BlockSpec(memory_space=pltpu.VMEM)] * count
+    scatters.finish()
 
 
 def line_sems():
@@ -603,48 +648,43 @@
 
 def call_forward(count, part, base, rows):
     shape = part.shape
-    return pl.pallas_call(
+    return fetching_call(
         functools.partial(forward_kernel, count),
-        out_shape=(
+        [part, base, rows],
+        (
             jax.ShapeDtypeStruct(shape, NARROW),
             jax.ShapeDtypeStruct(shape, WIDE),
             jax.ShapeDtypeStruct(shape, NARROW),
         ),
-        in_specs=vmem(3),
-        out_specs=tuple(vmem(3)),
-        scratch_shapes=[pltpu.VMEM(shape, NARROW)] * 3 + line_sems(),
-        compiler_params=pltpu.CompilerParams(
-            collective_id=1, has_side_effects=True, vmem_limit_bytes=VMEM_LIMIT
-        ),
-        name="forward_sum",
-    )(part, base, rows)
-
-
-def call_backward(count, groups, frames_axis, part, base, grad, below, rows, text, pairs):
+        [pltpu.VMEM(shape, NARROW)] * 3 + line_sems(),
+        1,
+        "forward_sum",
+    )
+
+
+def call_backward(count, groups, frames_axis, part, base, grad, below, rows, pairs, sources, widths):
     shape = part.shape
-    columns = [second.shape[1] for _, second in pairs]
-    results, scratch = Products.shapes(groups, frames_axis, columns, shape[1])
-    return pl.pallas_call(
-        functools.partial(backward_kernel, count, groups, frames_axis, len(pairs), bool(scratch)),
-        out_shape=(
+    results, scratch = Scatters.shapes(groups, frames_axis, shape[1], widths)
+    product = (shape[1], sum(second.shape[1] for _, second in pairs))
+    if not widths:
+        results = [jax.ShapeDtypeStruct(product, NARROW)]
+    return fetching_call(
+        functools.partial(backward_kernel, count, groups, frames_axis, widths),
+        [part, base, grad, below, rows, *(item for pair in pairs for item in pair), *sources],
+        (
             jax.ShapeDtypeStruct(shape, WIDE),
             jax.ShapeDtypeStruct(shape, NARROW),
             jax.ShapeDtypeStruct((8, shape[1]), WIDE),
-            jax.ShapeDtypeStruct((groups,) + text.shape, NARROW),
             *results,
         ),
-        in_specs=vmem(6 + 2 * len(pairs)),
-        out_specs=tuple(vmem(4 + len(results))),
-        scratch_shapes=[pltpu.VMEM(shape, NARROW)] * 4
+        ([pltpu.VMEM(product, NARROW)] if widths else [])
+        + [pltpu.VMEM(shape, NARROW)] * 4
         + [pltpu.VMEM((3, 8, shape[1]), WIDE)]
         + line_sems()
-        + GroupExchange.scratch(groups, frames_axis, text.shape)
         + scratch,
-        compiler_params=pltpu.CompilerParams(
-            collective_id=2, has_side_effects=True, vmem_limit_bytes=VMEM_LIMIT
-        ),
-        name="backward_sum",
-    )(part, base, grad, below, rows, text, *(item for pair in pairs for item in pair))
+        2,
+        "backward_sum",
+    )
 
 
 def head_mask(head, shape):
@@ -686,24 +726,29 @@
     return grad_query, grad_keys, grad_values
 
 
-def closing_kernel(count, groups, frames_axis, frames, scattered, *refs):
+def closing_kernel(count, groups, frames_axis, frames, widths, fetch, *refs):
     (
         low_ref, base_ref, grad_ref, small_ref, rows_ref, packed_ref, heads_ref, hidden_ref, in_ref, out_ref,
-        latent_ref, every_ref, in_result, out_result,
-        part_ref, grad_packed, key_rows, value_rows, probs_low, scores_low,
-        land, stage, line_rows, own_rows, tally,
-    ) = refs[:25]
-    line_send, line_recv, all_send, all_recv = refs[29:33]
+        text_ref, *refs,
+    ) = refs
+    sources, refs = refs[: len(widths) - 1], refs[max(len(widths) - 1, 0) :]
+    latent_ref, every_ref, text_all, *refs = refs
+    many = sum(len(columns) for columns in widths)
+    results, refs = refs[:many], refs[many:]
+    (
+        product_ref, part_ref, grad_packed, key_rows, value_rows, probs_low, scores_low,
+        land, stage, line_rows, own_rows, tally, *refs,
+    ) = refs
+    line_send, line_recv, all_send, all_recv = refs[4:8]
     place, group, here = (lax.axis_index(axis) for axis in (LINE, GROUP, FRAME))
     last = count - 1
     share = latent_ref.shape[1]
     local = out_ref.shape[0]
     everyone = groups * frames_axis
     rank = group * frames_axis + here
-    products = Products(
-        groups, frames_axis, [(hidden_ref, grad_packed), (low_ref, heads_ref)], [in_result, out_result],
-        refs[33:], scattered,
-    )
+    products = Products([(hidden_ref, grad_packed), (low_ref, heads_ref)], product_ref)
+    scatters = Scatters(groups, frames_axis, [*sources, product_ref] if widths else [], widths, results, refs[13:])
+    exchange = GroupExchange(groups, frames_axis, text_ref, text_all, refs[8:13])
 
     def member(ahead):
         to = lax.rem(rank + ahead, everyone)
@@ -722,14 +767,16 @@
         pl.semaphore_signal(barrier, inc=1, device_id=neighbour(ahead), device_id_type=MESH)
     lax.fori_loop(1, everyone, greet, 0)
     pl.semaphore_wait(barrier, last + everyone - 1)
+    fetch(0, 5, 8, 9, 10)
 
     def rows_of(owner):
         return pl.ds(pl.multiple_of(owner * share, share), share)
 
     passing = LineScatter(
-        count, place, frames, lambda owner, frame: part_ref[frame, rows_of(owner)], land, stage, refs[25:29]
+        count, place, frames, lambda owner, frame: part_ref[frame, rows_of(owner)], land, stage, refs[0:4]
     )
     patches = base_ref.shape[1]
+    exchange.start()
     for frame in range(frames):
         rows = slice(frame * patches, (frame + 1) * patches)
         given = dot(low_ref[rows], out_ref[...], 1, 1).astype(NARROW)
@@ -742,8 +789,17 @@
             parts = parts + dot(low, in_ref[i * local : (i + 1) * local], 1, 0)
         part_ref[frame] = parts.astype(NARROW)
         passing.relay_both(last, (frame,))
+        if frame == 0:
+            exchange.spread()
+    if last > 1:
+        passing.relay_both(last - 1, (0,))
+    fetch()
     for work in products.work():
         work()
+    if widths:
+        scatters.items[-1].start()
+    if last > 1:
+        passing.relay_both(last - 1, tuple(range(1, frames)))
 
     tally[...] = jnp.zeros_like(tally)
     depth = 32
@@ -774,10 +830,11 @@
 
     for ahead in range(1, count):
         line_copy(ahead).start()
-    for distance in range(last - 1, 0, -1):
+    if widths:
+        for work in scatters.folds(len(widths) - 1):
+            work()
+    for distance in range(last - 2, 0, -1):
         passing.relay_both(distance)
-        if scattered and distance == last - 1:
-            products.aside.fold_all()
     for ahead in range(1, count):
         line_copy(ahead).wait_recv()
     summed = line_rows[0]
@@ -811,27 +868,34 @@
         return carry
 
     lax.fori_loop(1, everyone, settle, 0)
-    products.finish()
-
-
-def call_closing(count, groups, frames_axis, low, base, grad, small, rows, packed, heads, hidden, in_w, out_w):
+    exchange.finish()
+    scatters.finish()
+
+
+def call_closing(
+    count, groups, frames_axis, low, base, grad, small, rows, packed, heads, hidden, in_w, out_w, text, sources, widths
+):
     frames, patches, features = base.shape
     everyone = groups * frames_axis
     share = patches // count
     local = out_w.shape[0]
-    results, scratch = Products.shapes(groups, frames_axis, [packed.shape[1], local], features)
+    results, scratch = Scatters.shapes(groups, frames_axis, features, widths)
+    product = (features, packed.shape[1] + local)
+    if not widths:
+        results = [jax.ShapeDtypeStruct(product, NARROW)]
     dma = pltpu.SemaphoreType.DMA
     wide_keys = local // HD * patches
-    return pl.pallas_call(
-        functools.partial(closing_kernel, count, groups, frames_axis, frames, bool(scratch)),
-        out_shape=(
+    return fetching_call(
+        functools.partial(closing_kernel, count, groups, frames_axis, frames, widths),
+        [low, base, grad, small, rows, packed, heads, hidden, in_w, out_w, text, *sources],
+        (
             jax.ShapeDtypeStruct((frames, share, features), NARROW),
             jax.ShapeDtypeStruct((everyone, 16, features), WIDE),
+            jax.ShapeDtypeStruct((groups,) + text.shape, NARROW),
             *results,
         ),
-        in_specs=vmem(10),
-        out_specs=tuple(vmem(4)),
-        scratch_shapes=[
+        ([pltpu.VMEM(product, NARROW)] if widths else [])
+        + [
             pltpu.VMEM((frames, patches, features), NARROW),
             pltpu.VMEM(packed.shape, NARROW),
             pltpu.VMEM((wide_keys, local), NARROW),
@@ -847,18 +911,105 @@
         + scatter_sems(count, frames)
         + [dma((count,))] * 2
         + [dma((everyone,))] * 2
+        + GroupExchange.scratch(groups, frames_axis, text.shape)
         + scratch,
-        compiler_params=pltpu.CompilerParams(
-            collective_id=4, has_side_effects=True, vmem_limit_bytes=VMEM_LIMIT
-        ),
-        name="closing",
-    )(low, base, grad, small, rows, packed, heads, hidden, in_w, out_w)
+        4,
+        "closing",
+    )
+
+
+def finishing_kernel(groups, frames_axis, modulation_rows, layouts, small_ref, ada_ref, text_ref, captions_ref, *refs):
+    many = len(layouts)
+    sources, refs = refs[:many], refs[many:]
+    ada_out, table_out, gain_out, caption_out, *results = refs
+    local = table_out.shape[1]
+    buckets = table_out.shape[0]
+    column = ada_out.shape[1]
+    features = small_ref.shape[2]
+    rank = lax.axis_index(GROUP) * frames_axis + lax.axis_index(FRAME)
+
+    def over_frames(group, row):
+        first = group * frames_axis
+        found = small_ref[first, row : row + 1]
+        for other in range(1, frames_axis):
+            found = found + small_ref[first + other, row : row + 1]
+        return found
+
+    gain = over_frames(0, 14)
+    for group in range(1, groups):
+        gain = gain + over_frames(group, 14)
+    gain_out[...] = gain
+
+    side = jnp.concatenate([small_ref[group * frames_axis, 15:16] for group in range(groups)], axis=0)
+    cond, chosen = side[:, 0:local], side[:, local : local + buckets]
+    below = 1.0 / (1.0 + jnp.exp(-cond))
+    act_low = (cond * below).astype(NARROW)
+    act_twice = jnp.concatenate([act_low, act_low], axis=0)
+    where = lax.broadcasted_iota(jnp.int32, (features, column), 0)
+    which = lax.broadcasted_iota(jnp.int32, (features, column), 1) + rank * column
+    select = jnp.where(where == which, 1.0, 0.0).astype(NARROW)
+    grad_act = jnp.zeros((2 * groups, local), WIDE)
+    for k, row in enumerate(modulation_rows):
+        rows = jnp.concatenate([over_frames(group, row) for group in range(groups)], axis=0)
+        pair = jnp.concatenate(split_pair(rows), axis=0)
+        grad_act = grad_act + dot(pair, ada_ref[k], 1, 1)
+        columns = dot(pair, select, 1, 0).astype(NARROW)
+        ada_out[k] = dot(columns, act_twice, 0, 0)
+    slope = below * (1.0 + cond * (1.0 - below))
+    grad_cond = (grad_act[0:groups] + grad_act[groups:]) * slope
+    spread = jnp.concatenate(split_pair(grad_cond), axis=0)
+    chosen = chosen.astype(NARROW)
+    table_out[...] = dot(jnp.concatenate([chosen, chosen], axis=0), spread, 0, 0)
+
+    slots = captions_ref.shape[1]
+    caption = dot(text_ref[0, 0:slots], captions_ref[0], 0, 0)
+    for group in range(1, groups):
+        caption = caption + dot(text_ref[group, 0:slots], captions_ref[group], 0, 0)
+    caption_out[...] = caption
+    for source, result, layout in zip(sources, results, layouts):
+        if layout == 0:
+            result[...] = source[...]
+        else:
+            parts = source.shape[1] // local
+            for i in range(parts):
+                values = source[:, i * local : (i + 1) * local]
+                if layout == 1:
+                    result[i] = values
+                else:
+                    result[:, i] = values
+
+
+def call_finishing(groups, frames_axis, buckets, modulation_rows, layouts, small, ada, text, captions, sources):
+    parts, local, features = ada.shape
+    block = features // (groups * frames_axis)
+
+    def shape_of(source, layout):
+        n = source.shape[1] // local
+        return (source.shape, (n, source.shape[0], local), (source.shape[0], n, local))[layout]
+
+    results = [
+        jax.ShapeDtypeStruct((parts, block, local), WIDE),
+        jax.ShapeDtypeStruct((buckets, local), WIDE),
+        jax.ShapeDtypeStruct((1, features), WIDE),
+        jax.ShapeDtypeStruct((local, captions.shape[2]), WIDE),
+    ]
+    results += [
+        jax.ShapeDtypeStruct(shape_of(source, layout), source.dtype) for source, layout in zip(sources, layouts)
+    ]
+    return pl.pallas_call(
+        functools.partial(finishing_kernel, groups, frames_axis, modulation_rows, layouts),
+        out_shape=tuple(results),
+        in_specs=vmem(4 + len(sources)),
+        out_specs=tuple(vmem(len(results))),
+        compiler_params=pltpu.CompilerParams(vmem_limit_bytes=62 * 2**20),
+        name="finishing",
+    )(small, ada, text, captions, *sources)
 
 
 def opening_kernel(
-    count, groups, frames_axis, latent_ref, act_ref, ada_ref, captions_ref,
-    base_ref, normed_ref, mods_ref, spread_ref,
-    land, ada, mine, others,
+    count, groups, frames_axis, latent_ref, act_ref, ada_ref, captions_ref, caption_full, caption_w,
+    base_ref, normed_ref, mods_ref, text_out, spread_ref,
+    caption_here, caption_here_w, caption_sem, land, ada, mine, others,
     up_send, down_send, land_recv, ada_sem, mods_send, mods_recv, cap_send, cap_recv, cap_local,
 ):
     place = lax.axis_index(LINE)
@@ -871,6 +1022,12 @@
 
     loads = [pltpu.make_async_copy(ada_ref.at[k], ada.at[k], ada_sem.at[k]) for k in range(parts)]
     for load in loads:
+        load.start()
+    text_loads = [
+        pltpu.make_async_copy(caption_full, caption_here, caption_sem.at[0]),
+        pltpu.make_async_copy(caption_w, caption_here_w, caption_sem.at[1]),
+    ]
+    for load in text_loads:
         load.start()
 
     barrier = pltpu.get_barrier_semaphore()
@@ -958,6 +1115,9 @@
     for ahead in range(1, count):
         mods_copy(ahead).start()
     others[place] = mine[...]
+    for load in text_loads:
+        load.wait()
+    text_out[...] = dot(caption_here[...], caption_here_w[...], 1, 1).astype(NARROW)
     for distance in range(2, count - 1):
         arrive(distance)
     for ahead in range(1, count):
@@ -1010,11 +1170,12 @@
     own_caption.wait()
 
 
-def call_opening(count, groups, frames_axis, latent, act, ada, captions):
+def call_opening(count, groups, frames_axis, latent, act, ada, captions, caption_w):
     frames, share, features = latent.shape
     parts = ada.shape[0]
     length, text_width = captions.shape
     width = text_width // (groups * frames_axis)
+    caption_full = captions
     if width % 128:
         blocks = captions.reshape(length, groups, frames_axis, width)
         captions = jnp.transpose(
@@ -1029,11 +1190,15 @@
             jax.ShapeDtypeStruct(full, WIDE),
             jax.ShapeDtypeStruct(full, NARROW),
             jax.ShapeDtypeStruct((16, features), WIDE),
+            jax.ShapeDtypeStruct((length, caption_w.shape[0]), NARROW),
             jax.ShapeDtypeStruct((groups, length, width), NARROW),
         ),
-        in_specs=vmem(2) + [anywhere] * 2,
-        out_specs=tuple(vmem(3) + [anywhere]),
+        in_specs=vmem(2) + [anywhere] * 4,
+        out_specs=tuple(vmem(4) + [anywhere]),
         scratch_shapes=[
+            pltpu.VMEM(caption_full.shape, NARROW),
+            pltpu.VMEM(caption_w.shape, NARROW),
+            dma((2,)),
             pltpu.VMEM((count, frames, share, features), NARROW),
             pltpu.VMEM(ada.shape, NARROW),
             pltpu.VMEM((16, features), WIDE),
@@ -1049,10 +1214,10 @@
             dma,
         ],
         compiler_params=pltpu.CompilerParams(
-            collective_id=3, has_side_effects=True, vmem_limit_bytes=VMEM_LIMIT
+            collective_id=3, has_side_effects=True, vmem_limit_bytes=62 * 2**20
         ),
         name="opening",
-    )(latent, act, ada, captions)
+    )(latent, act, ada, captions, caption_full, caption_w)
 
 
 STAGES = 4
@@ -1069,26 +1234,26 @@
     return 0.5 * values * (1.0 + bent), slope
 
 
-def middle_kernel(count, groups, frames_axis, frames, scattered, *refs):
+def middle_kernel(count, groups, frames_axis, frames, scattered, fetch, *refs):
     (
         first_ref, base_ref, cotangent_ref, rows_ref, bias_ref,
-        keys_ref, values_ref, query_w, out_w, up_w, down_w,
+        text_ref, text_w, query_w, out_w, up_w, down_w,
         base_three, grad_two, low_two, low_three, normed_three, heads_out, grad_query,
-        grad_keys, grad_values, sums_ref, extra_part, up_result, down_result,
+        grad_keys, grad_values, sums_ref, extra_part, text_rows, down_grad, up_result,
+        keys_ref, values_ref,
         normed_four, low_four, active, grad_inner, base_two, branch_two, query, grad_heads, part, mixed, tally,
         land, stage, total, cross, in_send, land_recv, cross_recv, out_send, out_recv, *scratch,
     ) = refs
     place = lax.axis_index(LINE)
     if scattered:
-        up_grad, down_grad, *scratch = scratch
-        asides = [
-            Scatter(groups, frames_axis, source, scratch[i * 8 : (i + 1) * 8])
-            for i, source in enumerate((up_grad, down_grad))
-        ]
+        up_grad, *scratch = scratch
+        scatters = Scatters(groups, frames_axis, [up_grad], [[up_grad.shape[1]]], [up_result], scratch)
+        asides = scatters.items
         greet_line(place, count, 0, asides[0].partners())
     else:
-        up_grad, down_grad, asides = up_result, down_result, []
+        up_grad, asides = up_result, []
         greet_line(place, count)
+    fetch(0, 1, 3)
     half = count // 2
     left = place < half
     level = jnp.where(left, place, count - 1 - place)
@@ -1292,23 +1457,30 @@
         rows = slice(frame * patches, (frame + 1) * patches)
         extra_part[rows] = dot(active[rows], down_w[...], 1, 0).astype(NARROW)
 
+    def text_pairs():
+        fetch.again(2, 4, 5, 6, 7, 8, 9, 10)
+        slots_here = text_ref.shape[1]
+        text_rows[slots_here:] = jnp.zeros((width - slots_here, text_rows.shape[1]), NARROW)
+        for owner in range(count):
+            text_rows[0:slots_here, owner * local : (owner + 1) * local] = text_ref[owner]
+        packed = dot(text_rows[...], text_w[...], 1, 1).astype(NARROW)
+        spread_heads(packed[:, 0:local], keys_ref)
+        spread_heads(packed[:, local:], values_ref)
+
     third = up_w.shape[0] // 3
-    late = {}
+    late = {(0, 1): [text_pairs]}
 
     def later(slot, chunk, work, *args):
         late.setdefault((slots - 3 + slot, chunk), []).append(functools.partial(work, *args))
 
     for i, spot in enumerate(((0, 0), (0, 1), (0, 2))):
         later(*spot, up_tile, i)
-    for i, spot in enumerate(((0, 7), (1, 0), (1, 1))):
-        later(*spot, down_tile, i)
+    for i in range(3):
+        later(2, 1 + i, down_tile, i)
     if asides:
         later(0, 2, asides[0].start)
-        later(1, 1, asides[1].start)
-        spots = (((1, 2), (1, 7), (2, 0), (2, 1)), ((2, 2), (2, 3), (2, 4), (2, 5)))
-        for aside, places in zip(asides, spots):
-            for i in range(aside.total):
-                later(*places[min(i, 3)], aside.fold, aside.total - 1 - i)
+        for i, work in enumerate(scatters.folds(0)):
+            later(*((1, 0), (1, 1), (1, 2), (1, 7))[min(i, 3)], work)
     for frame in range(frames):
         later(2, 6 + min(frame, 1), extra, frame)
 
@@ -1392,17 +1564,18 @@
     sums_ref[...] = jnp.zeros_like(sums_ref)
     for i in range(4):
         sums_ref[i : i + 1] = jnp.sum(tally[i], axis=0, keepdims=True)
-    for aside, result in zip(asides, (up_result, down_result)):
-        aside.finish([result])
+    for aside in asides:
+        aside.finish([up_result])
 
 
 def call_middle(
-    count, groups, frames_axis, frames, first, base, cotangent, rows, bias, keys, values, query_w, out_w, up_w, down_w
+    count, groups, frames_axis, frames, first, base, cotangent, rows, bias, text, text_w, query_w, out_w, up_w, down_w
 ):
     tokens, features = first.shape
     local, hidden = query_w.shape[0], up_w.shape[1]
     chunks = tokens // frames // MIDDLE_ROWS
     scattered = can_scatter(groups, frames_axis, features)
+    keys_shape = (local // HD * bias.shape[2], local)
 
     def wide(*shape):
         return jax.ShapeDtypeStruct(shape, WIDE)
@@ -1410,23 +1583,25 @@
     def narrow(*shape):
         return jax.ShapeDtypeStruct(shape, NARROW)
 
-    found, scratch = Products.shapes(groups, frames_axis, [hidden], features)
-    scratch = scratch[:1] * 2 + scratch[1:] * 2
+    found, scratch = [narrow(features, hidden)], []
+    if scattered:
+        found, scratch = Scatters.shapes(groups, frames_axis, features, [[hidden]])
+        scratch = [pltpu.VMEM((features, hidden), NARROW)] + scratch
     results = (
         [wide(tokens, features)] * 2
         + [narrow(tokens, features)] * 3
         + [narrow(tokens, local)] * 2
-        + [wide(*keys.shape)] * 2
-        + [wide(8, features), narrow(tokens, features)]
-        + found * 2
+        + [wide(*keys_shape)] * 2
+        + [wide(8, features), narrow(tokens, features), narrow(bias.shape[2], features), narrow(features, hidden)]
+        + found
     )
     sem = pltpu.SemaphoreType.DMA((STAGES * frames, chunks))
-    return pl.pallas_call(
+    return fetching_call(
         functools.partial(middle_kernel, count, groups, frames_axis, frames, scattered),
-        out_shape=tuple(results),
-        in_specs=vmem(11),
-        out_specs=tuple(vmem(len(results))),
-        scratch_shapes=[pltpu.VMEM((tokens, features), NARROW)] * 2
+        [first, base, cotangent, rows, bias, text, text_w, query_w, out_w, up_w, down_w],
+        tuple(results),
+        [pltpu.VMEM(keys_shape, NARROW)] * 2
+        + [pltpu.VMEM((tokens, features), NARROW)] * 2
         + [pltpu.VMEM((tokens, hidden), NARROW)] * 2
         + [
             pltpu.VMEM((tokens, features), WIDE),
@@ -1441,11 +1616,9 @@
         + [pltpu.VMEM((2, tokens, features), NARROW)]
         + [sem] * 5
         + scratch,
-        compiler_params=pltpu.CompilerParams(
-            collective_id=7, has_side_effects=True, vmem_limit_bytes=62 * 2**20
-        ),
-        name="middle",
-    )(first, base, cotangent, rows, bias, keys, values, query_w, out_w, up_w, down_w)
+        7,
+        "middle",
+    )
 
 
 def greet_frames(here, frames_axis):
@@ -1470,13 +1643,11 @@
 
 
 def per_head(values, columns):
-    high, rest = split_pair(values)
-    return dot(high, columns, 1, 0) + dot(rest, columns, 1, 0)
+    return dot(values.astype(NARROW), columns, 1, 0)
 
 
 def over_features(values, columns):
-    high, rest = split_pair(values)
-    return dot(high, columns, 1, 1) + dot(rest, columns, 1, 1)
+    return dot(values.astype(NARROW), columns, 1, 1)
 
 
 def window_probs(query, keys_of, bias_of, columns):
@@ -1490,7 +1661,7 @@
 
 
 def temporal_forward_kernel(
-    count, frames_axis, frames, hidden_ref, in_ref, out_ref, bias_ref, cotangent_ref, text_ref,
+    count, frames_axis, frames, fetch, hidden_ref, in_ref, out_ref, bias_ref, cotangent_ref, text_ref,
     query_ref, keys_ref, values_ref, heads_ref, part_ref, cotangent_full, text_full,
     halo_send, halo_recv, *sems,
 ):
@@ -1500,6 +1671,7 @@
     share = cotangent_ref.shape[1]
     last = count - 1
     greet_line(place, count, greet_frames(here, frames_axis))
+    fetch()
     cells = (keys_ref, values_ref)
 
     def shares(owner):
@@ -1605,37 +1777,43 @@
         + [narrow(tokens, local), narrow(tokens, features)]
         + [narrow(frames, share * count, features), narrow(count, *text.shape)]
     )
-    return pl.pallas_call(
+    return fetching_call(
         functools.partial(temporal_forward_kernel, count, frames_axis, frames),
-        out_shape=tuple(results),
-        in_specs=vmem(6),
-        out_specs=tuple(vmem(len(results))),
-        scratch_shapes=[pltpu.SemaphoreType.DMA((3, 2))] * 2 + gather_sems(count) * 2,
-        compiler_params=pltpu.CompilerParams(
-            collective_id=8, has_side_effects=True, vmem_limit_bytes=VMEM_LIMIT
-        ),
-        name="temporal_forward",
-    )(hidden, in_w, out_w, bias, cotangent, text)
+        [hidden, in_w, out_w, bias, cotangent, text],
+        tuple(results),
+        [pltpu.SemaphoreType.DMA((3, 2))] * 2 + gather_sems(count) * 2,
+        8,
+        "temporal_forward",
+    )
 
 
 def temporal_backward_kernel(
-    count, groups, frames_axis, frames, scattered,
-    grad_ref, in_ref, out_ref, bias_ref, query_ref, keys_ref, values_ref,
-    extra_ref, text_keys, text_values, text_w, text_rows, cross_hidden, cross_grad, cross_low, cross_heads,
-    grad_packed, part_ref, extra_own, text_own, query_result, keyval_result, out_result,
-    near_keys, near_values, rim_out, rim_in, halo_send, halo_recv, text_ref, text_low,
-    extra_land, extra_stage, text_land, text_stage, *sems,
+    count, groups, frames_axis, frames, widths, fetch, *refs
 ):
+    (
+        grad_ref, in_ref, out_ref, bias_ref, query_ref, keys_ref, values_ref,
+        extra_ref, text_keys, text_values, text_w, text_rows, cross_hidden, cross_grad, cross_low, cross_heads, *refs,
+    ) = refs
+    sources, refs = refs[: len(widths)], refs[len(widths) :]
+    grad_packed, part_ref, extra_own, text_own, product_ref, *refs = refs
+    results, refs = refs[: len(widths)], refs[len(widths) :]
+    (
+        near_keys, near_values, rim_out, rim_in, halo_send, halo_recv, text_ref, text_low,
+        extra_land, extra_stage, text_land, text_stage, *sems,
+    ) = refs
+    scatters = Scatters(groups, frames_axis, sources, widths, results, sems[8:])
     products = Products(
-        groups, frames_axis, [(cross_hidden, cross_grad), (text_rows, text_low), (cross_low, cross_heads)],
-        [query_result, keyval_result, out_result], sems[8:], scattered,
-    )
+        [(cross_hidden, cross_grad), (text_rows, text_low), (cross_low, cross_heads)], product_ref
+    ).work()
     place, here = lax.axis_index(LINE), lax.axis_index(FRAME)
     patches = grad_ref.shape[0] // frames
     local = out_ref.shape[0]
     share = extra_own.shape[1]
     last = count - 1
-    greet_line(place, count, greet_frames(here, frames_axis), products.partners())
+    greet_line(place, count, greet_frames(here, frames_axis), scatters.partners() if widths else ())
+    fetch(7, *range(16, 16 + len(sources)))
+    for item in scatters.items:
+        item.start()
 
     def shares(owner, frame):
         return extra_ref[frame, pl.ds(pl.multiple_of(owner * share, share), share)]
@@ -1646,6 +1824,64 @@
     ]
     moving[0].relay_both(last)
     near = (near_keys, near_values)
+    def halo(which):
+        to = here - 1 if which < 2 else here + 1
+        return remote(
+            rim_out.at[which], rim_in.at[which], halo_send.at[which], halo_recv.at[which], {FRAME: to}
+        )
+
+    has_next, has_previous = here < frames_axis - 1, here > 0
+
+    def frame_rows(frame):
+        return slice(frame * patches, (frame + 1) * patches)
+
+    fetch(0, 2, 3, 4, 5, 6)
+    columns = head_columns(local)
+    seen = set()
+
+    def add(item, cell, terms):
+        if (item, cell) in seen:
+            near[item][cell] += terms
+        else:
+            near[item][cell] = terms
+        seen.add((item, cell))
+
+    for frame in range(frames):
+        given = dot(grad_ref[frame_rows(frame)], out_ref[...], 1, 1).astype(NARROW).astype(WIDE)
+        asked = query_ref[frame_rows(frame)].astype(WIDE)
+        probs = window_probs(
+            asked,
+            lambda offset: keys_ref[frame + offset].astype(WIDE),
+            lambda offset: bias_ref[frame * WIN + offset : frame * WIN + offset + 1],
+            columns,
+        )
+        pulled = [per_head(given * values_ref[frame + offset].astype(WIDE), columns) for offset in range(WIN)]
+        shared = sum((probs[i] * pulled[i] for i in range(1, WIN)), probs[0] * pulled[0])
+        found = jnp.zeros((patches, local), WIDE)
+        for offset in range(WIN):
+            scores = HD ** (-0.5) * over_features(probs[offset] * (pulled[offset] - shared), columns)
+            found = found + scores * keys_ref[frame + offset].astype(WIDE)
+            add(0, frame + offset, scores * asked)
+            add(1, frame + offset, over_features(probs[offset], columns) * given)
+        grad_packed[frame_rows(frame), 0:local] = found.astype(NARROW)
+        if frame == 0:
+            for item in scatters.items:
+                item.fold_all()
+            if last > 1:
+                moving[0].relay_both(last - 1)
+
+    for which in range(3):
+
+        @pl.when(has_previous if which < 2 else has_next)
+        def _():
+            for item in range(2):
+                span = slice(item * local, (item + 1) * local)
+                rim_out[which, :, span] = near[item][which if which < 2 else frames + 2].astype(NARROW)
+            halo(which).start()
+
+    for distance in range(last - 2, 0, -1):
+        moving[0].relay_both(distance)
+    fetch()
     slots = text_low.shape[0]
     text_parts = jnp.zeros((slots, grad_ref.shape[1]), WIDE)
     for item, (source, factor) in enumerate(((text_keys, HD ** (-0.5)), (text_values, 1.0))):
@@ -1656,65 +1892,12 @@
     for owner in range(count):
         text_ref[owner] = text_parts[:, owner * local : (owner + 1) * local]
     moving[1].relay_both(last)
-
-
-    def halo(which):
-        to = here - 1 if which < 2 else here + 1
-        return remote(
-            rim_out.at[which], rim_in.at[which], halo_send.at[which], halo_recv.at[which], {FRAME: to}
-        )
-
-    has_next, has_previous = here < frames_axis - 1, here > 0
-
-    def frame_rows(frame):
-        return slice(frame * patches, (frame + 1) * patches)
-
-    columns = head_columns(local)
-    seen = set()
-
-    def add(item, cell, terms):
-        if (item, cell) in seen:
-            near[item][cell] += terms
-        else:
-            near[item][cell] = terms
-        seen.add((item, cell))
-
-    for frame in range(frames):
-        given = dot(grad_ref[frame_rows(frame)], out_ref[...], 1, 1).astype(NARROW).astype(WIDE)
-        asked = query_ref[frame_rows(frame)].astype(WIDE)
-        probs = window_probs(
-            asked,
-            lambda offset: keys_ref[frame + offset].astype(WIDE),
-            lambda offset: bias_ref[frame * WIN + offset : frame * WIN + offset + 1],
-            columns,
-        )
-        pulled = [per_head(given * values_ref[frame + offset].astype(WIDE), columns) for offset in range(WIN)]
-        shared = sum((probs[i] * pulled[i] for i in range(1, WIN)), probs[0] * pulled[0])
-        found = jnp.zeros((patches, local), WIDE)
-        for offset in range(WIN):
-            scores = HD ** (-0.5) * over_features(probs[offset] * (pulled[offset] - shared), columns)
-            found = found + scores * keys_ref[frame + offset].astype(WIDE)
-            add(0, frame + offset, scores * asked)
-            add(1, frame + offset, over_features(probs[offset], columns) * given)
-        grad_packed[frame_rows(frame), 0:local] = found.astype(NARROW)
-
-    for which in range(3):
-
-        @pl.when(has_previous if which < 2 else has_next)
-        def _():
-            for item in range(2):
-                span = slice(item * local, (item + 1) * local)
-                rim_out[which, :, span] = near[item][which if which < 2 else frames + 2].astype(NARROW)
-            halo(which).start()
-
-    folds = fold_works(products)
-    for work in products.work():
+    for i, work in enumerate(products):
         work()
-    for distance in range(last - 1, 0, -1):
-        for item in moving:
-            item.relay_both(distance)
-        for work in folds if distance == last - 1 else ():
-            work()
+        if last - 1 - i > 0:
+            moving[1].relay_both(last - 1 - i)
+    for distance in range(last - 1 - len(products), 0, -1):
+        moving[1].relay_both(distance)
 
     for which in range(3):
 
@@ -1745,12 +1928,12 @@
         def _():
             halo(which).wait_send()
 
-    products.finish()
+    scatters.finish()
 
 
 def call_temporal_backward(
     count, groups, frames_axis, grad, in_w, out_w, bias, query, keys, values, extra, text_keys, text_values, text_w,
-    text_rows, *cross_pairs,
+    text_rows, cross_pairs, sources, widths,
 ):
     tokens, features = grad.shape
     frames, patches = extra.shape[:2]
@@ -1761,19 +1944,19 @@
     def narrow(*shape):
         return jax.ShapeDtypeStruct(shape, NARROW)
 
-    found, scratch = Products.shapes(groups, frames_axis, [local, 2 * local, local], features)
     results = (
         [narrow(tokens, 3 * local)]
         + [narrow(tokens, features), jax.ShapeDtypeStruct((frames, share, features), WIDE)]
-        + [narrow(slots, local)]
-        + found
-    )
-    return pl.pallas_call(
-        functools.partial(temporal_backward_kernel, count, groups, frames_axis, frames, bool(scratch)),
-        out_shape=tuple(results),
-        in_specs=vmem(16),
-        out_specs=tuple(vmem(len(results))),
-        scratch_shapes=[pltpu.VMEM((frames + 3, patches, local), WIDE)] * 2
+        + [narrow(slots, local), narrow(features, 4 * local)]
+    )
+    found, scratch = Scatters.shapes(groups, frames_axis, features, widths)
+    results = results + found
+    return fetching_call(
+        functools.partial(temporal_backward_kernel, count, groups, frames_axis, frames, widths),
+        [grad, in_w, out_w, bias, query, keys, values, extra, text_keys, text_values, text_w, text_rows,
+        *cross_pairs, *sources,],
+        tuple(results),
+        [pltpu.VMEM((frames + 3, patches, local), WIDE)] * 2
         + [pltpu.VMEM((3, patches, 2 * local), NARROW)] * 2
         + [pltpu.SemaphoreType.DMA((3,))] * 2
         + [pltpu.VMEM((count, slots, local), NARROW), pltpu.VMEM((slots, 2 * local), NARROW)]
@@ -1782,11 +1965,9 @@
         + scatter_sems(count, frames)
         + scatter_sems(count, 1)
         + scratch,
-        compiler_params=pltpu.CompilerParams(
-            collective_id=9, has_side_effects=True, vmem_limit_bytes=VMEM_LIMIT
-        ),
-        name="temporal_backward",
-    )(grad, in_w, out_w, bias, query, keys, values, extra, text_keys, text_values, text_w, text_rows, *cross_pairs)
+        9,
+        "temporal_backward",
+    )
 
 
 def attend_forward(query, keys, values):
@@ -1845,12 +2026,11 @@
     cond_row = jnp.sum(chosen[:, None] * time_table.astype(WIDE), axis=0)
     act_low = swish_act(cond_row).astype(NARROW)
     caption_here = captions[0].reshape(slots, text_width)
-    base_grid, normed_grid, mods, caption_share = call_opening(
+    base_grid, normed_grid, mods, text_part, caption_share = call_opening(
         count, groups, frames_axis, latent[0], jnp.broadcast_to(act_low[None], (16, local)),
-        jnp.transpose(ada_weight, (1, 0, 2)), caption_here,
+        jnp.transpose(ada_weight, (1, 0, 2)), caption_here, caption_proj.T,
     )
     base_zero, spatial_hidden = flat(base_grid), flat(normed_grid)
-    text_part = dot(caption_here, caption_proj, 1, 0).astype(NARROW)
 
     def rows_of(*rows):
         filled = [jnp.zeros((features,), WIDE)] * (8 - len(rows))
@@ -1889,53 +2069,58 @@
         count, frames_axis, temporal_hidden, temporal_in, temporal_outproj, window_bias, cotangent[0], text_part
     )
     cotangent_full = flat(cotangent_full)
-    text_rows = jnp.transpose(text_full, (1, 0, 2)).reshape(slots, features)
 
     slot_pad = -slots % 128
-    text_rows = jnp.pad(text_rows, ((0, slot_pad), (0, 0)))
-    text_packed = dot(text_rows, keyval_in, 1, 1).astype(NARROW)
     slot_index = jnp.arange(slots)
     key_valid = (own_clip[:, None] == (slot_index // text_length)[None, :]) & (
         slot_index % text_length < jnp.repeat(text_counts[0], text_length)
     )[None, :]
     bias = jnp.pad(jnp.where(key_valid, 0.0, NEGATIVE), ((0, 0), (0, slot_pad)), constant_values=NEGATIVE)
     bias = jnp.broadcast_to(bias[:, None], (frames, 8, slots + slot_pad))
-    mask_of_head = (jnp.arange(local) // HD)[None, :] == jnp.arange(local // HD)[:, None]
-
-    def by_head(values):
-        return jnp.where(mask_of_head[:, None], values[None], 0).reshape(-1, local)
-
     (
         base_three, grad_two, grad_temporal_low, grad_cross_low, cross_hidden, cross_flat, grad_cross_packed,
-        text_grad_keys, text_grad_values, sums_middle, mlp_part, grad_up, grad_down,
+        text_grad_keys, text_grad_values, sums_middle, mlp_part, text_rows, grad_down, grad_up,
     ) = call_middle(
         count, groups, frames_axis, frames, temporal_part, base_one, cotangent_full,
         rows_of(mods[5], cross_gain.astype(WIDE), 1.0 + mods[7], mods[6], mods[8]), bias,
-        by_head(text_packed[:, :local]), by_head(text_packed[:, local:]),
-        query_in, cross_outproj, mlp_up, mlp_down,
-    )
-
-    def summed(found):
-        return found if can_scatter(groups, frames_axis, features) else sum_matrix_grads(found)
-
-    grad_up, grad_down = summed([grad_up, grad_down])
-
-    grad_temporal_packed, temporal_grad_part, mlp_out, text_grad, *found = call_temporal_backward(
+        text_full, keyval_in, query_in, cross_outproj, mlp_up, mlp_down,
+    )
+
+    def outside(packed, widths):
+        return sum_matrix_grads(
+            [
+                item[:, sum(columns[:i]) : sum(columns[: i + 1])]
+                for item, columns in zip(packed, widths)
+                for i in range(len(columns))
+            ]
+        )
+
+    if not can_scatter(groups, frames_axis, features):
+        (grad_up,) = outside([grad_up], [[grad_up.shape[1]]])
+
+    inside = can_scatter(groups, frames_axis, features)
+    down_widths = [[grad_down.shape[1]]]
+    grad_temporal_packed, temporal_grad_part, mlp_out, text_grad, grad_cross, *found = call_temporal_backward(
         count, groups, frames_axis, grad_temporal_low, temporal_in, temporal_outproj, window_bias,
         temporal_query, temporal_keys, temporal_values, grid(mlp_part), text_grad_keys, text_grad_values,
-        keyval_in, text_rows, cross_hidden, grad_cross_packed, grad_cross_low, cross_flat,
-    )
-    grad_query_cross, grad_keyval_cross, grad_outproj_cross = summed(found)
+        keyval_in, text_rows, [cross_hidden, grad_cross_packed, grad_cross_low, cross_flat],
+        [grad_down] if inside else [], down_widths if inside else [],
+    )
+    (grad_down,) = found if inside else outside([grad_down], down_widths)
     output = (own(base_three) + mods[8] * mlp_out).astype(NARROW)[None]
     gate_mlp_part = jnp.sum(cotangent[0].astype(WIDE) * mlp_out, axis=(0, 1))
-    grad_one, grad_spatial_low, sums_temporal, text_grad_all, *found = call_backward(
+    cross_widths, qkv_widths = [local, 2 * local, local], [3 * local, local]
+    grad_one, grad_spatial_low, sums_temporal, *found = call_backward(
         count, groups, frames_axis, temporal_grad_part, base_one, grad_two, spatial_out,
-        rows_of(1.0 + mods[4], mods[2]), text_grad,
+        rows_of(1.0 + mods[4], mods[2]),
         [(temporal_hidden, grad_temporal_packed), (grad_temporal_low, temporal_flat)],
-    )
-    grad_inproj_temporal, grad_outproj_temporal = summed(found)
-    caption_rows = caption_share.reshape(groups * slots, -1)
-    grad_caption = dot(caption_rows, text_grad_all[:, 0:slots].reshape(groups * slots, local), 0, 0)
+        [grad_cross] if inside else [], [cross_widths, qkv_widths] if inside else [],
+    )
+    if not inside:
+        found = outside([grad_cross, found[0]], [cross_widths, qkv_widths])
+    (
+        grad_query_cross, grad_keyval_cross, grad_outproj_cross, grad_inproj_temporal, grad_outproj_temporal,
+    ) = found
 
     side_row = jnp.pad(jnp.concatenate([cond_row, chosen]), (0, features - local - chosen.shape[0]))
     blank = jnp.zeros((features,), WIDE)
@@ -1947,44 +2132,41 @@
             sums_middle[1], sums_middle[2], side_row,
         ]
     )
-    grad_latent, small_all, *found = call_closing(
+    grad_latent, small_all, text_grad_all, *found = call_closing(
         count, groups, frames_axis, grad_spatial_low, grid(base_zero), grid(grad_one), small,
         rows_of(1.0 + mods[1]), spatial_packed, spatial_flat, spatial_hidden, spatial_in, spatial_outproj,
-    )
-    grad_inproj_spatial, grad_outproj_spatial = summed(found)
-
-    small_all = small_all.reshape(groups, frames_axis, 16, features)
-    small_sums = jnp.sum(small_all, axis=1)
-    modulation_grad = jnp.stack([small_sums[:, i] for i in (0, 1, 8, 9, 10, 11, 12, 13, 2)], axis=1)
-    grad_gain = jnp.sum(small_sums[:, 14], axis=0)
-    cond_all = small_all[:, 0, 15, 0:local]
-    chosen_all = small_all[:, 0, 15, local : local + chosen.shape[0]]
-    act_all, swish_pull = jax.vjp(swish_act, cond_all)
-    act_all = act_all.astype(NARROW).astype(WIDE)
-    column = features // (groups * frames_axis)
-    rank = lax.axis_index(BOTH)
-    column_grads = lax.dynamic_slice_in_dim(modulation_grad, rank * column, column, axis=2)
-    grad_ada = jnp.einsum("gc,gkd->ckd", act_all, column_grads, precision=HIGHEST)
-    grad_act = jnp.einsum("ckd,gkd->gc", ada_weight.astype(WIDE), modulation_grad, precision=HIGHEST)
-    grad_cond = swish_pull(grad_act)[0]
-    grad_table = jnp.einsum("gn,gc->nc", chosen_all, grad_cond, precision=HIGHEST)
-
-    def unpack(values, parts):
-        return values.reshape(values.shape[0], parts, -1)
-
+        text_grad, [], [qkv_widths] if inside else [],
+    )
+    if not inside:
+        found = outside([found[0]], [qkv_widths])
+    grad_inproj_spatial, grad_outproj_spatial = found
+
+    grad_ada, grad_table, grad_gain, grad_caption, *found = call_finishing(
+        groups, frames_axis, chosen.shape[0], (0, 1, 8, 9, 10, 11, 12, 13, 2), (0, 1, 0, 1, 0, 0, 2, 0, 0, 0),
+        small_all, jnp.transpose(ada_weight, (1, 0, 2)), text_grad_all, caption_share,
+        [
+            grad_latent.reshape(frames * share, features), grad_inproj_spatial, grad_outproj_spatial,
+            grad_inproj_temporal, grad_outproj_temporal, grad_query_cross, grad_keyval_cross,
+            grad_outproj_cross, grad_up, grad_down,
+        ],
+    )
+    (
+        grad_latent, grad_inproj_spatial, grad_outproj_spatial, grad_inproj_temporal, grad_outproj_temporal,
+        grad_query_cross, grad_keyval_cross, grad_outproj_cross, grad_up, grad_down,
+    ) = found
     return (
         output,
-        grad_latent[None],
+        grad_latent.reshape(1, frames, share, features),
         grad_table,
-        grad_ada,
-        unpack(grad_inproj_spatial, 3),
+        jnp.transpose(grad_ada, (2, 0, 1)),
+        jnp.transpose(grad_inproj_spatial, (1, 0, 2)),
         grad_outproj_spatial.T,
-        unpack(grad_inproj_temporal, 3),
+        jnp.transpose(grad_inproj_temporal, (1, 0, 2)),
         grad_outproj_temporal.T,
-        grad_caption,
-        grad_gain,
+        grad_caption.T,
+        grad_gain[0],
         grad_query_cross,
-        unpack(grad_keyval_cross, 2),
+        grad_keyval_cross,
         grad_outproj_cross.T,
         grad_up,
         grad_down.T,

time: 463 us -> 424 us (0.916)
  the two profiles are of different devices: /device:TPU:0 before, /device:TPU:15 now
where the time goes in v3:
time: 424 us; the launch traced here: 415 us
  Pallas kernels  390 us (92%)
  local copies, waits for them, and re-layouts  9.34 us (2%)
  matrix products  8.79 us (2%)
  other arithmetic  5.24 us (1%)
    pallas_call x6, Pallas kernels, fetching_call(): pl.pallas_call(body, out_shape=tuple(out_shape), in_specs=[pl.BlockSpec(m...  349 us
    pallas_call x1, Pallas kernels, call_opening(): pl.pallas_call(functools.partial(opening_kernel, count, groups, frames_ax...  30.3 us
    pallas_call x1, Pallas kernels, call_finishing(): pl.pallas_call(functools.partial(finishing_kernel, groups, frames_axis, m...  11.2 us

profile of v3, /device:TPU:15, one launch (start us, length us, event | category | flops | bytes accessed | tf_op | source)
XLA Modules:
  0.0 415.5 jit_solution(6241807181891539672)
XLA Ops:
  1.3 0.8 multiply_reduce_fusion.2
  2.1 0.6 broadcast_in_dim.26.act_ref
  2.7 30.3 %opening.1 = (f32[2,256,1152]{2,1,0:T(8,128)}, bf16[2,256,1152]{2,1,0:T(8,128)(2,1)}, f32[16,1152]{1,0:T(8,128)}, bf16[240,288]{1,0:T(8,128)(2,1)}, bf16[4,240,512]{2,1,0:T(8,128)(2,1)}) custom-call(bf16[2,64,1152]{2,1,0:T(8,128)(2,1)} %bitcast.79, bf16[16,288]{1,0:T(8,128)(2,1)} %broadcast_in_dim.26.act_ref, bf16[9,288,1152]{2,1,0:T(8,128)(2,1)} %bitcast.57, ...), custom_call_target="tpu_custom_call" | custom-call | tf_op jit(solution)/shard_map/opening/pallas_call | solution.py:1187
  33.0 2.8 convolution_convert_fusion.1.refs_5_
  35.8 0.4 fusion.26
  36.2 0.3 reshape.140
  36.5 0.3 reshape.141
  36.9 0.0 copy-done
  36.9 2.2 fusion.27
  39.0 0.3 reshape.139
  39.4 0.0 copy-start.3
  39.4 2.0 fusion.2
  41.4 0.3 copy.50
  41.7 0.0 copy-done.3
  41.8 1.9 convolution_convert_fusion.refs_0_
  43.6 0.0 copy-done.5
  43.7 0.7 stack.46.refs_2_
  44.4 36.8 %forward_sum.1 = (bf16[512,1152]{1,0:T(8,128)(2,1)}, f32[512,1152]{1,0:T(8,128)}, bf16[512,1152]{1,0:T(8,128)(2,1)}) custom-call(bf16[512,1152]{1,0:T(8,128)(2,1)} %convolution_convert_fusion.refs_0_, f32[512,1152]{1,0:T(8,128)} %bitcast.59, f32[8,1152]{1,0:T(8,128)} %stack.46.refs_2_), custom_call_target="tpu_custom_call" | custom-call | tf_op jit(solution)/shard_map/forward_sum/pallas_call | solution.py:334
  81.2 0.1 pad_dynamic-slice_fusion
  81.3 0.0 copy-done.7
  81.3 0.2 compare_reduce_fusion.2
  81.5 0.1 and_bitcast_fusion.2
  81.6 0.1 pad.27.clone
  81.6 0.1 add_select_fusion
  81.7 0.1 copy.51
  81.8 0.1 select_n.43
  81.9 0.7 broadcast_in_dim.48.refs_3_
  82.6 33.3 %temporal_forward.1 = (bf16[512,288]{1,0:T(8,128)(2,1)}, bf16[5,256,288]{2,1,0:T(8,128)(2,1)}, bf16[5,256,288]{2,1,0:T(8,128)(2,1)}, bf16[512,288]{1,0:T(8,128)(...) custom-call(bf16[512,1152]{1,0:T(8,128)(2,1)} %get-tuple-element.80.refs_0_.refs_5_, ...), custom_call_target="tpu_custom_call" | custom-call | tf_op jit(solution)/shard_map/temporal_forward/pallas_call | solution.py:334
  115.9 0.7 stack.54.refs_3_
  116.6 0.1 slice.82
  116.6 0.1 broadcast_in_dim.49
  116.7 0.1 reshape.131
  116.8 0.1 and_select_fusion
  116.9 0.6 broadcast_in_dim.52.refs_4_
  117.5 131.4 %middle.1 = (f32[512,1152]{1,0:T(8,128)}, f32[512,1152]{1,0:T(8,128)}, bf16[512,1152]{1,0:T(8,128)(2,1)}, bf16[512,1152]{1,0:T(8,128)(2,1)}, bf16[512,1152]{1,0:...) custom-call(bf16[512,1152]{1,0:T(8,128)(2,1)} %get-tuple-element.82., ...), custom_call_target="tpu_custom_call" | custom-call | tf_op jit(solution)/shard_map/middle/pallas_call | solution.py:334
  248.9 51.6 %temporal_backward.1 = (bf16[512,864]{1,0:T(8,128)(2,1)}, bf16[512,1152]{1,0:T(8,128)(2,1)}, f32[2,64,1152]{2,1,0:T(8,128)}, bf16[256,288]{1,0:T(8,128)(2,1)}, b...) custom-call(bf16[512,1152]{1,0:T(8,128)(2,1)} %get-tuple-element.87.refs_0_.refs_7_, bf16[864,1152]{1,0:T(8,128)(2,1)} %bitcast.61, ...), custom_call_target="tpu_custom_call" | custom-call | tf_op jit(solution)/shard_map/temporal_backward/pallas_call | solution.py:334
  300.6 0.7 pad_maximum_fusion
  301.2 46.2 %backward_sum.1 = (f32[512,1152]{1,0:T(8,128)}, bf16[512,1152]{1,0:T(8,128)(2,1)}, f32[8,1152]{1,0:T(8,128)}, f32[144,288]{1,0:T(8,128)}, f32[144,576]{1,0:T(8,1...) custom-call(bf16[512,1152]{1,0:T(8,128)(2,1)} %get-tuple-element.101.refs_0_, ...), custom_call_target="tpu_custom_call" | custom-call | tf_op jit(solution)/shard_map/backward_sum/pallas_call | solution.py:334
  347.5 0.8 slice.93
  348.3 0.8 slice.92
  349.0 0.0 copy-done.2
  349.0 1.9 multiply_reduce_fusion.1
  351.0 0.1 select_maximum_fusion
  351.1 1.3 stack.58.refs_3_
  352.4 0.9 copy.52.refs_6_
  353.3 49.2 %closing.1 = (bf16[2,64,1152]{2,1,0:T(8,128)(2,1)}, f32[8,16,1152]{2,1,0:T(8,128)}, bf16[4,256,288]{2,1,0:T(8,128)(2,1)}, f32[144,864]{1,0:T(8,128)}, f32[144,288]{1,0:T(8,128)}) custom-call(bf16[512,1152]{1,0:T(8,128)(2,1)} %get-tuple-element.107.refs_0_, f32[2,256,1152]{2,1,0:T(8,128)} %get-tuple-element.78.refs_1_, f32[2,256,1152]{2,1,0:T(8,128)} %bitcast.67, ...), custom_call_target="tpu_custom_call" | custom-call | tf_op jit(solution)/shard_map/closing/pallas_call | solution.py:334
  402.5 11.2 %finishing.1 = (f32[9,144,288]{2,1,0:T(8,128)}, f32[8,288]{1,0:T(8,128)}, f32[1,1152]{1,0:T(1,128)}, f32[288,512]{1,0:T(8,128)}, bf16[128,1152]{1,0:T(8,128)(2,1...) custom-call(f32[8,16,1152]{2,1,0:T(8,128)} %get-tuple-element.112.sm, ...), custom_call_target="tpu_custom_call" | custom-call | tf_op jit(solution)/shard_map/finishing/pallas_call | solution.py:999
  413.7 1.3 reduce.4
  (31 shorter events, 0.2 us)
Async XLA Ops:
  2.7 30.3 %copy-start.1 = (bf16[1152,3,288]{0,2,1:T(8,128)(2,1)S(1)}, bf16[1152,3,288]{0,2,1:T(8,128)(2,1)}, u32[]{:S(2)}) copy-start(bf16[1152,3,288]{0,2,1:T(8,128)(2,1)} %param.28) | copy-start | bytes 5971972
  35.8 1.1 copy-start
  39.4 2.4 copy-start.3
  41.4 2.3 copy-start.5
  43.6 37.6 %copy-start.9 = (s32[1,4]{1,0:T(1,128)S(1)}, s32[1,4]{1,0:T(1,128)}, u32[]{:S(2)}) copy-start(s32[1,4]{1,0:T(1,128)} %param.23) | copy-start | bytes 52
  43.6 37.7 %copy-start.7 = (s32[1,2,4]{2,1,0:T(2,128)S(1)}, s32[1,2,4]{2,1,0:T(2,128)}, u32[]{:S(2)}) copy-start(s32[1,2,4]{2,1,0:T(2,128)} %param.24) | copy-start | bytes 100
  82.6 33.3 %copy-start.8 = (bf16[1152]{0:T(1024)(128)(2,1)S(1)}, bf16[1152]{0:T(1024)(128)(2,1)}, u32[]{:S(2)}) copy-start(bf16[1152]{0:T(1024)(128)(2,1)} %param.33) | copy-start | bytes 6916
  82.6 34.1 %copy-start.10 = (s32[1,2]{1,0:T(1,128)S(1)}, s32[1,2]{1,0:T(1,128)}, u32[]{:S(2)}) copy-start(s32[1,2]{1,0:T(1,128)} %param.25) | copy-start | bytes 28
  301.2 47.8 %copy-start.2 = (bf16[1,2,64,1152]{3,2,1,0:T(8,128)(2,1)S(1)}, bf16[1,2,64,1152]{3,2,1,0:T(8,128)(2,1)}, u32[]{:S(2)}) copy-start(bf16[1,2,64,1152]{3,2,1,0:T(8,128)(2,1)} %param.39) | copy-start | bytes 884740
  301.2 47.8 %copy-start.4 = (f32[2,64,1152]{2,1,0:T(8,128)S(1)}, f32[2,64,1152]{2,1,0:T(8,128)}, u32[]{:S(2)}) copy-start(f32[2,64,1152]{2,1,0:T(8,128)} %get-tuple-element.100) | copy-start | bytes 1769476
  301.2 49.7 %copy-start.6 = (f32[8,1152]{1,0:T(8,128)S(1)}, f32[8,1152]{1,0:T(8,128)}, u32[]{:S(2)}) copy-start(f32[8,1152]{1,0:T(8,128)} %get-tuple-element.110) | copy-start | bytes 110596
